TPU v7x, 32 devices: a whole 2x2x4 slice. The times are simulated.
32 devices in a mesh: dp: 8 (over y, x, core), mp: 4 (over z).
Axes of the slice: x: 2, y: 2, z: 4, core: 2. Of those that a mesh axis runs over, the one named last changes fastest.
Arguments:
- tokens: bfloat16 [16, 1024, 1024], P('dp', 'mp'), may hold values from -6 to 6
- cotangent: bfloat16 [16, 1024, 1024], P('dp', 'mp'), may hold values from -6 to 6
- lengths: int32 [16], P('dp'), may hold values from 102 to 1024, as said below
- buckets: int32 [1024], replicated, may hold values from 0 to 31, as said below
- step_count: int32 [1], replicated, may hold values from 1 to 5
- qkv_weight: float32 [1024, 3, 1024], P(None, None, 'mp')
- out_weight: float32 [1024, 1024], P('mp')
- up_weight: float32 [1024, 4096], P(None, 'mp')
- down_weight: float32 [4096, 1024], P('mp')
- up_bias: float32 [4096], P('mp'), may hold values from -4 to 4
- rel_bias: float32 [32, 16], P(None, 'mp'), may hold values from -6 to 6
- norm_vectors: float32 [6, 1024], replicated
- qkv_moments: float32 [2, 1024, 3, 1024], P(None, 'dp', None, 'mp'), as said below
- out_moments: float32 [2, 1024, 1024], P(None, 'mp', 'dp'), as said below
- up_moments: float32 [2, 1024, 4096], P(None, 'dp', 'mp'), as said below
- down_moments: float32 [2, 4096, 1024], P(None, 'mp', 'dp'), as said below
- bias_moments: float32 [2, 4096], P(None, 'mp'), as said below
- rel_moments: float32 [2, 32, 16], P(None, None, 'mp'), as said below
- vector_moments: float32 [2, 6, 1024], replicated, as said below
Outputs:
- block_out: bfloat16 [16, 1024, 1024], P('dp', 'mp')
- input_grad: float32 [16, 1024, 1024], P('dp', 'mp')
- qkv_new: float32 [1024, 3, 1024], P('dp', None, 'mp')
- qkv_state: float32 [2, 1024, 3, 1024], P(None, 'dp', None, 'mp')
- out_new: float32 [1024, 1024], P('mp', 'dp')
- out_state: float32 [2, 1024, 1024], P(None, 'mp', 'dp')
- up_new: float32 [1024, 4096], P('dp', 'mp')
- up_state: float32 [2, 1024, 4096], P(None, 'dp', 'mp')
- down_new: float32 [4096, 1024], P('mp', 'dp')
- down_state: float32 [2, 4096, 1024], P(None, 'mp', 'dp')
- bias_new: float32 [4096], P('mp')
- bias_state: float32 [2, 4096], P(None, 'mp')
- rel_new: float32 [32, 16], P(None, 'mp')
- rel_state: float32 [2, 32, 16], P(None, None, 'mp')
- vector_new: float32 [6, 1024], replicated
- vector_state: float32 [2, 6, 1024], replicated
- norm_values: float32 [2, 12], replicated
Inputs may be any that keep to these rules, and one draw needn't show every extreme that they name: `lengths`: some sequence has all 1024 positions valid. buckets never fall with the distance, are 0 at distance 0 and 31 at distance 1024 - 1. `qkv_moments`: index 1 of the first dimension holds positive second moments. `out_moments`: index 1 of the first dimension holds positive second moments. `up_moments`: index 1 of the first dimension holds positive second moments. `down_moments`: index 1 of the first dimension holds positive second moments. `bias_moments`: index 1 of the first dimension holds positive second moments. `rel_moments`: index 1 of the first dimension holds positive second moments. `vector_moments`: index 1 of the first dimension holds positive second moments.
All inputs are finite; a program needn't handle non-finite values.
Results may differ from a plain program's by a relative error of at most 0.017.
Values may be sent and summed in bfloat16 or wider, within the bound.
No kernel may reach another device: no remote copies, remote signals or barrier semaphores. Data moves between devices by JAX's collectives and lax.ppermute only.
A program may use at most 192 MiB of HBM per device.

v0:
```python
import jax
import jax.numpy as jnp
from jax import lax
from jax.experimental import pallas as pl
from jax.experimental.pallas import tpu as pltpu
from jax.sharding import PartitionSpec as P

HD = 64
f32 = jnp.float32
bf16 = jnp.bfloat16

norm_eps = 1e-05
adam_eps = 1e-06
learn_rate = 0.25
weight_decay = 0.1
masked_score = -1000000000.0
score_scale = HD ** (-0.5)
kernel_bytes = 48 << 20

in_vmem = pl.BlockSpec(memory_space=pltpu.VMEM)
in_smem = pl.BlockSpec(memory_space=pltpu.SMEM)


def dot_nt(left, right):
    return lax.dot_general(left, right, (((1,), (1,)), ((), ())), preferred_element_type=f32)


def dot_nn(left, right):
    return lax.dot_general(left, right, (((1,), (0,)), ((), ())), preferred_element_type=f32)


def dot_tn(left, right):
    return lax.dot_general(left, right, (((0,), (0,)), ((), ())), preferred_element_type=f32)


def tile_of(rows):
    return min(256, rows)


def bias_tiles(line_ref, head, tiles, tile):
    causal = lax.broadcasted_iota(jnp.int32, (tile, tile), 0) <= lax.broadcasted_iota(
        jnp.int32, (tile, tile), 1
    )
    made = []
    for kk in range(tiles):
        line = line_ref[head : head + 1, kk * 2 * tile : (kk + 1) * 2 * tile]
        wide = jnp.broadcast_to(line, (tile, 2 * tile))
        made.append(pltpu.roll(wide, tile, 1, stride=1, stride_axis=0)[:, :tile])
    made[0] = jnp.where(causal, made[0], masked_score)
    return made


def scores_of(keys, query, toeplitz, block, tile, key_pos, length):
    count = (block + 1) * tile
    raw = dot_nt(keys[:count], query)
    raw = raw + jnp.concatenate([toeplitz[block - j] for j in range(block + 1)], axis=0)
    return jnp.where(key_pos[:count] < length, raw, masked_score)


def attend_kernel(heads, length_ref, qkv_ref, line_ref, ctx_ref, lse_ref):
    rows = qkv_ref.shape[0]
    tile = tile_of(rows)
    tiles = rows // tile
    width = heads * HD
    length = length_ref[0]
    key_pos = lax.broadcasted_iota(jnp.int32, (rows, tile), 0)
    for head in range(heads):
        toeplitz = bias_tiles(line_ref, head, tiles, tile)
        cols = slice(head * HD, (head + 1) * HD)
        keys = qkv_ref[:, width + head * HD : width + (head + 1) * HD]
        vals = qkv_ref[:, 2 * width + head * HD : 2 * width + (head + 1) * HD]
        for block in range(tiles):
            here = slice(block * tile, (block + 1) * tile)
            count = (block + 1) * tile
            query = qkv_ref[here, cols] * jnp.asarray(score_scale, bf16)
            raw = scores_of(keys, query, toeplitz, block, tile, key_pos, length)
            top = jnp.max(raw, axis=0, keepdims=True)
            grown = jnp.exp(raw - top)
            total = jnp.sum(grown, axis=0, keepdims=True)
            probs = (grown * (1.0 / total)).astype(bf16)
            ctx_ref[here, cols] = dot_tn(probs, vals[:count]).astype(bf16)
            lse_ref[head : head + 1, here] = top + jnp.log(total)


def attend_back_kernel(
    heads,
    length_ref,
    qkv_ref,
    line_ref,
    lse_ref,
    grad_ref,
    out_ref,
    dist_ref,
    key_acc,
    val_acc,
    diag_acc,
):
    rows = qkv_ref.shape[0]
    tile = tile_of(rows)
    tiles = rows // tile
    width = heads * HD
    length = length_ref[0]
    key_pos = lax.broadcasted_iota(jnp.int32, (rows, tile), 0)
    for head in range(heads):
        toeplitz = bias_tiles(line_ref, head, tiles, tile)
        cols = slice(head * HD, (head + 1) * HD)
        key_cols = slice(width + head * HD, width + (head + 1) * HD)
        val_cols = slice(2 * width + head * HD, 2 * width + (head + 1) * HD)
        keys = qkv_ref[:, key_cols]
        vals = qkv_ref[:, val_cols]
        key_acc[...] = jnp.zeros_like(key_acc)
        val_acc[...] = jnp.zeros_like(val_acc)
        diag_acc[...] = jnp.zeros_like(diag_acc)
        for block in range(tiles):
            here = slice(block * tile, (block + 1) * tile)
            count = (block + 1) * tile
            query = qkv_ref[here, cols] * jnp.asarray(score_scale, bf16)
            grad = grad_ref[here, cols]
            raw = scores_of(keys, query, toeplitz, block, tile, key_pos, length)
            probs = jnp.exp(raw - lse_ref[head : head + 1, here])
            pgrad = dot_nt(vals[:count], grad)
            drop = jnp.sum(probs * pgrad, axis=0, keepdims=True)
            sgrad = (probs * (pgrad - drop)).astype(bf16)
            val_acc[:count] += dot_nn(probs.astype(bf16), grad)
            key_acc[:count] += dot_nn(sgrad, query)
            out_ref[here, cols] = (dot_tn(sgrad, keys[:count]) * score_scale).astype(bf16)
            wide = sgrad.astype(f32)
            for j in range(block + 1):
                diag_acc[block - j] += wide[j * tile : (j + 1) * tile]
        out_ref[:, key_cols] = key_acc[...].astype(bf16)
        out_ref[:, val_cols] = val_acc[...].astype(bf16)
        for kk in range(tiles):
            held = jnp.concatenate([diag_acc[kk], jnp.zeros((tile, tile), f32)], axis=1)
            half = tile // 2
            while half >= 1:
                held = held[:half] + pltpu.roll(held[half : 2 * half], 2 * tile - half, 1)
                half //= 2
            dist_ref[head : head + 1, kk * 2 * tile : (kk + 1) * 2 * tile] = pltpu.roll(held, tile, 1)


def attend(length, qkv, line, heads):
    rows = qkv.shape[0]
    return pl.pallas_call(
        lambda *refs: attend_kernel(heads, *refs),
        out_shape=(
            jax.ShapeDtypeStruct((rows, heads * HD), bf16),
            jax.ShapeDtypeStruct((heads, rows), f32),
        ),
        in_specs=[in_smem, in_vmem, in_vmem],
        out_specs=(in_vmem, in_vmem),
        compiler_params=pltpu.CompilerParams(vmem_limit_bytes=kernel_bytes),
        cost_estimate=pl.CostEstimate(
            flops=heads * rows * rows * HD * 32,
            bytes_accessed=4 << 20,
            transcendentals=heads * rows * rows,
        ),
        name="attend",
    )(length, qkv, line)


def attend_back(length, qkv, line, lse, grad, heads):
    rows = qkv.shape[0]
    tile = tile_of(rows)
    return pl.pallas_call(
        lambda *refs: attend_back_kernel(heads, *refs),
        out_shape=(
            jax.ShapeDtypeStruct((rows, 3 * heads * HD), bf16),
            jax.ShapeDtypeStruct((heads, 2 * rows), f32),
        ),
        in_specs=[in_smem, in_vmem, in_vmem, in_vmem, in_vmem],
        out_specs=(in_vmem, in_vmem),
        scratch_shapes=[
            pltpu.VMEM((rows, HD), f32),
            pltpu.VMEM((rows, HD), f32),
            pltpu.VMEM((rows // tile, tile, tile), f32),
        ],
        compiler_params=pltpu.CompilerParams(vmem_limit_bytes=kernel_bytes),
        cost_estimate=pl.CostEstimate(
            flops=heads * rows * rows * HD * 64,
            bytes_accessed=4 << 20,
            transcendentals=heads * rows * rows,
        ),
        name="attend_back",
    )(length, qkv, line, lse, grad)


class Places:
    def __init__(self, per):
        self.per = per
        self.dp_n = lax.axis_size("dp")
        self.mp_n = lax.axis_size("mp")
        self.q_n = self.dp_n // 2
        self.slots = 2 * per
        self.t_n = self.mp_n // self.slots
        assert self.dp_n % 2 == 0 and self.mp_n % self.slots == 0
        dp_i = lax.axis_index("dp")
        mp_i = lax.axis_index("mp")
        self.dp_i, self.mp_i = dp_i, mp_i
        self.q, self.c = dp_i // 2, lax.rem(dp_i, 2)
        self.s, self.t = mp_i // self.t_n, lax.rem(mp_i, self.t_n)
        self.home = self.s // per
        self.at_home = self.c == self.home
        self.q_bits = []
        while (1 << len(self.q_bits)) < self.q_n:
            self.q_bits.append(1 << len(self.q_bits))
        assert (1 << len(self.q_bits)) == self.q_n

    def move(self, values, target):
        pairs = []
        for q in range(self.q_n):
            for c in range(2):
                for s in range(self.slots):
                    for t in range(self.t_n):
                        found = target(q, c, s, t)
                        if found is not None:
                            nq, nc, ns, nt = found
                            pairs.append(
                                (
                                    (q * 2 + c) * self.mp_n + s * self.t_n + t,
                                    (nq * 2 + nc) * self.mp_n + ns * self.t_n + nt,
                                )
                            )
        return lax.ppermute(values, ("dp", "mp"), pairs)

    def to_core(self, values):
        return self.move(values, lambda q, c, s, t: (q, 1 - c, s, t))

    def to_slot(self, values, step):
        return self.move(values, lambda q, c, s, t: (q, c, (s + step) % self.slots, t))

    def to_chip(self, values, bit):
        return self.move(values, lambda q, c, s, t: (q ^ bit, c, s, t))

    def to_team(self, values, step):
        return self.move(values, lambda q, c, s, t: (q, c, s, (t + step) % self.t_n))

    def relative(self, values, dim):
        size = values.shape[dim] // self.q_n
        return jnp.concatenate(
            [
                lax.dynamic_slice_in_dim(values, (self.q ^ k) * size, size, dim)
                for k in range(self.q_n)
            ],
            axis=dim,
        )

    def block_at(self, step):
        return lax.rem(self.s + step, self.slots) * self.t_n + self.t

    def collect(self, local):
        count, width = local.shape[1:]
        whole = jnp.zeros((count * self.mp_n, width), local.dtype)
        for step in range(self.slots):
            slot = lax.rem(self.s + step, self.slots)
            piece = lax.dynamic_index_in_dim(
                local, jnp.clip(slot - self.per * self.c, 0, self.per - 1), 0, keepdims=False
            )
            if step > 0:
                piece = self.move(
                    piece,
                    lambda q, c, s, t: (
                        (q, c, (s + step) % self.slots, t)
                        if (s + step) % self.slots // self.per == c
                        else None
                    ),
                )
            other = self.move(
                piece, lambda q, c, s, t: (q, 1 - c, s, t) if c == s // self.per else None
            )
            piece = jnp.where(self.at_home, piece, other)
            origin = lax.rem(self.s + self.slots - step, self.slots)
            for turn in range(self.t_n):
                got = self.to_team(piece, turn) if turn > 0 else piece
                from_t = lax.rem(self.t + self.t_n - turn, self.t_n)
                whole = lax.dynamic_update_slice_in_dim(
                    whole, got, (origin * self.t_n + from_t) * count, 0
                )
        return whole

    def deliver(self, blocks):
        arrived = []
        for step in range(self.slots):
            flip, index = step // self.per, step % self.per
            value = blocks[index]
            if step > 0:
                value = self.move(
                    value,
                    lambda q, c, s, t: (
                        (q, s // self.per, (s + step) % self.slots, t)
                        if c == (s // self.per) ^ flip
                        else None
                    ),
                )
            arrived.append(value)
        results = []
        for index in range(self.per):
            slot = self.per * self.c + index
            step = lax.rem(self.s + self.slots - slot, self.slots)
            picked = arrived[0]
            for number in range(1, self.slots):
                picked = jnp.where(step == number, arrived[number], picked)
            results.append(picked)
        return jnp.stack(results)

    def share(self, values, length, flip, team):
        side = jnp.where(self.at_home, 0, 1) ^ flip
        parts = []
        for index in range(self.per):
            slot = lax.rem(self.s + self.per * side + index, self.slots)
            block = slot * self.t_n + lax.rem(self.t + team, self.t_n)
            parts.append(lax.dynamic_slice_in_dim(values, block * length, length, 0))
        return jnp.concatenate(parts, axis=0)

    def sum_share(self, partial, length):
        total = self.share(partial, length, 0, 0).astype(f32)
        for team in range(self.t_n):
            for flip in (0, 1):
                if (team, flip) != (0, 0):
                    sent = self.share(partial, length, flip, team).astype(bf16)
                    total = total + self.move(
                        sent, lambda q, c, s, t: (q, c ^ flip, s, (t + team) % self.t_n)
                    ).astype(f32)
        return total

    def sum_team(self, partial):
        total = partial.astype(f32)
        total = total + self.to_core(partial).astype(f32)
        if self.t_n > 1:
            low = total.astype(bf16)
            for team in range(1, self.t_n):
                total = total + self.to_team(low, team).astype(f32)
        return total

    def gather_chips(self, piece, first_bit):
        bits = self.q_bits if first_bit == 0 else self.q_bits[::-1]
        pieces = {0: piece}
        for bit in bits:
            for k in list(pieces):
                pieces[k | bit] = self.to_chip(pieces[k], bit)
        return jnp.concatenate([pieces[k] for k in range(self.q_n)], axis=0)

    def scatter_chips(self, values, first_bit):
        count = values.shape[0] // self.q_n
        bits = self.q_bits if first_bit == 0 else self.q_bits[::-1]
        pieces = {k: values[k * count : (k + 1) * count] for k in range(self.q_n)}
        for number, bit in enumerate(bits):
            last = number == len(bits) - 1
            for k in [k for k in pieces if k & bit]:
                got = self.to_chip(pieces.pop(k).astype(bf16), bit).astype(f32)
                pieces[k ^ bit] = pieces[k ^ bit].astype(f32) + got
        return pieces[0]

    def sum_all(self, values, chips_only=False):
        if not chips_only:
            values = values + self.to_core(values)
        for low in range(0, len(self.q_bits), 2):
            bits = self.q_bits[low : low + 2]
            got = [self.to_chip(values, bit) for bit in bits]
            if len(bits) == 2:
                both = self.to_chip(values, bits[0] | bits[1])
                values = (values + got[0]) + (got[1] + both)
            else:
                values = values + got[0]
        if not chips_only:
            bit, bits = 1, []
            while bit < self.mp_n:
                bits.append(bit)
                bit *= 2
            flip = lambda mask: self.move(
                values,
                lambda q, c, s, t: (
                    q,
                    c,
                    ((s * self.t_n + t) ^ mask) // self.t_n,
                    ((s * self.t_n + t) ^ mask) % self.t_n,
                ),
            )
            for low in range(0, len(bits), 2):
                pair = bits[low : low + 2]
                if len(pair) == 2:
                    one, two, both = flip(pair[0]), flip(pair[1]), flip(pair[0] | pair[1])
                    values = (values + one) + (two + both)
                else:
                    values = values + flip(pair[0])
        return values


def norm_parts(values):
    center = values - jnp.mean(values, axis=-1, keepdims=True)
    spread = jnp.mean(center * center, axis=-1, keepdims=True)
    inverse = lax.rsqrt(spread + norm_eps)
    return (center * inverse, inverse)


def norm_back(upstream, normed, inverse, gain_vec):
    scaled = upstream * gain_vec
    return inverse * (
        scaled
        - jnp.mean(scaled, axis=-1, keepdims=True)
        - normed * jnp.mean(scaled * normed, axis=-1, keepdims=True)
    )


def adjust(weight, first, second, gradient, decay_rate, first_fix, second_fix):
    first_new = 0.9 * first + 0.1 * gradient
    second_new = 0.999 * second + 0.001 * gradient * gradient
    update = (
        first_new / first_fix / (jnp.sqrt(second_new / second_fix) + adam_eps) + decay_rate * weight
    )
    return (first_new, second_new, update)


def gelu_parts(values):
    half = 0.5 * (1.0 + lax.erf(values * (0.5**0.5)))
    bell = jnp.exp(-0.5 * values * values) * 0.3989422804014327
    return (values * half, half + values * bell)


def local(
    tokens,
    cotangent,
    lengths,
    buckets,
    step_count,
    qkv_weight,
    out_weight,
    up_weight,
    down_weight,
    up_bias,
    rel_bias,
    norm_vectors,
    qkv_moments,
    out_moments,
    up_moments,
    down_moments,
    bias_moments,
    rel_moments,
    vector_moments,
):
    per, length_rows, width = tokens.shape
    at = Places(per)
    seq_len = length_rows * at.mp_n
    blocks = at.slots
    q_n, c, q = at.q_n, at.c, at.q
    head_width = out_weight.shape[0] // 2
    heads = head_width // HD
    units = up_weight.shape[1] // 2
    bucket_count, local_heads = rel_bias.shape

    inputs_low = at.collect(at.relative(tokens, 2))
    all_lengths = lengths
    length_grid = at.move(
        all_lengths, lambda q, c, s, t: (q, 1 - c, s, t)
    )
    four = jnp.where(
        c == 0,
        jnp.concatenate([all_lengths, length_grid]),
        jnp.concatenate([length_grid, all_lengths]),
    )
    length = lax.dynamic_slice_in_dim(four, at.s, 1, 0)
    row_keep = jnp.arange(seq_len)[:, None] < length[0]
    row_mask = row_keep.astype(f32)
    vectors = at.relative(norm_vectors, 1)

    def half(values, dim, size):
        return lax.dynamic_slice_in_dim(values, c * size, size, dim)

    attn_own = at.relative(
        jnp.concatenate(
            [
                half(qkv_weight, 2, head_width).reshape(width, 3 * head_width).astype(bf16),
                half(out_weight, 0, head_width).astype(bf16).T,
            ],
            axis=1,
        ),
        0,
    )
    up_own = at.relative(half(up_weight, 1, units).astype(bf16), 0)
    down_own = at.relative(half(down_weight, 0, units).astype(bf16).T, 0)
    part = width // q_n
    small_own = jnp.concatenate(
        [half(up_bias, 0, units), half(rel_bias, 1, heads).T.reshape(-1)]
    )
    attn_w, up_w, down_w, small = [attn_own], [up_own], [down_own], [small_own]
    for step in range(1, blocks):
        small.append(at.to_slot(small_own, step))
        piece = at.to_slot(attn_own[:part], step)
        attn_w.append(at.gather_chips(piece, step % 2))
    for step in range(1, blocks):
        piece = at.to_slot(up_own[:part], step)
        up_w.append(at.gather_chips(piece, 0))
        piece = at.to_slot(down_own[:part], step)
        down_w.append(at.gather_chips(piece, 1))
    qkv_w = [values[:, : 3 * head_width] for values in attn_w]
    out_w = [values[:, 3 * head_width :] for values in attn_w]

    tile = tile_of(seq_len)
    tiles = seq_len // tile
    padded = jnp.concatenate([jnp.zeros((tile,), jnp.int32), buckets])
    spread = jnp.concatenate(
        [padded[kk * tile : (kk + 2) * tile] for kk in range(tiles)]
    )
    choose = (jnp.arange(bucket_count, dtype=jnp.int32)[:, None] == spread[None, :]).astype(f32)
    rel_rows = jnp.concatenate(
        [values[units:].reshape(heads, bucket_count) for values in small], axis=0
    )
    lines = jnp.dot(rel_rows, choose, precision=lax.Precision.HIGHEST)

    inputs = inputs_low.astype(f32)
    first_normed, first_inverse = norm_parts(inputs)
    first_low = (first_normed * vectors[0] + vectors[1]).astype(bf16)
    qkv, contexts, totals = [], [], []
    for r in range(blocks):
        qkv.append(dot_nn(first_low, qkv_w[r]).astype(bf16))
        context, total = attend(length, qkv[r], lines[r * heads : (r + 1) * heads], heads)
        contexts.append(context)
        totals.append(total)
    mixed = dot_nt(contexts[0], out_w[0])
    for r in range(1, blocks):
        mixed = mixed + dot_nt(contexts[r], out_w[r])
    mixed = at.sum_team(jnp.where(row_keep, mixed, 0.0).astype(bf16))
    middle = inputs + (mixed + vectors[4]) * row_mask
    second_normed, second_inverse = norm_parts(middle)
    second_low = (second_normed * vectors[2] + vectors[3]).astype(bf16)
    acts, slopes = [], []
    for r in range(blocks):
        pre = dot_nn(second_low, up_w[r]) + small[r][:units]
        act, slope = gelu_parts(pre)
        acts.append(act.astype(bf16))
        slopes.append(slope)
    fed = dot_nt(acts[0], down_w[0])
    for r in range(1, blocks):
        fed = fed + dot_nt(acts[r], down_w[r])
    fed_share = at.sum_share(fed.astype(bf16), length_rows)
    middle_share = at.share(middle, length_rows, 0, 0)
    mask_share = at.share(row_mask, length_rows, 0, 0)
    out_share = (middle_share + (fed_share + vectors[5]) * mask_share).astype(bf16)
    block_out = at.deliver(
        [out_share[i * length_rows : (i + 1) * length_rows] for i in range(per)]
    )
    block_out = at.relative(block_out, 2)

    incoming_low = at.collect(at.relative(cotangent, 2))
    kept = jnp.where(row_keep, incoming_low, jnp.zeros_like(incoming_low))
    fed_bias_grad = jnp.sum(kept.astype(f32), axis=0)
    back = None
    mlp_grads, bias_grads = [], []
    for r in range(blocks):
        down_grad = dot_tn(kept, acts[r]).astype(bf16)
        pre_low = (dot_nn(kept, down_w[r]) * slopes[r]).astype(bf16)
        bias_grads.append(jnp.sum(pre_low.astype(f32), axis=0))
        up_grad = dot_tn(second_low, pre_low).astype(bf16)
        term = dot_nt(pre_low, up_w[r])
        back = term if back is None else back + term
        mlp_grads.append((up_grad, down_grad))
    second_grad = at.sum_team(back.astype(bf16))
    lead = jnp.where((c == 0) & (at.t == 0), 1.0, 0.0)
    gain_two = jnp.sum(second_grad * second_normed, axis=0)
    shift_two = jnp.sum(second_grad, axis=0)
    middle_grad = incoming_low.astype(f32) + norm_back(
        second_grad, second_normed, second_inverse, vectors[2]
    )
    branch = jnp.where(row_keep, middle_grad, 0.0).astype(bf16)
    mix_bias_grad = jnp.sum(branch.astype(f32), axis=0)
    back = None
    attn_grads, rel_grads = [], []
    for r in range(blocks):
        context_grad = dot_nn(branch, out_w[r]).astype(bf16)
        proj_grad, dist = attend_back(
            length, qkv[r], lines[r * heads : (r + 1) * heads], totals[r], context_grad, heads
        )
        rel_grads.append(dist)
        qkv_grad = dot_tn(first_low, proj_grad).astype(bf16)
        out_grad = dot_tn(branch, contexts[r]).astype(bf16)
        attn_grads.append((qkv_grad, out_grad))
        term = dot_nt(proj_grad, qkv_w[r])
        back = term if back is None else back + term
    rel_grad = lax.dot_general(
        jnp.concatenate(rel_grads, axis=0),
        choose,
        (((1,), (1,)), ((), ())),
        precision=lax.Precision.HIGHEST,
    )
    first_grad = at.sum_share(back.astype(bf16), length_rows)
    normed_share = at.share(first_normed, length_rows, 0, 0)
    inverse_share = at.share(first_inverse, length_rows, 0, 0)
    middle_grad_share = at.share(middle_grad, length_rows, 0, 0)
    gain_one = jnp.sum(first_grad * normed_share, axis=0)
    shift_one = jnp.sum(first_grad, axis=0)
    input_share = middle_grad_share + norm_back(
        first_grad, normed_share, inverse_share, vectors[0]
    )
    input_share = input_share.astype(bf16)
    input_grad = at.deliver(
        [input_share[i * length_rows : (i + 1) * length_rows] for i in range(per)]
    )
    input_grad = at.relative(input_grad, 2).astype(f32)

    vector_grad = jnp.concatenate(
        [
            jnp.stack([gain_one, shift_one]),
            lead * jnp.stack([gain_two, shift_two, mix_bias_grad, fed_bias_grad]),
        ]
    )
    vector_grad = at.sum_all(at.relative(vector_grad, 1))

    def own_sum(pieces):
        total = pieces[0]
        for step in range(1, blocks):
            total = total + at.to_slot(pieces[step], blocks - step).astype(f32)
        return total

    def both_halves(mine, other, dim):
        return jnp.where(
            c == 0,
            jnp.concatenate([mine, other], axis=dim),
            jnp.concatenate([other, mine], axis=dim),
        )

    def scattered(parts, first_bit):
        low = []
        for step in range(blocks):
            piece = at.scatter_chips(parts[step], (first_bit + step) % 2)
            low.append(piece if step == 0 else piece.astype(bf16))
        mine = own_sum(low)
        rows = part // 2
        sent = lax.dynamic_slice_in_dim(mine, (1 - c) * rows, rows, 0)
        return lax.dynamic_slice_in_dim(mine, c * rows, rows, 0), at.to_core(sent)

    up_sum = both_halves(*scattered([pair[0] for pair in mlp_grads], 0), 1)
    down_sum = both_halves(*scattered([pair[1] for pair in mlp_grads], 1), 1).T
    rows = part // 2
    mine, other = scattered([pair[0] for pair in attn_grads], 0)
    qkv_sum = both_halves(
        mine.reshape(rows, 3, head_width), other.reshape(rows, 3, head_width), 2
    )
    out_sum = both_halves(*scattered([pair[1] for pair in attn_grads], 1), 1).T
    small_grads = [
        jnp.concatenate(
            [bias_grads[r], rel_grad[r * heads : (r + 1) * heads].reshape(-1)]
        )
        for r in range(blocks)
    ]
    small_mine = at.sum_all(own_sum(small_grads), chips_only=True)
    small_other = at.to_core(small_mine)
    bias_sum = both_halves(small_mine[:units], small_other[:units], 0)
    rel_sum = both_halves(
        small_mine[units:].reshape(heads, bucket_count),
        small_other[units:].reshape(heads, bucket_count),
        0,
    ).T

    def own_part(values, dim):
        count = values.shape[dim] // at.dp_n
        return lax.dynamic_slice_in_dim(values, at.dp_i * count, count, dim)

    steps_done = step_count[0].astype(f32)
    first_fix = 1.0 - jnp.power(jnp.float32(0.9), steps_done)
    second_fix = 1.0 - jnp.power(jnp.float32(0.999), steps_done)
    pieces = [
        (own_part(qkv_weight, 0), qkv_moments, qkv_sum, weight_decay),
        (own_part(out_weight, 1), out_moments, out_sum, weight_decay),
        (own_part(up_weight, 0), up_moments, up_sum, weight_decay),
        (own_part(down_weight, 1), down_moments, down_sum, weight_decay),
        (up_bias, bias_moments, bias_sum, 0.0),
        (rel_bias, rel_moments, rel_sum, 0.0),
        (norm_vectors, vector_moments, vector_grad, 0.0),
    ]
    adjusted = [
        adjust(weight, moments[0], moments[1], grad, decay, first_fix, second_fix)
        for weight, moments, grad, decay in pieces
    ]
    lead_dp = (at.dp_i == 0).astype(f32)
    share = [1.0, 1.0, 1.0, 1.0, lead_dp, lead_dp]
    squares = jnp.stack(
        [share[i] * jnp.sum(pieces[i][0] * pieces[i][0]) for i in range(6)]
        + [share[i] * jnp.sum(adjusted[i][2] * adjusted[i][2]) for i in range(6)]
    )
    squares = at.sum_all(squares)
    vector_sq = jnp.sum(norm_vectors * norm_vectors, axis=1)
    vector_up_sq = jnp.sum(adjusted[6][2] * adjusted[6][2], axis=1)
    weight_norm = jnp.sqrt(jnp.concatenate([squares[:6], vector_sq]))
    update_norm = jnp.sqrt(jnp.concatenate([squares[6:], vector_up_sq]))
    trust_ratio = weight_norm / (update_norm + adam_eps)
    results = [block_out, input_grad]
    for index in range(6):
        results.append(pieces[index][0] - learn_rate * trust_ratio[index] * adjusted[index][2])
        results.append(jnp.stack([adjusted[index][0], adjusted[index][1]]))
    results.append(norm_vectors - learn_rate * trust_ratio[6:][:, None] * adjusted[6][2])
    results.append(jnp.stack([adjusted[6][0], adjusted[6][1]]))
    results.append(jnp.stack([weight_norm, update_norm]))
    return tuple(results)


def solution(mesh):
    return jax.shard_map(
        local,
        mesh=mesh,
        in_specs=(
            P("dp", "mp", None),
            P("dp", "mp", None),
            P("dp"),
            P(),
            P(),
            P(None, None, "mp"),
            P("mp", None),
            P(None, "mp"),
            P("mp", None),
            P("mp"),
            P(None, "mp"),
            P(),
            P(None, "dp", None, "mp"),
            P(None, "mp", "dp"),
            P(None, "dp", "mp"),
            P(None, "mp", "dp"),
            P(None, "mp"),
            P(None, None, "mp"),
            P(),
        ),
        out_specs=(
            P("dp", "mp", None),
            P("dp", "mp", None),
            P("dp", None, "mp"),
            P(None, "dp", None, "mp"),
            P("mp", "dp"),
            P(None, "mp", "dp"),
            P("dp", "mp"),
            P(None, "dp", "mp"),
            P("mp", "dp"),
            P(None, "mp", "dp"),
            P("mp"),
            P(None, "mp"),
            P(None, "mp"),
            P(None, None, "mp"),
            P(),
            P(),
            P(),
        ),
        check_vma=False,
    )
```

profile of v0, /device:TPU:1, one launch (start us, length us, event | category | flops | bytes accessed | tf_op | source)
XLA Modules:
  0.0 710.3 jit_solution(8953012842970888505)
XLA Ops:
  56.5 8.9 %collective-permute-done.15 = bf16[256,512]{0,1:T(8,128)(2,1)S(1)} collective-permute-done((bf16[256,512]{0,1:T(8,128)(2,1)}, bf16[256,512]{0,1:T(8,128)(2,1)S(1)}, u32[]{:S(2)}, u32[]{:S(2)}) %collective-permute-start.15) | collective-permute-done | bytes 262176 | tf_op jit(solution)/shard_map/ppermute | solution.py:223
  65.5 10.5 %collective-permute-start.36 = (bf16[256,512]{0,1:T(8,128)(2,1)S(1)}, bf16[256,512]{0,1:T(8,128)(2,1)}, u32[]{:S(2)}, u32[]{:S(2)}) collective-permute-start(bf16[256,512]{0,1:T(8,128)(2,1)S(1)} %get-tuple-element.180), channel_id=1, source_target_pairs={{0,2},{1,3},{2,0},{3,1},{4,6},{5,7},{6,4},{7,5},{8,10},{9,11},{10,... | collective-permute-start | bytes 786440 | tf_op jit(solution)/shard_map/ppermute | solution.py:223
  83.9 26.4 %collective-permute-done.32 = bf16[256,512]{1,0:T(8,128)(2,1)S(1)} collective-permute-done((bf16[256,512]{1,0:T(8,128)(2,1)}, bf16[256,512]{1,0:T(8,128)(2,1)S(1)}, u32[]{:S(2)}, u32[]{:S(2)}) %collective-permute-start.32) | collective-permute-done | bytes 262176 | tf_op jit(solution)/shard_map/ppermute | solution.py:223
  178.1 5.3 collective-permute-done.6
  225.0 4.7 collective-permute-start.57
  314.1 8.6 %collective-permute-done.97 = bf16[256,512]{0,1:T(8,128)(2,1)S(1)} collective-permute-done((bf16[256,512]{0,1:T(8,128)(2,1)S(1)}, bf16[256,512]{0,1:T(8,128)(2,1)S(1)}, u32[]{:S(2)}, u32[]{:S(2)}) %collective-permute-start.97) | collective-permute-done | bytes 262176 | tf_op jit(solution)/shard_map/ppermute | solution.py:223
  324.2 6.0 collective-permute-done.104
  347.0 4.4 collective-permute-done.125
  357.1 15.9 %collective-permute-start.118 = (bf16[256,512]{0,1:T(8,128)(2,1)S(1)}, bf16[256,512]{0,1:T(8,128)(2,1)S(1)}, u32[]{:S(2)}, u32[]{:S(2)}) collective-permute-start(bf16[256,512]{0,1:T(8,128)(2,1)S(1)} %add_convert_fusion.9), channel_id=1, source_target_pairs={{0,3},{1,0},{2,1},{3,2},{4,7},{5,4},{6,5},{7,6},{8,11},{9,8},{10,9... | collective-permute-start | bytes 786440 | tf_op jit(solution)/shard_map/ppermute | solution.py:223
  381.7 10.2 %collective-permute-done.122 = bf16[256,512]{0,1:T(8,128)(2,1)S(1)} collective-permute-done((bf16[256,512]{0,1:T(8,128)(2,1)S(1)}, bf16[256,512]{0,1:T(8,128)(2,1)S(1)}, u32[]{:S(2)}, u32[]{:S(2)}) %collective-permute-start.122) | collective-permute-done | bytes 262176 | tf_op jit(solution)/shard_map/ppermute | solution.py:223
  391.9 11.8 %collective-permute-start.110 = (bf16[256,512]{0,1:T(8,128)(2,1)S(1)}, bf16[256,512]{0,1:T(8,128)(2,1)S(1)}, u32[]{:S(2)}, u32[]{:S(2)}) collective-permute-start(bf16[256,512]{0,1:T(8,128)(2,1)S(1)} %add_convert_fusion.12), channel_id=1, source_target_pairs={{0,1},{1,2},{2,3},{3,0},{4,5},{5,6},{6,7},{7,4},{8,9},{9,10},{10,1... | collective-permute-start | bytes 786440 | tf_op jit(solution)/shard_map/ppermute | solution.py:223
  406.9 8.7 %collective-permute-done.106 = bf16[256,512]{0,1:T(8,128)(2,1)S(1)} collective-permute-done((bf16[256,512]{0,1:T(8,128)(2,1)S(1)}, bf16[256,512]{0,1:T(8,128)(2,1)S(1)}, u32[]{:S(2)}, u32[]{:S(2)}) %collective-permute-start.106) | collective-permute-done | bytes 262176 | tf_op jit(solution)/shard_map/ppermute | solution.py:223
  440.9 7.5 %collective-permute-done.50 = bf16[256,1024]{1,0:T(8,128)(2,1)} collective-permute-done((bf16[256,1024]{1,0:T(8,128)(2,1)}, bf16[256,1024]{1,0:T(8,128)(2,1)}, u32[]{:S(2)}, u32[]{:S(2)}) %collective-permute-start.50) | collective-permute-done | bytes 524320 | tf_op jit(solution)/shard_map/ppermute | solution.py:223
  456.5 7.0 convert_reduce_fusion.2
  472.2 8.2 %attend_back.5 = (bf16[1024,384]{1,0:T(8,128)(2,1)S(1)}, f32[2,2048]{1,0:T(2,128)S(1)}) custom-call(s32[1]{0:T(128)} %dynamic_slice.252.refs_0_, bf16[1024,384]{1,0:T(8,128)(2,1)S(1)} %copy-done.13, f32[2,2048]{1,0:T(2,128)S(1)} %copy-done.7, f32[2,1024]{1,0:T(2,128)S(1)} %get-tuple-element.39.refs_3_, bf16[1024,128]{1,0:T(8,128)(2,1)S(1)} %convolution_convert_fusion.22.refs_4_), custom_call_target="tpu_custom_call" | custom-call | flops 8589934592 | bytes 4194304 | tf_op jit(solution)/shard_map/attend_back/pallas_call | solution.py:164
  485.8 8.1 %attend_back.4 = (bf16[1024,384]{1,0:T(8,128)(2,1)S(1)}, f32[2,2048]{1,0:T(2,128)S(1)}) custom-call(s32[1]{0:T(128)} %dynamic_slice.252.refs_0_, bf16[1024,384]{1,0:T(8,128)(2,1)S(1)} %convolution_convert_fusion.15.refs_1_, f32[2,2048]{1,0:T(2,128)S(1)} %get-tuple-element.234.refs_2_, f32[2,1024]{1,0:T(2,128)S(1)} %get-tuple-element.37.refs_3_, ...), custom_call_target="tpu_custom_call" | custom-call | flops 8589934592 | bytes 4194304 | tf_op jit(solution)/shard_map/attend_back/pallas_call | solution.py:164
  499.0 8.5 %attend_back.6 = (bf16[1024,384]{1,0:T(8,128)(2,1)S(1)}, f32[2,2048]{1,0:T(2,128)S(1)}) custom-call(s32[1]{0:T(128)} %dynamic_slice.252.refs_0_, bf16[1024,384]{1,0:T(8,128)(2,1)S(1)} %copy-done.11, f32[2,2048]{1,0:T(2,128)S(1)} %copy-done.5, f32[2,1024]{1,0:T(2,128)S(1)} %get-tuple-element.41.refs_3_, bf16[1024,128]{1,0:T(8,128)(2,1)S(1)} %convolution_convert_fusion.21.refs_4_), custom_call_target="tpu_custom_call" | custom-call | flops 8589934592 | bytes 4194304 | tf_op jit(solution)/shard_map/attend_back/pallas_call | solution.py:164
  512.7 8.1 %attend_back.7 = (bf16[1024,384]{1,0:T(8,128)(2,1)S(1)}, f32[2,2048]{1,0:T(2,128)S(1)}) custom-call(s32[1]{0:T(128)} %dynamic_slice.252.refs_0_, bf16[1024,384]{1,0:T(8,128)(2,1)S(1)} %copy-done.9, f32[2,2048]{1,0:T(2,128)S(1)} %copy-done.3, f32[2,1024]{1,0:T(2,128)S(1)} %get-tuple-element.43.refs_3_, bf16[1024,128]{1,0:T(8,128)(2,1)S(1)} %convolution_convert_fusion.20.refs_4_), custom_call_target="tpu_custom_call" | custom-call | flops 8589934592 | bytes 4194304 | tf_op jit(solution)/shard_map/attend_back/pallas_call | solution.py:164
  596.2 7.0 collective-permute-start.95
  617.9 6.3 collective-permute-start.60
  624.5 7.4 %collective-permute-start.79 = (f32[128,384]{0,1:T(8,128)S(1)}, f32[128,384]{0,1:T(8,128)S(1)}, u32[]{:S(2)}, u32[]{:S(2)}) collective-permute-start(f32[128,384]{0,1:T(8,128)S(1)} %get-tuple-element.219), channel_id=1, source_target_pairs={{0,4},{1,5},{2,6},{3,7},{4,0},{5,1},{6,2},{7,3},{8,12},{9,13},{10,... | collective-permute-start | bytes 589832 | tf_op jit(solution)/shard_map/ppermute | solution.py:223
  636.0 5.9 stack.152
  675.6 7.2 %collective-permute-start.61 = (bf16[256,1024]{1,0:T(8,128)(2,1)}, bf16[256,1024]{1,0:T(8,128)(2,1)}, u32[]{:S(2)}, u32[]{:S(2)}) collective-permute-start(bf16[256,1024]{1,0:T(8,128)(2,1)} %get-tuple-element.162), channel_id=1, source_target_pairs={{2,5},{3,6},{4,3},{5,0},{10,13},{11,14},{12,11},{13,8},{18,21},{19... | collective-permute-start | bytes 1572872 | tf_op jit(solution)/shard_map/ppermute | solution.py:223
  699.8 6.1 collective-permute-done.62
  (931 shorter events, 490.1 us)
Async XLA Ops:
  2.4 48.4 %collective-permute-start.8 = (f32[576]{0:T(1024)S(1)}, f32[576]{0:T(1024)S(1)}, u32[]{:S(2)}, u32[]{:S(2)}) collective-permute-start(f32[576]{0:T(1024)S(1)} %pad_maximum_fusion.31), channel_id=1, source_target_pairs={{0,1},{1,2},{2,3},{3,0},{4,5},{5,6},{6,7},{7,4},{8,9},{9,10},{10,1... | collective-permute-start | bytes 6920 | tf_op jit(solution)/shard_map/ppermute | solution.py:223
  4.5 46.4 %collective-permute-start.9 = (f32[576]{0:T(1024)S(1)}, f32[576]{0:T(1024)S(1)}, u32[]{:S(2)}, u32[]{:S(2)}) collective-permute-start(f32[576]{0:T(1024)S(1)} %pad_maximum_fusion.31), channel_id=1, source_target_pairs={{0,2},{1,3},{2,0},{3,1},{4,6},{5,7},{6,4},{7,5},{8,10},{9,11},{10,... | collective-permute-start | bytes 6920 | tf_op jit(solution)/shard_map/ppermute | solution.py:223
  6.8 44.9 %collective-permute-start.10 = (f32[576]{0:T(1024)S(1)}, f32[576]{0:T(1024)S(1)}, u32[]{:S(2)}, u32[]{:S(2)}) collective-permute-start(f32[576]{0:T(1024)S(1)} %pad_maximum_fusion.31), channel_id=1, source_target_pairs={{0,3},{1,0},{2,1},{3,2},{4,7},{5,4},{6,5},{7,6},{8,11},{9,8},{10,9... | collective-permute-start | bytes 6920 | tf_op jit(solution)/shard_map/ppermute | solution.py:223
  15.1 37.8 %collective-permute-start.11 = (bf16[256,512]{0,1:T(8,128)(2,1)}, bf16[256,512]{0,1:T(8,128)(2,1)}, u32[]{:S(2)}, u32[]{:S(2)}) collective-permute-start(bf16[256,512]{0,1:T(8,128)(2,1)} %get-tuple-element.186), channel_id=1, source_target_pairs={{0,1},{1,2},{2,3},{3,0},{4,5},{5,6},{6,7},{7,4},{8,9},{9,10},{10,1... | collective-permute-start | bytes 786440 | tf_op jit(solution)/shard_map/ppermute | solution.py:223
  15.5 29.6 %collective-permute-start.7 = (s32[2]{0:T(128)S(1)}, s32[2]{0:T(128)S(1)}, u32[]{:S(2)}, u32[]{:S(2)}) collective-permute-start(s32[2]{0:T(128)S(1)} %copy-done.172), channel_id=1, source_target_pairs={{0,4},{1,5},{2,6},{3,7},{4,0},{5,1},{6,2},{7,3},{8,12},{9,13},{10,... | collective-permute-start | bytes 32 | tf_op jit(solution)/shard_map/ppermute | solution.py:223
  65.4 44.9 %collective-permute-start.32 = (bf16[256,512]{1,0:T(8,128)(2,1)}, bf16[256,512]{1,0:T(8,128)(2,1)S(1)}, u32[]{:S(2)}, u32[]{:S(2)}) collective-permute-start(bf16[256,512]{1,0:T(8,128)(2,1)} %get-tuple-element.184), channel_id=1, source_target_pairs={{0,2},{1,3},{2,0},{3,1},{4,6},{5,7},{6,4},{7,5},{8,10},{9,11},{10,... | collective-permute-start | bytes 786440 | tf_op jit(solution)/shard_map/ppermute | solution.py:223
  65.5 50.6 %collective-permute-start.36 = (bf16[256,512]{0,1:T(8,128)(2,1)S(1)}, bf16[256,512]{0,1:T(8,128)(2,1)}, u32[]{:S(2)}, u32[]{:S(2)}) collective-permute-start(bf16[256,512]{0,1:T(8,128)(2,1)S(1)} %get-tuple-element.180), channel_id=1, source_target_pairs={{0,2},{1,3},{2,0},{3,1},{4,6},{5,7},{6,4},{7,5},{8,10},{9,11},{10,... | collective-permute-start | bytes 786440 | tf_op jit(solution)/shard_map/ppermute | solution.py:223
  76.6 42.3 %collective-permute-start.52 = (bf16[256,1024]{1,0:T(8,128)(2,1)S(1)}, bf16[256,1024]{1,0:T(8,128)(2,1)S(1)}, u32[]{:S(2)}, u32[]{:S(2)}) collective-permute-start(bf16[256,1024]{1,0:T(8,128)(2,1)S(1)} %get-tuple-element.166), channel_id=1, source_target_pairs={{0,4},{1,5},{6,2},{7,3},{8,12},{9,13},{14,10},{15,11},{16,20},{17,... | collective-permute-start | bytes 1572872 | tf_op jit(solution)/shard_map/ppermute | solution.py:223
  78.0 42.7 %collective-permute-start = (bf16[256,1024]{1,0:T(8,128)(2,1)S(1)}, bf16[256,1024]{1,0:T(8,128)(2,1)S(1)}, u32[]{:S(2)}, u32[]{:S(2)}) collective-permute-start(bf16[256,1024]{1,0:T(8,128)(2,1)S(1)} %get-tuple-element.192), channel_id=1, source_target_pairs={{0,4},{1,5},{6,2},{7,3},{8,12},{9,13},{14,10},{15,11},{16,20},{17,... | collective-permute-start | bytes 1572872 | tf_op jit(solution)/shard_map/ppermute | solution.py:223
  83.2 76.0 %collective-permute-start.1 = (bf16[256,1024]{1,0:T(8,128)(2,1)}, bf16[256,1024]{1,0:T(8,128)(2,1)S(1)}, u32[]{:S(2)}, u32[]{:S(2)}) collective-permute-start(bf16[256,1024]{1,0:T(8,128)(2,1)} %get-tuple-element.191), channel_id=1, source_target_pairs={{0,1},{3,0},{5,6},{6,7},{8,9},{11,8},{13,14},{14,15},{16,17},{19,1... | collective-permute-start | bytes 1572872 | tf_op jit(solution)/shard_map/ppermute | solution.py:223
  110.4 50.1 %collective-permute-start.3 = (bf16[256,1024]{1,0:T(8,128)(2,1)}, bf16[256,1024]{1,0:T(8,128)(2,1)S(1)}, u32[]{:S(2)}, u32[]{:S(2)}) collective-permute-start(bf16[256,1024]{1,0:T(8,128)(2,1)} %get-tuple-element.190), channel_id=1, source_target_pairs={{2,0},{3,1},{4,6},{5,7},{10,8},{11,9},{12,14},{13,15},{18,16},{19,... | collective-permute-start | bytes 1572872 | tf_op jit(solution)/shard_map/ppermute | solution.py:223
  171.9 47.5 %collective-permute-start.53 = (bf16[256,1024]{1,0:T(8,128)(2,1)}, bf16[256,1024]{1,0:T(8,128)(2,1)}, u32[]{:S(2)}, u32[]{:S(2)}) collective-permute-start(bf16[256,1024]{1,0:T(8,128)(2,1)} %get-tuple-element.165), channel_id=1, source_target_pairs={{0,1},{3,0},{5,6},{6,7},{8,9},{11,8},{13,14},{14,15},{16,17},{19,1... | collective-permute-start | bytes 1572872 | tf_op jit(solution)/shard_map/ppermute | solution.py:223
  173.4 46.5 %collective-permute-start.37 = (bf16[256,512]{0,1:T(8,128)(2,1)}, bf16[256,512]{0,1:T(8,128)(2,1)}, u32[]{:S(2)}, u32[]{:S(2)}) collective-permute-start(bf16[256,512]{0,1:T(8,128)(2,1)} %collective-permute-done.36), channel_id=1, source_target_pairs={{0,8},{1,9},{2,10},{3,11},{4,12},{5,13},{6,14},{7,15},{8,0},{9,1},... | collective-permute-start | bytes 786440 | tf_op jit(solution)/shard_map/ppermute | solution.py:223
  174.3 48.2 %collective-permute-start.38 = (bf16[256,512]{0,1:T(8,128)(2,1)}, bf16[256,512]{0,1:T(8,128)(2,1)}, u32[]{:S(2)}, u32[]{:S(2)}) collective-permute-start(bf16[256,512]{0,1:T(8,128)(2,1)} %collective-permute-done.36), channel_id=1, source_target_pairs={{0,16},{1,17},{2,18},{3,19},{4,20},{5,21},{6,22},{7,23},{8,24},{9,... | collective-permute-start | bytes 786440 | tf_op jit(solution)/shard_map/ppermute | solution.py:223
  177.8 47.1 %collective-permute-start.43 = (bf16[256,512]{1,0:T(8,128)(2,1)}, bf16[256,512]{1,0:T(8,128)(2,1)}, u32[]{:S(2)}, u32[]{:S(2)}) collective-permute-start(bf16[256,512]{1,0:T(8,128)(2,1)} %collective-permute-done.41), channel_id=1, source_target_pairs={{0,16},{1,17},{2,18},{3,19},{4,20},{5,21},{6,22},{7,23},{8,24},{9,... | collective-permute-start | bytes 786440 | tf_op jit(solution)/shard_map/ppermute | solution.py:223
  183.4 46.2 %collective-permute-start.47 = (bf16[256,512]{0,1:T(8,128)(2,1)}, bf16[256,512]{0,1:T(8,128)(2,1)}, u32[]{:S(2)}, u32[]{:S(2)}) collective-permute-start(bf16[256,512]{0,1:T(8,128)(2,1)} %collective-permute-done.46), channel_id=1, source_target_pairs={{0,8},{1,9},{2,10},{3,11},{4,12},{5,13},{6,14},{7,15},{8,0},{9,1},... | collective-permute-start | bytes 786440 | tf_op jit(solution)/shard_map/ppermute | solution.py:223
  286.2 45.2 %collective-permute-start.115 = (bf16[256,512]{0,1:T(8,128)(2,1)}, bf16[256,512]{0,1:T(8,128)(2,1)}, u32[]{:S(2)}, u32[]{:S(2)}) collective-permute-start(bf16[256,512]{0,1:T(8,128)(2,1)} %get-tuple-element.140), channel_id=1, source_target_pairs={{0,8},{1,9},{2,10},{3,11},{4,12},{5,13},{6,14},{7,15},{8,0},{9,1},... | collective-permute-start | bytes 786440 | tf_op jit(solution)/shard_map/ppermute | solution.py:223
  288.4 44.3 %collective-permute-start.119 = (bf16[256,512]{0,1:T(8,128)(2,1)}, bf16[256,512]{0,1:T(8,128)(2,1)}, u32[]{:S(2)}, u32[]{:S(2)}) collective-permute-start(bf16[256,512]{0,1:T(8,128)(2,1)} %get-tuple-element.142), channel_id=1, source_target_pairs={{0,16},{1,17},{2,18},{3,19},{4,20},{5,21},{6,22},{7,23},{8,24},{9,... | collective-permute-start | bytes 786440 | tf_op jit(solution)/shard_map/ppermute | solution.py:223
  309.4 30.9 %collective-permute-start.123 = (bf16[256,512]{0,1:T(8,128)(2,1)S(1)}, bf16[256,512]{0,1:T(8,128)(2,1)S(1)}, u32[]{:S(2)}, u32[]{:S(2)}) collective-permute-start(bf16[256,512]{0,1:T(8,128)(2,1)S(1)} %copy-done.129), channel_id=1, source_target_pairs={{0,8},{1,9},{2,10},{3,11},{4,12},{5,13},{6,14},{7,15},{8,0},{9,1},... | collective-permute-start | bytes 786440 | tf_op jit(solution)/shard_map/ppermute | solution.py:223
  373.4 46.0 %collective-permute-start.48 = (bf16[512,1024]{1,0:T(8,128)(2,1)S(1)}, bf16[512,1024]{1,0:T(8,128)(2,1)S(1)}, u32[]{:S(2)}, u32[]{:S(2)}) collective-permute-start(bf16[512,1024]{1,0:T(8,128)(2,1)S(1)} %pad_maximum_fusion.5), channel_id=1, source_target_pairs={{0,4},{1,5},{2,6},{3,7},{4,0},{5,1},{6,2},{7,3},{8,12},{9,13},{10,... | collective-permute-start | bytes 3145736 | tf_op jit(solution)/shard_map/ppermute | solution.py:223
  403.9 47.3 %collective-permute-start.59 = (bf16[1024,1024]{1,0:T(8,128)(2,1)}, bf16[1024,1024]{1,0:T(8,128)(2,1)}, u32[]{:S(2)}, u32[]{:S(2)}) collective-permute-start(bf16[1024,1024]{1,0:T(8,128)(2,1)} %add_convert_fusion.1), channel_id=1, source_target_pairs={{0,4},{1,5},{2,6},{3,7},{4,0},{5,1},{6,2},{7,3},{8,12},{9,13},{10,... | collective-permute-start | bytes 6291464 | tf_op jit(solution)/shard_map/ppermute | solution.py:223
  526.9 37.7 %collective-permute-start.81 = (bf16[256,128]{0,1:T(8,128)(2,1)}, bf16[256,128]{0,1:T(8,128)(2,1)S(1)}, u32[]{:S(2)}, u32[]{:S(2)}) collective-permute-start(bf16[256,128]{0,1:T(8,128)(2,1)} %get-tuple-element.222), channel_id=1, source_target_pairs={{0,16},{1,17},{2,18},{3,19},{4,20},{5,21},{6,22},{7,23},{8,24},{9,... | collective-permute-start | bytes 196616 | tf_op jit(solution)/shard_map/ppermute | solution.py:223
  528.9 36.7 %collective-permute-start.84 = (bf16[256,128]{0,1:T(8,128)(2,1)}, bf16[256,128]{0,1:T(8,128)(2,1)S(1)}, u32[]{:S(2)}, u32[]{:S(2)}) collective-permute-start(bf16[256,128]{0,1:T(8,128)(2,1)} %get-tuple-element.224), channel_id=1, source_target_pairs={{0,8},{1,9},{2,10},{3,11},{4,12},{5,13},{6,14},{7,15},{8,0},{9,1},... | collective-permute-start | bytes 196616 | tf_op jit(solution)/shard_map/ppermute | solution.py:223
  617.9 40.5 %collective-permute-start.60 = (bf16[512,1024]{1,0:T(8,128)(2,1)}, bf16[512,1024]{1,0:T(8,128)(2,1)}, u32[]{:S(2)}, u32[]{:S(2)}) collective-permute-start(bf16[512,1024]{1,0:T(8,128)(2,1)} %pad_maximum_fusion.9), channel_id=1, source_target_pairs={{0,4},{1,5},{2,6},{3,7},{4,0},{5,1},{6,2},{7,3},{8,12},{9,13},{10,... | collective-permute-start | bytes 3145736 | tf_op jit(solution)/shard_map/ppermute | solution.py:223
  (298 other events, 4100.3 us)
where the time goes:
time: 720 us; the launch traced here: 710 us
  starting transfers between devices  228 us (32%)
  waiting for transfers between devices  159 us (22%)
  matrix products  90.8 us (13%)
  local copies, waits for them, and re-layouts  88.9 us (12%)
  other arithmetic  82.2 us (11%)
  Pallas kernels  49 us (7%)
  between operations  11.5 us (2%)
    ppermute x149, starting transfers between devices, move(): return lax.ppermute(values, ('dp', 'mp'), pairs)  228 us
    ppermute x149, waiting for transfers between devices, move(): return lax.ppermute(values, ('dp', 'mp'), pairs)  159 us
    dot_general x16, matrix products, dot_nt(): lax.dot_general(left, right, (((1,), (1,)), ((), ())), preferred_element_...  39.3 us
    unnamed x385, local copies, waits for them, and re-layouts  33.2 us
    pallas_call x4, Pallas kernels, attend_back(): pl.pallas_call(lambda *refs: attend_back_kernel(heads, *refs), out_shape=...  32.9 us
    dot_general x16, matrix products, dot_nn(): lax.dot_general(left, right, (((1,), (0,)), ((), ())), preferred_element_...  27.8 us
    dot_general x16, matrix products, dot_tn(): lax.dot_general(left, right, (((0,), (0,)), ((), ())), preferred_element_...  23.3 us
    pallas_call x4, Pallas kernels, attend(): pl.pallas_call(lambda *refs: attend_kernel(heads, *refs), out_shape=(jax....  16.1 us
  transfers between devices with their start and end apart: 149, of which 53 were waited for; matrix products, arithmetic and copies ran while one was open for 24% of the time, Pallas kernels for 2%

commit v1 on v0

--- a/solution.py
+++ b/solution.py
@@ -15,7 +15,8 @@
 weight_decay = 0.1
 masked_score = -1000000000.0
 score_scale = HD ** (-0.5)
-kernel_bytes = 48 << 20
+kernel_bytes = 16 << 20
+back_bytes = 24 << 20
 
 in_vmem = pl.BlockSpec(memory_space=pltpu.VMEM)
 in_smem = pl.BlockSpec(memory_space=pltpu.SMEM)
@@ -174,7 +175,7 @@
             pltpu.VMEM((rows, HD), f32),
             pltpu.VMEM((rows // tile, tile, tile), f32),
         ],
-        compiler_params=pltpu.CompilerParams(vmem_limit_bytes=kernel_bytes),
+        compiler_params=pltpu.CompilerParams(vmem_limit_bytes=back_bytes),
         cost_estimate=pl.CostEstimate(
             flops=heads * rows * rows * HD * 64,
             bytes_accessed=4 << 20,
@@ -182,6 +183,14 @@
         ),
         name="attend_back",
     )(length, qkv, line, lse, grad)
+
+
+def tie(*values):
+    return lax.optimization_barrier(values)
+
+
+def after(values, *others):
+    return lax.optimization_barrier((values, *others))[0]
 
 
 class Places:
@@ -198,6 +207,7 @@
         self.dp_i, self.mp_i = dp_i, mp_i
         self.q, self.c = dp_i // 2, lax.rem(dp_i, 2)
         self.s, self.t = mp_i // self.t_n, lax.rem(mp_i, self.t_n)
+        assert per == 2
         self.home = self.s // per
         self.at_home = self.c == self.home
         self.q_bits = []
@@ -226,7 +236,7 @@
         return self.move(values, lambda q, c, s, t: (q, 1 - c, s, t))
 
     def to_slot(self, values, step):
-        return self.move(values, lambda q, c, s, t: (q, c, (s + step) % self.slots, t))
+        return self.move(values, lambda q, c, s, t: (q, c, s ^ step, t))
 
     def to_chip(self, values, bit):
         return self.move(values, lambda q, c, s, t: (q ^ bit, c, s, t))
@@ -247,66 +257,53 @@
     def block_at(self, step):
         return lax.rem(self.s + step, self.slots) * self.t_n + self.t
 
-    def collect(self, local):
-        count, width = local.shape[1:]
-        whole = jnp.zeros((count * self.mp_n, width), local.dtype)
-        for step in range(self.slots):
-            slot = lax.rem(self.s + step, self.slots)
-            piece = lax.dynamic_index_in_dim(
-                local, jnp.clip(slot - self.per * self.c, 0, self.per - 1), 0, keepdims=False
-            )
-            if step > 0:
-                piece = self.move(
-                    piece,
-                    lambda q, c, s, t: (
-                        (q, c, (s + step) % self.slots, t)
-                        if (s + step) % self.slots // self.per == c
-                        else None
-                    ),
-                )
-            other = self.move(
-                piece, lambda q, c, s, t: (q, 1 - c, s, t) if c == s // self.per else None
-            )
-            piece = jnp.where(self.at_home, piece, other)
-            origin = lax.rem(self.s + self.slots - step, self.slots)
+    def collect_piece(self, local, step):
+        piece = lax.dynamic_index_in_dim(local, (self.s ^ step) % 2, 0, keepdims=False)
+        if step == 0:
+            return piece
+        return self.move(
+            piece,
+            lambda q, c, s, t: (
+                (q, c, s ^ step, t) if (s ^ step) // self.per == c else None
+            ),
+        )
+
+    def collect_end(self, pieces):
+        count, width = pieces[0].shape
+        whole = jnp.zeros((count * self.mp_n, width), pieces[0].dtype)
+        for step, piece in enumerate(pieces):
             for turn in range(self.t_n):
-                got = self.to_team(piece, turn) if turn > 0 else piece
+                piece_t = self.to_team(piece, turn) if turn > 0 else piece
                 from_t = lax.rem(self.t + self.t_n - turn, self.t_n)
                 whole = lax.dynamic_update_slice_in_dim(
-                    whole, got, (origin * self.t_n + from_t) * count, 0
+                    whole, piece_t, ((self.s ^ step) * self.t_n + from_t) * count, 0
                 )
         return whole
 
-    def deliver(self, blocks):
-        arrived = []
-        for step in range(self.slots):
-            flip, index = step // self.per, step % self.per
-            value = blocks[index]
-            if step > 0:
-                value = self.move(
-                    value,
-                    lambda q, c, s, t: (
-                        (q, s // self.per, (s + step) % self.slots, t)
-                        if c == (s // self.per) ^ flip
-                        else None
-                    ),
-                )
-            arrived.append(value)
-        results = []
-        for index in range(self.per):
-            slot = self.per * self.c + index
-            step = lax.rem(self.s + self.slots - slot, self.slots)
-            picked = arrived[0]
-            for number in range(1, self.slots):
-                picked = jnp.where(step == number, arrived[number], picked)
-            results.append(picked)
-        return jnp.stack(results)
+    def collect_both(self, whole):
+        other = self.move(
+            whole, lambda q, c, s, t: (q, 1 - c, s, t) if c == s // self.per else None
+        )
+        return jnp.where(self.at_home, whole, other)
+
+    def deliver_first(self, blocks):
+        got = self.move(
+            blocks, lambda q, c, s, t: (q, 1 - c, s ^ 2, t) if c != s // 2 else None
+        )
+        return jnp.where(self.at_home, blocks, got)
+
+    def deliver_second(self, pair):
+        count = pair.shape[0] // 2
+        got = self.to_slot(pair[count:], 1)
+        mine = pair[:count]
+        even = self.s % 2 == 0
+        return jnp.stack([jnp.where(even, mine, got), jnp.where(even, got, mine)])
 
     def share(self, values, length, flip, team):
         side = jnp.where(self.at_home, 0, 1) ^ flip
         parts = []
         for index in range(self.per):
-            slot = lax.rem(self.s + self.per * side + index, self.slots)
+            slot = self.s ^ (self.per * side + index)
             block = slot * self.t_n + lax.rem(self.t + team, self.t_n)
             parts.append(lax.dynamic_slice_in_dim(values, block * length, length, 0))
         return jnp.concatenate(parts, axis=0)
@@ -331,24 +328,73 @@
                 total = total + self.to_team(low, team).astype(f32)
         return total
 
-    def gather_chips(self, piece, first_bit):
-        bits = self.q_bits if first_bit == 0 else self.q_bits[::-1]
+    def spread_inner(self, own, one):
+        both = jnp.concatenate([own, one], axis=1)
+        return self.move(both, lambda q, c, s, t: (q, c, s ^ 3, t) if s in (1, 2) else None)
+
+    def spread_outer(self, inner):
+        return self.move(inner, lambda q, c, s, t: (q, c, s ^ 1, t) if s in (1, 2) else None)
+
+    def spread_pair(self, inner, outer):
+        size = inner.shape[1] // 2
+        turned = jnp.concatenate([inner[:, size:], inner[:, :size]], axis=1)
+        return jnp.where((self.s == 1) | (self.s == 2), turned, outer)
+
+    def fold_outer(self, far):
+        size = far.shape[1] // 2
+        got = self.move(far, lambda q, c, s, t: (q, c, s ^ 1, t) if s in (0, 3) else None)
+        return far.astype(f32) + jnp.concatenate([got[:, size:], got[:, :size]], axis=1).astype(f32)
+
+    def fold_inner(self, far):
+        size = far.shape[1] // 2
+        got = self.move(
+            far.astype(bf16), lambda q, c, s, t: (q, c, s ^ 3, t) if s in (1, 2) else None
+        ).astype(f32)
+        return got[:, :size], got[:, size:]
+
+    def bits_from(self, first):
+        return self.q_bits[first:] + self.q_bits[:first]
+
+    def gather_chips(self, piece, first):
         pieces = {0: piece}
-        for bit in bits:
+        for bit in self.bits_from(first):
             for k in list(pieces):
                 pieces[k | bit] = self.to_chip(pieces[k], bit)
-        return jnp.concatenate([pieces[k] for k in range(self.q_n)], axis=0)
-
-    def scatter_chips(self, values, first_bit):
-        count = values.shape[0] // self.q_n
-        bits = self.q_bits if first_bit == 0 else self.q_bits[::-1]
-        pieces = {k: values[k * count : (k + 1) * count] for k in range(self.q_n)}
+        return [pieces[k] for k in range(self.q_n)]
+
+    def gather_start(self, piece):
+        return {bit: self.to_chip(piece, bit) for bit in self.q_bits}
+
+    def gather_end(self, piece, near, first):
+        pieces = {0: piece}
+        for bit in self.bits_from(first):
+            for k in list(pieces):
+                pieces[k | bit] = near[bit] if k == 0 else self.to_chip(pieces[k], bit)
+        return [pieces[k] for k in range(self.q_n)]
+
+    def scatter_order(self, first):
+        order = [0]
+        for bit in reversed(self.bits_from(first)):
+            order = order + [k | bit for k in order]
+        return order
+
+    def scatter_first(self, kept, sent, first):
+        got = self.to_chip(sent, self.bits_from(first)[0])
+        half = kept.shape[0] // 2
+        if len(self.q_bits) == 1:
+            return kept.astype(f32) + got.astype(f32), None
+        sent_on = (kept[half:].astype(f32) + got[half:].astype(f32)).astype(bf16)
+        return kept[:half].astype(f32) + got[:half].astype(f32), sent_on
+
+    def scatter_rest(self, halves, first):
+        total, sent = halves
+        bits = self.bits_from(first)[1:]
         for number, bit in enumerate(bits):
-            last = number == len(bits) - 1
-            for k in [k for k in pieces if k & bit]:
-                got = self.to_chip(pieces.pop(k).astype(bf16), bit).astype(f32)
-                pieces[k ^ bit] = pieces[k ^ bit].astype(f32) + got
-        return pieces[0]
+            total = total + self.to_chip(sent, bit).astype(f32)
+            if number + 1 < len(bits):
+                half = total.shape[0] // 2
+                total, sent = total[:half], total[half:].astype(bf16)
+        return total
 
     def sum_all(self, values, chips_only=False):
         if not chips_only:
@@ -385,6 +431,264 @@
         return values
 
 
+def pack_attn_kernel(place_ref, qkv_ref, out_ref, qkv_full, out_full, piece_ref):
+    size = qkv_ref.shape[2]
+    for j in range(3):
+        qkv_full[:, j * size : (j + 1) * size] = qkv_ref[j].astype(bf16)
+    out_full[...] = out_ref[...].T.astype(bf16)
+
+    @pl.when(pl.program_id(0) == 0)
+    def _():
+        piece_ref[:, : 3 * size] = qkv_full[...]
+        piece_ref[:, 3 * size :] = out_full[...]
+
+
+def pack_mlp_kernel(place_ref, up_ref, down_ref, up_full, down_full, up_piece, down_piece):
+    up_full[...] = up_ref[...].astype(bf16)
+    down_full[...] = down_ref[...].T.astype(bf16)
+
+    @pl.when(pl.program_id(0) == 0)
+    def _():
+        up_piece[...] = up_full[...]
+        down_piece[...] = down_full[...]
+
+
+def packs_in_kernels(at, width, head_width):
+    return (width // at.q_n) % 128 == 0 and head_width % 128 == 0
+
+
+def pack_attn(at, qkv_weight, out_weight, head_width, after):
+    width = qkv_weight.shape[0]
+    part = width // at.q_n
+    if packs_in_kernels(at, width, head_width):
+        place = tie(jnp.stack([at.q, at.c]).astype(jnp.int32), after)[0]
+        sizes = (3 * head_width, head_width)
+        return pl.pallas_call(
+            pack_attn_kernel,
+            grid_spec=pltpu.PrefetchScalarGridSpec(
+                num_scalar_prefetch=1,
+                grid=(at.q_n,),
+                in_specs=[
+                    pl.BlockSpec((3, part, head_width), lambda k, p: (0, p[0] ^ k, p[1])),
+                    pl.BlockSpec((head_width, part), lambda k, p: (p[1], p[0] ^ k)),
+                ],
+                out_specs=tuple(pl.BlockSpec((part, n), lambda k, p: (k, 0)) for n in sizes)
+                + (pl.BlockSpec((part, sum(sizes)), lambda k, p: (0, 0)),),
+            ),
+            out_shape=tuple(jax.ShapeDtypeStruct((width, n), bf16) for n in sizes)
+            + (jax.ShapeDtypeStruct((part, sum(sizes)), bf16),),
+            name="pack_attn",
+        )(place, jnp.transpose(qkv_weight, (1, 0, 2)), out_weight)
+    qkv = lax.dynamic_slice_in_dim(qkv_weight, at.c * head_width, head_width, 2)
+    out = lax.dynamic_slice_in_dim(out_weight, at.c * head_width, head_width, 0)
+    qkv = at.relative(qkv.reshape(width, 3 * head_width).astype(bf16), 0)
+    out = at.relative(out.astype(bf16).T, 0)
+    return qkv, out, jnp.concatenate([qkv[:part], out[:part]], axis=1)
+
+
+def pack_mlp(at, up_weight, down_weight, head_width, units, after):
+    width = up_weight.shape[0]
+    part = width // at.q_n
+    if packs_in_kernels(at, width, head_width):
+        place = tie(jnp.stack([at.q, at.c]).astype(jnp.int32), after)[0]
+        return pl.pallas_call(
+            pack_mlp_kernel,
+            grid_spec=pltpu.PrefetchScalarGridSpec(
+                num_scalar_prefetch=1,
+                grid=(at.q_n,),
+                in_specs=[
+                    pl.BlockSpec((part, units), lambda k, p: (p[0] ^ k, p[1])),
+                    pl.BlockSpec((units, part), lambda k, p: (p[1], p[0] ^ k)),
+                ],
+                out_specs=(
+                    pl.BlockSpec((part, units), lambda k, p: (k, 0)),
+                    pl.BlockSpec((part, units), lambda k, p: (k, 0)),
+                    pl.BlockSpec((part, units), lambda k, p: (0, 0)),
+                    pl.BlockSpec((part, units), lambda k, p: (0, 0)),
+                ),
+            ),
+            out_shape=(jax.ShapeDtypeStruct((width, units), bf16),) * 2
+            + (jax.ShapeDtypeStruct((part, units), bf16),) * 2,
+            name="pack_mlp",
+        )(place, up_weight, down_weight)
+    up = lax.dynamic_slice_in_dim(up_weight, at.c * units, units, 1).astype(bf16)
+    down = lax.dynamic_slice_in_dim(down_weight, at.c * units, units, 0).astype(bf16).T
+    up, down = at.relative(up, 0), at.relative(down, 0)
+    return up, down, up[:part], down[:part]
+
+
+def halves_kernel(order, shape, *refs):
+    operands, (kept_ref, sent_ref) = refs[:-2], refs[-2:]
+    part = operands[0].shape[1] // len(order)
+    middle = len(order) // 2
+    for index, block in enumerate(order):
+        target = kept_ref if index < middle else sent_ref
+        rows = slice(index % middle * part, (index % middle + 1) * part)
+        col = 0
+        number = 0
+        for count in shape:
+            left = operands[number][:, block * part : (block + 1) * part]
+            number += 1
+            for _ in range(count):
+                right_ref = operands[number]
+                number += 1
+                size = right_ref.shape[1]
+                target[rows, col : col + size] = dot_tn(left, right_ref[...]).astype(bf16)
+                col += size
+
+
+def grad_halves(at, pairs, first):
+    rows, width = pairs[0][0].shape
+    part = width // at.q_n
+    order = at.scatter_order(first)
+    middle = at.q_n // 2
+    cols = sum(right.shape[1] for _, rights in pairs for right in rights)
+    if part % 128 == 0:
+        halves = jax.ShapeDtypeStruct((middle * part, cols), bf16)
+        operands = [value for left, rights in pairs for value in (left, *rights)]
+        return pl.pallas_call(
+            lambda *refs: halves_kernel(order, [len(rights) for _, rights in pairs], *refs),
+            in_specs=[in_vmem] * len(operands),
+            out_specs=(in_vmem, in_vmem),
+            out_shape=(halves, halves),
+            compiler_params=pltpu.CompilerParams(vmem_limit_bytes=kernel_bytes),
+            cost_estimate=pl.CostEstimate(
+                flops=3 * rows * width * cols, bytes_accessed=1 << 20, transcendentals=0
+            ),
+            name="grad_halves",
+        )(*operands)
+    return tuple(
+        jnp.concatenate(
+            [
+                jnp.concatenate(
+                    [
+                        dot_tn(left[:, k * part : (k + 1) * part], right).astype(bf16)
+                        for left, rights in pairs
+                        for right in rights
+                    ],
+                    axis=1,
+                )
+                for k in side
+            ],
+            axis=0,
+        )
+        for side in (order[:middle], order[middle:])
+    )
+
+
+def adjust(weight, first, second, gradient, decay_rate, first_fix, second_fix):
+    first_new = 0.9 * first + 0.1 * gradient
+    second_new = 0.999 * second + 0.001 * gradient * gradient
+    update = (
+        first_new / first_fix / (jnp.sqrt(second_new / second_fix) + adam_eps) + decay_rate * weight
+    )
+    return (first_new, second_new, update)
+
+
+def in_order(c, mine, other):
+    return jnp.where(c == 0, mine, other), jnp.where(c == 0, other, mine)
+
+
+def adjust_into(index, weight, moments_ref, gradient, fixes_ref, state_ref, update_ref, sums_ref):
+    first_new, second_new, update = adjust(
+        weight, moments_ref[0], moments_ref[1], gradient, weight_decay, fixes_ref[0], fixes_ref[1]
+    )
+    state_ref[0] = first_new
+    state_ref[1] = second_new
+    update_ref[...] = update
+    sums_ref[2 * index] = jnp.sum(weight * weight)
+    sums_ref[2 * index + 1] = jnp.sum(update * update)
+
+
+def adjust_attn_kernel(
+    place_ref, fixes_ref, mine_ref, other_ref, qkv_ref, out_ref, qkv_moments, out_moments,
+    qkv_state, out_state, qkv_update, out_update, sums_ref,
+):
+    size = qkv_ref.shape[2] // 2
+    one, two = in_order(place_ref[1], mine_ref[...], other_ref[...])
+    parts = [
+        jnp.concatenate([one[:, j * size : (j + 1) * size], two[:, j * size : (j + 1) * size]], 1)
+        for j in range(4)
+    ]
+    adjust_into(
+        0, qkv_ref[...], qkv_moments, jnp.stack(parts[:3]), fixes_ref, qkv_state, qkv_update, sums_ref
+    )
+    adjust_into(
+        1, out_ref[...], out_moments, parts[3].T, fixes_ref, out_state, out_update, sums_ref
+    )
+
+
+def adjust_mlp_kernel(
+    place_ref, fixes_ref, mine_ref, other_ref, up_ref, down_ref, up_moments, down_moments,
+    up_state, down_state, up_update, down_update, sums_ref,
+):
+    size = up_ref.shape[1] // 2
+    one, two = in_order(place_ref[1], mine_ref[...], other_ref[...])
+    down_grad = jnp.concatenate([one[:, :size], two[:, :size]], axis=1)
+    up_grad = jnp.concatenate([one[:, size:], two[:, size:]], axis=1)
+    adjust_into(0, up_ref[...], up_moments, up_grad, fixes_ref, up_state, up_update, sums_ref)
+    adjust_into(
+        1, down_ref[...], down_moments, down_grad.T, fixes_ref, down_state, down_update, sums_ref
+    )
+
+
+def own_spec(shape, dim, count):
+    block = list(shape)
+    block[dim] //= count
+    return pl.BlockSpec(
+        tuple(block), lambda i, p: tuple(p[0] if d == dim else 0 for d in range(len(shape)))
+    )
+
+
+def whole_spec(shape):
+    return pl.BlockSpec(shape, lambda i, p: (0,) * len(shape))
+
+
+def adjust_pair(at, kernel, place, fixes, mine, other, weights, dims, moments):
+    parts = [m.shape[1:] for m in moments]
+    shapes = [jax.ShapeDtypeStruct(m.shape, f32) for m in moments]
+    shapes += [jax.ShapeDtypeStruct(p, f32) for p in parts]
+    return pl.pallas_call(
+        kernel,
+        grid_spec=pltpu.PrefetchScalarGridSpec(
+            num_scalar_prefetch=1,
+            grid=(1,),
+            in_specs=[in_smem, whole_spec(mine.shape), whole_spec(other.shape)]
+            + [own_spec(w.shape, d, at.dp_n) for w, d in zip(weights, dims)]
+            + [whole_spec(m.shape) for m in moments],
+            out_specs=tuple(whole_spec(s.shape) for s in shapes) + (in_smem,),
+        ),
+        out_shape=tuple(shapes) + (jax.ShapeDtypeStruct((4,), f32),),
+        compiler_params=pltpu.CompilerParams(vmem_limit_bytes=back_bytes),
+        name="adjust_pair",
+    )(place, fixes, mine, other, *weights, *moments)
+
+
+def apply_kernel(place_ref, rates_ref, *refs):
+    count = len(refs) // 3
+    for index in range(count):
+        refs[2 * count + index][...] = (
+            refs[index][...] - rates_ref[index] * refs[count + index][...]
+        )
+
+
+def apply_updates(at, place, rates, weights, dims, updates):
+    return pl.pallas_call(
+        apply_kernel,
+        grid_spec=pltpu.PrefetchScalarGridSpec(
+            num_scalar_prefetch=1,
+            grid=(1,),
+            in_specs=[in_smem]
+            + [own_spec(w.shape, d, at.dp_n) for w, d in zip(weights, dims)]
+            + [whole_spec(u.shape) for u in updates],
+            out_specs=tuple(whole_spec(u.shape) for u in updates),
+        ),
+        out_shape=tuple(jax.ShapeDtypeStruct(u.shape, f32) for u in updates),
+        compiler_params=pltpu.CompilerParams(vmem_limit_bytes=back_bytes),
+        name="apply_updates",
+    )(place, rates, *weights, *updates)
+
+
 def norm_parts(values):
     center = values - jnp.mean(values, axis=-1, keepdims=True)
     spread = jnp.mean(center * center, axis=-1, keepdims=True)
@@ -399,15 +703,6 @@
         - jnp.mean(scaled, axis=-1, keepdims=True)
         - normed * jnp.mean(scaled * normed, axis=-1, keepdims=True)
     )
-
-
-def adjust(weight, first, second, gradient, decay_rate, first_fix, second_fix):
-    first_new = 0.9 * first + 0.1 * gradient
-    second_new = 0.999 * second + 0.001 * gradient * gradient
-    update = (
-        first_new / first_fix / (jnp.sqrt(second_new / second_fix) + adam_eps) + decay_rate * weight
-    )
-    return (first_new, second_new, update)
 
 
 def gelu_parts(values):
@@ -447,17 +742,13 @@
     units = up_weight.shape[1] // 2
     bucket_count, local_heads = rel_bias.shape
 
-    inputs_low = at.collect(at.relative(tokens, 2))
-    all_lengths = lengths
-    length_grid = at.move(
-        all_lengths, lambda q, c, s, t: (q, 1 - c, s, t)
-    )
-    four = jnp.where(
+    other_lengths = at.to_core(lengths)
+    all_lengths = jnp.where(
         c == 0,
-        jnp.concatenate([all_lengths, length_grid]),
-        jnp.concatenate([length_grid, all_lengths]),
-    )
-    length = lax.dynamic_slice_in_dim(four, at.s, 1, 0)
+        jnp.concatenate([lengths, other_lengths]),
+        jnp.concatenate([other_lengths, lengths]),
+    )
+    length = lax.dynamic_slice_in_dim(all_lengths, at.s, 1, 0)
     row_keep = jnp.arange(seq_len)[:, None] < length[0]
     row_mask = row_keep.astype(f32)
     vectors = at.relative(norm_vectors, 1)
@@ -465,34 +756,115 @@
     def half(values, dim, size):
         return lax.dynamic_slice_in_dim(values, c * size, size, dim)
 
-    attn_own = at.relative(
-        jnp.concatenate(
-            [
-                half(qkv_weight, 2, head_width).reshape(width, 3 * head_width).astype(bf16),
-                half(out_weight, 0, head_width).astype(bf16).T,
-            ],
-            axis=1,
-        ),
-        0,
-    )
-    up_own = at.relative(half(up_weight, 1, units).astype(bf16), 0)
-    down_own = at.relative(half(down_weight, 0, units).astype(bf16).T, 0)
     part = width // q_n
     small_own = jnp.concatenate(
         [half(up_bias, 0, units), half(rel_bias, 1, heads).T.reshape(-1)]
     )
-    attn_w, up_w, down_w, small = [attn_own], [up_own], [down_own], [small_own]
-    for step in range(1, blocks):
-        small.append(at.to_slot(small_own, step))
-        piece = at.to_slot(attn_own[:part], step)
-        attn_w.append(at.gather_chips(piece, step % 2))
-    for step in range(1, blocks):
-        piece = at.to_slot(up_own[:part], step)
-        up_w.append(at.gather_chips(piece, 0))
-        piece = at.to_slot(down_own[:part], step)
-        down_w.append(at.gather_chips(piece, 1))
-    qkv_w = [values[:, : 3 * head_width] for values in attn_w]
-    out_w = [values[:, 3 * head_width :] for values in attn_w]
+    qkv_cols = 3 * head_width
+    attn_cols = 4 * head_width
+    high = lax.reduce_precision(small_own, 8, 7)
+    rest = small_own - high
+    mid = lax.reduce_precision(rest, 8, 7)
+    three = jnp.concatenate([high, mid, rest - mid]).astype(bf16)
+    small_rows = -(-three.size // (16 * attn_cols)) * 16
+    three = jnp.pad(three, (0, small_rows * attn_cols - three.size)).reshape(small_rows, attn_cols)
+
+    def small_of(rows_low):
+        flat = rows_low.reshape(-1).astype(f32)
+        count = small_own.size
+        return (flat[:count] + flat[count : 2 * count]) + flat[2 * count : 3 * count]
+
+    tokens_near = at.relative(tokens, 2)
+    token_pieces = {step: at.collect_piece(tokens_near, step) for step in (0, 2, 3, 1)}
+    qkv_own, out_own, attn_piece = pack_attn(
+        at, qkv_weight, out_weight, head_width, tokens_near
+    )
+    attn_piece = jnp.concatenate([attn_piece, three], axis=0)
+    attn_one = at.to_slot(attn_piece, 1)
+    up_own, down_own, up_piece, down_piece = pack_mlp(
+        at, up_weight, down_weight, head_width, units, attn_piece
+    )
+    mlp_piece = jnp.concatenate([up_piece, down_piece], axis=1)
+    attn_one = after(attn_one, token_pieces[1], mlp_piece)
+    attn_inner = at.spread_inner(attn_piece, attn_one)
+    attn_near = at.gather_start(attn_one[:part])
+    tokens_there = (after(token_pieces[2], attn_one), token_pieces[3])
+    token_pieces[2] = tokens_there[0]
+    mlp_one = at.to_slot(after(mlp_piece, *tokens_there), 1)
+    inputs_home = at.collect_end([token_pieces[k] for k in range(blocks)])
+    attn_pieces = at.gather_end(
+        attn_one[:part], {b: after(v, *tokens_there) for b, v in attn_near.items()}, 0
+    )
+    inputs_low = at.collect_both(inputs_home)
+    inputs_low = after(inputs_low, attn_inner, *attn_pieces)
+    attn_outer = at.spread_outer(attn_inner)
+    up_one, down_one = mlp_one[:, :units], mlp_one[:, units:]
+    up_inner = at.spread_inner(up_piece, up_one)
+    mlp_near = at.gather_start(mlp_one)
+    turn = 1 % len(at.q_bits)
+    attn_pair = at.spread_pair(attn_inner, attn_outer)
+    pair_first = after(attn_pair[:part], *mlp_near.values(), up_inner)
+    pair_near = at.gather_start(pair_first)
+    up_outer = at.spread_outer(after(up_inner, *mlp_near.values()))
+    down_inner = at.spread_inner(after(down_piece, up_inner, *mlp_near.values()), down_one)
+    near_done = (*pair_near.values(), up_outer, down_inner)
+    pair_near = {b: after(v, *near_done) for b, v in pair_near.items()}
+    small = [
+        small_own,
+        small_of(attn_one[part:]),
+        small_of(attn_pair[part:, :attn_cols]),
+        small_of(attn_pair[part:, attn_cols:]),
+    ]
+    qkv_w = [qkv_own, jnp.concatenate([v[:, :qkv_cols] for v in attn_pieces], axis=0)]
+    out_w = [out_own, jnp.concatenate([v[:, qkv_cols:] for v in attn_pieces], axis=0)]
+    pair_pieces = []
+    for k in range(2):
+        cols = slice(k * attn_cols, (k + 1) * attn_cols)
+        pieces = at.gather_end(
+            pair_first[:, cols], {b: v[:, cols] for b, v in pair_near.items()}, k * turn
+        )
+        pair_pieces += pieces
+        qkv_w.append(jnp.concatenate([v[:, :qkv_cols] for v in pieces], axis=0))
+        out_w.append(jnp.concatenate([v[:, qkv_cols:] for v in pieces], axis=0))
+    down_outer = at.spread_outer(after(down_inner, *near_done))
+    incoming_near = at.relative(after(cotangent, *near_done), 2)
+    incoming_pieces = {step: at.collect_piece(incoming_near, step) for step in (2, 3)}
+    mlp_near = {b: after(v, *pair_pieces) for b, v in mlp_near.items()}
+    up_one_pieces = at.gather_end(up_one, {b: v[:, :units] for b, v in mlp_near.items()}, 0)
+    down_one_pieces = at.gather_end(
+        down_one, {b: v[:, units:] for b, v in mlp_near.items()}, turn
+    )
+    one_done = (*up_one_pieces, *down_one_pieces, down_outer)
+    up_pair = after(at.spread_pair(up_inner, up_outer), *one_done)
+    up_near = at.gather_start(up_pair)
+    incoming_near = after(incoming_near, *one_done)
+    incoming_pieces.update({step: at.collect_piece(incoming_near, step) for step in (0, 1)})
+    down_pair = after(at.spread_pair(down_inner, down_outer), *up_near.values())
+
+    def pair_halves(piece, near, first):
+        halves = []
+        for k in range(2):
+            cols = slice(k * units, (k + 1) * units)
+            halves.append(
+                at.gather_end(piece[:, cols], {b: v[:, cols] for b, v in near.items()}, k * turn)
+            )
+        return [jnp.concatenate(pair, axis=1) for pair in zip(*halves)]
+
+    up_pair_pieces = pair_halves(up_pair, up_near, 0)
+    down_near = at.gather_start(down_pair)
+    down_near = {b: after(v, *up_pair_pieces) for b, v in down_near.items()}
+    down_pair_pieces = pair_halves(down_pair, down_near, turn)
+    incoming_home = at.collect_end([incoming_pieces[k] for k in range(blocks)])
+    up_w = [
+        up_own,
+        jnp.concatenate(up_one_pieces, axis=0),
+        jnp.concatenate(up_pair_pieces, axis=0),
+    ]
+    down_w = [
+        down_own,
+        jnp.concatenate(down_one_pieces, axis=0),
+        jnp.concatenate(down_pair_pieces, axis=0),
+    ]
 
     tile = tile_of(seq_len)
     tiles = seq_len // tile
@@ -511,7 +883,14 @@
     first_low = (first_normed * vectors[0] + vectors[1]).astype(bf16)
     qkv, contexts, totals = [], [], []
     for r in range(blocks):
-        qkv.append(dot_nn(first_low, qkv_w[r]).astype(bf16))
+        qkv_r = dot_nn(first_low, qkv_w[r]).astype(bf16)
+        if r == 0:
+            qkv_r = after(qkv_r, mlp_one)
+        if r == 1:
+            qkv_r = after(qkv_r, attn_outer)
+        if r == 3:
+            qkv_r = after(qkv_r, *one_done)
+        qkv.append(qkv_r)
         context, total = attend(length, qkv[r], lines[r * heads : (r + 1) * heads], heads)
         contexts.append(context)
         totals.append(total)
@@ -519,41 +898,51 @@
     for r in range(1, blocks):
         mixed = mixed + dot_nt(contexts[r], out_w[r])
     mixed = at.sum_team(jnp.where(row_keep, mixed, 0.0).astype(bf16))
+    mixed = after(mixed, *up_near.values())
     middle = inputs + (mixed + vectors[4]) * row_mask
     second_normed, second_inverse = norm_parts(middle)
     second_low = (second_normed * vectors[2] + vectors[3]).astype(bf16)
     acts, slopes = [], []
-    for r in range(blocks):
-        pre = dot_nn(second_low, up_w[r]) + small[r][:units]
+    biases = [small[0][:units], small[1][:units], jnp.concatenate([small[2][:units], small[3][:units]])]
+    for r in range(3):
+        pre = dot_nn(second_low, up_w[r]) + biases[r]
         act, slope = gelu_parts(pre)
         acts.append(act.astype(bf16))
         slopes.append(slope)
     fed = dot_nt(acts[0], down_w[0])
-    for r in range(1, blocks):
+    for r in range(1, 3):
         fed = fed + dot_nt(acts[r], down_w[r])
-    fed_share = at.sum_share(fed.astype(bf16), length_rows)
+    incoming_low = at.collect_both(incoming_home)
+    kept = jnp.where(row_keep, incoming_low, jnp.zeros_like(incoming_low))
+    fed_bias_grad = jnp.sum(kept.astype(f32), axis=0)
+    bias_grads = [None] * blocks
+
+    def back_through(r, kept=kept):
+        pre_low = (dot_nn(kept, down_w[r]) * slopes[r]).astype(bf16)
+        return pre_low, jnp.sum(pre_low.astype(f32), axis=0), dot_nt(pre_low, up_w[r])
+
+    down_far = at.scatter_first(*grad_halves(at, [(kept, [acts[2]])], 0), 0)
+    down_near_halves = grad_halves(at, [(kept, [acts[0], acts[1]])], 0)
+    fed_low = after(fed.astype(bf16), *down_near_halves)
+    fed_share = at.sum_share(fed_low, length_rows)
     middle_share = at.share(middle, length_rows, 0, 0)
     mask_share = at.share(row_mask, length_rows, 0, 0)
     out_share = (middle_share + (fed_share + vectors[5]) * mask_share).astype(bf16)
-    block_out = at.deliver(
-        [out_share[i * length_rows : (i + 1) * length_rows] for i in range(per)]
-    )
-    block_out = at.relative(block_out, 2)
-
-    incoming_low = at.collect(at.relative(cotangent, 2))
-    kept = jnp.where(row_keep, incoming_low, jnp.zeros_like(incoming_low))
-    fed_bias_grad = jnp.sum(kept.astype(f32), axis=0)
-    back = None
-    mlp_grads, bias_grads = [], []
-    for r in range(blocks):
-        down_grad = dot_tn(kept, acts[r]).astype(bf16)
-        pre_low = (dot_nn(kept, down_w[r]) * slopes[r]).astype(bf16)
-        bias_grads.append(jnp.sum(pre_low.astype(f32), axis=0))
-        up_grad = dot_tn(second_low, pre_low).astype(bf16)
-        term = dot_nt(pre_low, up_w[r])
-        back = term if back is None else back + term
-        mlp_grads.append((up_grad, down_grad))
-    second_grad = at.sum_team(back.astype(bf16))
+    pre_pair, bias_pair, back = back_through(2)
+    bias_grads[2], bias_grads[3] = bias_pair[:units], bias_pair[units:]
+    up_far_halves = grad_halves(at, [(second_low, [pre_pair])], 1)
+    up_far = at.scatter_first(*up_far_halves, 1)
+    out_pair = at.deliver_first(out_share)
+    kept_late = after(kept, out_share, *up_far_halves)
+    pre_own, bias_grads[0], term = back_through(0, kept_late)
+    back = back + term
+    pre_one, bias_grads[1], term = back_through(1, kept_late)
+    back = back + term
+    up_near_halves = grad_halves(at, [(second_low, [pre_own, pre_one])], 1)
+    back_low = after(back.astype(bf16), *up_near_halves)
+    second_grad = at.sum_team(back_low)
+    second_grad = after(second_grad, *down_far)
+    down_far = at.scatter_rest(down_far, 0)
     lead = jnp.where((c == 0) & (at.t == 0), 1.0, 0.0)
     gain_two = jnp.sum(second_grad * second_normed, axis=0)
     shift_two = jnp.sum(second_grad, axis=0)
@@ -563,18 +952,69 @@
     branch = jnp.where(row_keep, middle_grad, 0.0).astype(bf16)
     mix_bias_grad = jnp.sum(branch.astype(f32), axis=0)
     back = None
-    attn_grads, rel_grads = [], []
-    for r in range(blocks):
-        context_grad = dot_nn(branch, out_w[r]).astype(bf16)
+    rel_grads = [None] * blocks
+    context_grads = [dot_nn(branch, out_w[r]).astype(bf16) for r in range(blocks)]
+    own_cols = slice(0, units)
+    far_cols = slice(units, 2 * units)
+    attn_sums = [None] * blocks
+    attn_halves = [None] * blocks
+    for r in reversed(range(blocks)):
+        context_grad = context_grads[r]
+        if r == 3:
+            context_grad = after(context_grad, *up_far, out_pair)
+            up_far = at.scatter_rest([after(v, out_pair) for v in up_far], 1)
+            out_pair = after(out_pair, *up_far_halves)
+            block_out = at.deliver_second(out_pair)
+        if r == 2:
+            context_grad = after(context_grad, down_far, up_far, block_out)
+            mlp_far = jnp.concatenate(
+                [
+                    down_far[:, own_cols],
+                    up_far[:, own_cols],
+                    down_far[:, far_cols],
+                    up_far[:, far_cols],
+                ],
+                axis=1,
+            ).astype(bf16)
+            mlp_far = at.fold_outer(after(mlp_far, block_out))
+            down_near_halves = [after(v, up_far, block_out) for v in down_near_halves]
+            up_near_halves = [after(v, down_far, block_out) for v in up_near_halves]
+            down_near_sum = at.scatter_first(*down_near_halves, 0)
+            up_near_sum = at.scatter_first(*up_near_halves, 1)
+        if r == 0:
+            context_grad = after(context_grad, *down_near_sum, *up_near_sum, mlp_far)
+            mlp_one, mlp_own = at.fold_inner(after(mlp_far, *up_near_sum))
+            for k in (3, 2):
+                held = [after(v, *down_near_sum, *up_near_sum) for v in attn_halves[k]]
+                attn_sums[k] = at.scatter_first(*held, k % 2)
+            down_near_sum = at.scatter_rest(down_near_sum, 0)
+            up_near_sum = at.scatter_rest(up_near_sum, 1)
         proj_grad, dist = attend_back(
             length, qkv[r], lines[r * heads : (r + 1) * heads], totals[r], context_grad, heads
         )
-        rel_grads.append(dist)
-        qkv_grad = dot_tn(first_low, proj_grad).astype(bf16)
-        out_grad = dot_tn(branch, contexts[r]).astype(bf16)
-        attn_grads.append((qkv_grad, out_grad))
+        rel_grads[r] = dist
+        attn_halves[r] = grad_halves(
+            at, [(first_low, [proj_grad]), (branch, [contexts[r]])], r % 2
+        )
         term = dot_nt(proj_grad, qkv_w[r])
         back = term if back is None else back + term
+    there = (*attn_sums[3], *attn_sums[2], down_near_sum, up_near_sum)
+    for k in (1, 0):
+        held = [after(v, *there) for v in attn_halves[k]]
+        attn_sums[k] = at.scatter_first(*held, k % 2)
+    for k in (3, 2, 1, 0):
+        attn_sums[k] = at.scatter_rest(attn_sums[k], k % 2)
+    mlp_one = mlp_one + jnp.concatenate(
+        [down_near_sum[:, far_cols], up_near_sum[:, far_cols]], axis=1
+    )
+    mlp_own = mlp_own + jnp.concatenate(
+        [down_near_sum[:, own_cols], up_near_sum[:, own_cols]], axis=1
+    )
+    mlp_mine = mlp_own + at.to_slot(mlp_one.astype(bf16), 1).astype(f32)
+    attn_far = jnp.concatenate([attn_sums[2], attn_sums[3]], axis=1).astype(bf16)
+    attn_one_sum, attn_own_sum = at.fold_inner(at.fold_outer(attn_far))
+    attn_one_sum = (attn_one_sum + attn_sums[1]).astype(bf16)
+    attn_mine = attn_own_sum + attn_sums[0] + at.to_slot(attn_one_sum, 1).astype(f32)
     rel_grad = lax.dot_general(
         jnp.concatenate(rel_grads, axis=0),
         choose,
@@ -590,11 +1030,20 @@
     input_share = middle_grad_share + norm_back(
         first_grad, normed_share, inverse_share, vectors[0]
     )
-    input_share = input_share.astype(bf16)
-    input_grad = at.deliver(
-        [input_share[i * length_rows : (i + 1) * length_rows] for i in range(per)]
-    )
-    input_grad = at.relative(input_grad, 2).astype(f32)
+    input_pair = at.deliver_first(input_share.astype(bf16))
+    input_grad = at.relative(at.deliver_second(input_pair), 2).astype(f32)
+
+    def by_place(rows_of):
+        around = jnp.stack(rows_of)
+        moved = []
+        for place in range(blocks):
+            picked = around[0]
+            for k in range(1, blocks):
+                picked = jnp.where(at.s ^ k == place, around[k], picked)
+            moved.append(picked)
+        moved = jnp.stack(moved)[:, None, None, :]
+        here = (jnp.arange(at.t_n)[:, None] == at.t) & (jnp.arange(2)[None, :] == c)
+        return jnp.where(here[None, :, :, None], moved, 0.0).reshape(at.mp_n, 2, -1)
 
     vector_grad = jnp.concatenate(
         [
@@ -602,93 +1051,122 @@
             lead * jnp.stack([gain_two, shift_two, mix_bias_grad, fed_bias_grad]),
         ]
     )
-    vector_grad = at.sum_all(at.relative(vector_grad, 1))
-
-    def own_sum(pieces):
-        total = pieces[0]
-        for step in range(1, blocks):
-            total = total + at.to_slot(pieces[step], blocks - step).astype(f32)
-        return total
-
-    def both_halves(mine, other, dim):
-        return jnp.where(
-            c == 0,
-            jnp.concatenate([mine, other], axis=dim),
-            jnp.concatenate([other, mine], axis=dim),
-        )
-
-    def scattered(parts, first_bit):
-        low = []
-        for step in range(blocks):
-            piece = at.scatter_chips(parts[step], (first_bit + step) % 2)
-            low.append(piece if step == 0 else piece.astype(bf16))
-        mine = own_sum(low)
-        rows = part // 2
+    small_grad = by_place(
+        [
+            jnp.concatenate([bias_grads[r], rel_grad[r * heads : (r + 1) * heads].reshape(-1)])
+            for r in range(blocks)
+        ]
+    )
+    joined = at.sum_all(
+        jnp.concatenate([at.relative(vector_grad, 1).reshape(-1), small_grad.reshape(-1)])
+    )
+    vector_grad = joined[: vector_grad.size].reshape(vector_grad.shape)
+    small_sum = lax.dynamic_index_in_dim(
+        joined[vector_grad.size :].reshape(small_grad.shape), at.mp_i, 0, keepdims=False
+    )
+    bias_sum = small_sum[:, :units].reshape(-1)
+    rel_sum = small_sum[:, units:].reshape(2 * heads, bucket_count).T
+
+    rows = part // 2
+
+    def exchanged(mine):
         sent = lax.dynamic_slice_in_dim(mine, (1 - c) * rows, rows, 0)
         return lax.dynamic_slice_in_dim(mine, c * rows, rows, 0), at.to_core(sent)
 
-    up_sum = both_halves(*scattered([pair[0] for pair in mlp_grads], 0), 1)
-    down_sum = both_halves(*scattered([pair[1] for pair in mlp_grads], 1), 1).T
-    rows = part // 2
-    mine, other = scattered([pair[0] for pair in attn_grads], 0)
-    qkv_sum = both_halves(
-        mine.reshape(rows, 3, head_width), other.reshape(rows, 3, head_width), 2
-    )
-    out_sum = both_halves(*scattered([pair[1] for pair in attn_grads], 1), 1).T
-    small_grads = [
-        jnp.concatenate(
-            [bias_grads[r], rel_grad[r * heads : (r + 1) * heads].reshape(-1)]
-        )
-        for r in range(blocks)
-    ]
-    small_mine = at.sum_all(own_sum(small_grads), chips_only=True)
-    small_other = at.to_core(small_mine)
-    bias_sum = both_halves(small_mine[:units], small_other[:units], 0)
-    rel_sum = both_halves(
-        small_mine[units:].reshape(heads, bucket_count),
-        small_other[units:].reshape(heads, bucket_count),
-        0,
-    ).T
-
-    def own_part(values, dim):
-        count = values.shape[dim] // at.dp_n
-        return lax.dynamic_slice_in_dim(values, at.dp_i * count, count, dim)
+    mlp_mine, mlp_other = exchanged(mlp_mine)
+    attn_mine, attn_other = exchanged(attn_mine)
 
     steps_done = step_count[0].astype(f32)
     first_fix = 1.0 - jnp.power(jnp.float32(0.9), steps_done)
     second_fix = 1.0 - jnp.power(jnp.float32(0.999), steps_done)
-    pieces = [
-        (own_part(qkv_weight, 0), qkv_moments, qkv_sum, weight_decay),
-        (own_part(out_weight, 1), out_moments, out_sum, weight_decay),
-        (own_part(up_weight, 0), up_moments, up_sum, weight_decay),
-        (own_part(down_weight, 1), down_moments, down_sum, weight_decay),
-        (up_bias, bias_moments, bias_sum, 0.0),
-        (rel_bias, rel_moments, rel_sum, 0.0),
-        (norm_vectors, vector_moments, vector_grad, 0.0),
+    vector_pieces = [
+        (up_bias, bias_moments, bias_sum),
+        (rel_bias, rel_moments, rel_sum),
+        (norm_vectors, vector_moments, vector_grad),
     ]
-    adjusted = [
-        adjust(weight, moments[0], moments[1], grad, decay, first_fix, second_fix)
-        for weight, moments, grad, decay in pieces
+    vector_adjusted = [
+        adjust(weight, moments[0], moments[1], grad, 0.0, first_fix, second_fix)
+        for weight, moments, grad in vector_pieces
     ]
+    qkv_view = jnp.transpose(qkv_weight, (1, 0, 2))
+    qkv_mom = jnp.transpose(qkv_moments, (0, 2, 1, 3))
+    weights = [qkv_view, out_weight, up_weight, down_weight]
+    dims = [1, 1, 0, 1]
+    in_kernels = rows % 128 == 0
+    if in_kernels:
+        place = jnp.stack([at.dp_i, c]).astype(jnp.int32)
+        fixes = jnp.stack([first_fix, second_fix])
+        up_state, down_state, up_update, down_update, mlp_squares = adjust_pair(
+            at, adjust_mlp_kernel, place, fixes, mlp_mine, mlp_other,
+            weights[2:], dims[2:], [up_moments, down_moments],
+        )
+        qkv_state, out_state, qkv_update, out_update, attn_squares = adjust_pair(
+            at, adjust_attn_kernel, place, fixes, attn_mine, attn_other,
+            weights[:2], dims[:2], [qkv_mom, out_moments],
+        )
+        squares = jnp.concatenate([attn_squares, mlp_squares])
+        updates = [qkv_update, out_update, up_update, down_update]
+        states = [qkv_state, out_state, up_state, down_state]
+    else:
+        one, two = in_order(c, attn_mine, attn_other)
+        parts = [
+            jnp.concatenate(
+                [v[:, j * head_width : (j + 1) * head_width] for v in (one, two)], axis=1
+            )
+            for j in range(4)
+        ]
+        one, two = in_order(c, mlp_mine, mlp_other)
+        grads = [
+            jnp.stack(parts[:3]),
+            parts[3].T,
+            jnp.concatenate([one[:, units:], two[:, units:]], axis=1),
+            jnp.concatenate([one[:, :units], two[:, :units]], axis=1).T,
+        ]
+        own_weights, updates, states, squares = [], [], [], []
+        for weight, dim, moments, grad in zip(
+            weights, dims, [qkv_mom, out_moments, up_moments, down_moments], grads
+        ):
+            count = weight.shape[dim] // at.dp_n
+            weight = lax.dynamic_slice_in_dim(weight, at.dp_i * count, count, dim)
+            first_new, second_new, update = adjust(
+                weight, moments[0], moments[1], grad, weight_decay, first_fix, second_fix
+            )
+            own_weights.append(weight)
+            updates.append(update)
+            states.append(jnp.stack([first_new, second_new]))
+            squares += [jnp.sum(weight * weight), jnp.sum(update * update)]
+        squares = jnp.stack(squares)
     lead_dp = (at.dp_i == 0).astype(f32)
-    share = [1.0, 1.0, 1.0, 1.0, lead_dp, lead_dp]
-    squares = jnp.stack(
-        [share[i] * jnp.sum(pieces[i][0] * pieces[i][0]) for i in range(6)]
-        + [share[i] * jnp.sum(adjusted[i][2] * adjusted[i][2]) for i in range(6)]
-    )
-    squares = at.sum_all(squares)
-    vector_sq = jnp.sum(norm_vectors * norm_vectors, axis=1)
-    vector_up_sq = jnp.sum(adjusted[6][2] * adjusted[6][2], axis=1)
-    weight_norm = jnp.sqrt(jnp.concatenate([squares[:6], vector_sq]))
-    update_norm = jnp.sqrt(jnp.concatenate([squares[6:], vector_up_sq]))
-    trust_ratio = weight_norm / (update_norm + adam_eps)
-    results = [block_out, input_grad]
-    for index in range(6):
-        results.append(pieces[index][0] - learn_rate * trust_ratio[index] * adjusted[index][2])
-        results.append(jnp.stack([adjusted[index][0], adjusted[index][1]]))
-    results.append(norm_vectors - learn_rate * trust_ratio[6:][:, None] * adjusted[6][2])
-    results.append(jnp.stack([adjusted[6][0], adjusted[6][1]]))
-    results.append(jnp.stack([weight_norm, update_norm]))
+    small_squares = jnp.stack(
+        [
+            lead_dp * jnp.sum(values * values)
+            for values in (up_bias, vector_adjusted[0][2], rel_bias, vector_adjusted[1][2])
+        ]
+    )
+    squares = at.sum_all(jnp.concatenate([squares, small_squares])).reshape(6, 2)
+    vector_squares = jnp.stack(
+        [jnp.sum(v * v, axis=1) for v in (norm_vectors, vector_adjusted[2][2])], axis=1
+    )
+    norms = jnp.sqrt(jnp.concatenate([squares, vector_squares]))
+    rates = learn_rate * (norms[:, 0] / (norms[:, 1] + adam_eps))
+    if in_kernels:
+        new = apply_updates(at, place, rates[:4], weights, dims, updates)
+    else:
+        new = [own_weights[k] - rates[k] * updates[k] for k in range(4)]
+    new, states = list(new), list(states)
+    new[0] = jnp.transpose(new[0], (1, 0, 2))
+    states[0] = jnp.transpose(states[0], (0, 2, 1, 3))
+    results = [at.relative(block_out, 2), input_grad]
+    for k in range(4):
+        results += [new[k], states[k]]
+    for k in range(2):
+        first_new, second_new, update = vector_adjusted[k]
+        results.append(vector_pieces[k][0] - rates[4 + k] * update)
+        results.append(jnp.stack([first_new, second_new]))
+    first_new, second_new, update = vector_adjusted[2]
+    results.append(norm_vectors - rates[6:, None] * update)
+    results.append(jnp.stack([first_new, second_new]))
+    results.append(norms.T)
     return tuple(results)
 
 

time: 720 us -> 534 us (0.74)
  starting transfers between devices: 228 us -> 134 us
  waiting for transfers between devices: 159 us -> 88.5 us
  Pallas kernels: 49 us -> 85.2 us
  matrix products: 90.8 us -> 65.9 us
  local copies, waits for them, and re-layouts: 88.9 us -> 67.6 us
    ppermute x149 -> x82, starting transfers between devices: 228 us -> 134 us  [move(): return lax.ppermute(values, ('dp', 'mp'), pairs)]
    ppermute x149 -> x82, waiting for transfers between devices: 159 us -> 88.5 us  [move(): return lax.ppermute(values, ('dp', 'mp'), pairs)]
    pallas_call x0 -> x13, Pallas kernels: none -> 35.8 us  [the longest x8 17.8 us: grad_halves(): pl.pallas_call(lambda *refs: halves_kernel(order, [len(rights) for _, rig...]
    dot_general x16 -> x0, matrix products: 23.3 us -> none  [dot_tn(): lax.dot_general(left, right, (((0,), (0,)), ((), ())), preferred_element_...]
    unnamed x385 -> x355, local copies, waits for them, and re-layouts: 33.2 us -> 22.9 us
    slice x31 -> x53, local copies, waits for them, and re-layouts: 19.5 us -> 29.7 us  [the longest x5 4.04 us: local(): qkv_w.append(jnp.concatenate([v[:, :qkv_cols] for v in pieces], axis=0))]
    add x6 -> x15, other arithmetic: 1.5 us -> 9.68 us  [the longest x4 3.66 us: scatter_rest(): total = total + self.to_chip(sent, bit).astype(f32)]
    convert_element_type x30 -> x15, other arithmetic: 13.7 us -> 19.7 us  [the longest x8 8.52 us: scatter_first(): sent_on = (kept[half:].astype(f32) + got[half:].astype(f32)).astype(bf16)]
  transfers between devices with their start and end apart: 149 -> 82, of which waited for: 53 -> 19; matrix products, arithmetic and copies ran while one was open for 24% -> 35% of each run, Pallas kernels for 2% -> 15%
where the time goes in v1:
time: 534 us; the launch traced here: 524 us
  starting transfers between devices  134 us (25%)
  waiting for transfers between devices  88.5 us (17%)
  Pallas kernels  85.2 us (16%)
  other arithmetic  75.3 us (14%)
  local copies, waits for them, and re-layouts  67.6 us (13%)
  matrix products  65.9 us (12%)
  between operations  7.71 us (1%)
    ppermute x82, starting transfers between devices, move(): return lax.ppermute(values, ('dp', 'mp'), pairs)  134 us
    ppermute x82, waiting for transfers between devices, move(): return lax.ppermute(values, ('dp', 'mp'), pairs)  88.5 us
    dot_general x14, matrix products, dot_nt(): lax.dot_general(left, right, (((1,), (1,)), ((), ())), preferred_element_...  34.1 us
    pallas_call x4, Pallas kernels, attend_back(): pl.pallas_call(lambda *refs: attend_back_kernel(heads, *refs), out_shape=...  33.1 us
    dot_general x14, matrix products, dot_nn(): lax.dot_general(left, right, (((1,), (0,)), ((), ())), preferred_element_...  31.3 us
    unnamed x355, local copies, waits for them, and re-layouts  22.9 us
    pallas_call x8, Pallas kernels, grad_halves(): pl.pallas_call(lambda *refs: halves_kernel(order, [len(rights) for _, rig...  17.8 us
    pallas_call x4, Pallas kernels, attend(): pl.pallas_call(lambda *refs: attend_kernel(heads, *refs), out_shape=(jax....  16.3 us
  transfers between devices with their start and end apart: 82, of which 19 were waited for; matrix products, arithmetic and copies ran while one was open for 35% of the time, Pallas kernels for 15%

profile of v1, /device:TPU:1, one launch (start us, length us, event | category | flops | bytes accessed | tf_op | source)
XLA Modules:
  0.0 523.7 jit_solution(18078487671073036318)
XLA Ops:
  4.9 8.2 %collective-permute-start.1 = (bf16[256,1024]{1,0:T(8,128)(2,1)}, bf16[256,1024]{1,0:T(8,128)(2,1)}, u32[]{:S(2)}, u32[]{:S(2)}) collective-permute-start(bf16[256,1024]{1,0:T(8,128)(2,1)} %get-tuple-element.357), channel_id=1, source_target_pairs={{2,0},{3,1},{4,6},{5,7},{10,8},{11,9},{12,14},{13,15},{18,16},{19,... | collective-permute-start | bytes 1572872 | tf_op jit(solution)/shard_map/ppermute | solution.py:233
  13.7 4.6 pack_attn.1
  23.9 5.4 %pack_mlp.1 = (bf16[1024,512]{1,0:T(8,128)(2,1)}, bf16[1024,512]{1,0:T(8,128)(2,1)}, bf16[256,512]{1,0:T(8,128)(2,1)}, bf16[256,512]{1,0:T(8,128)(2,1)}) custom-call(s32[2]{0:T(128)} %pad_add_fusion.1.place_ref, f32[1024,1024]{1,0:T(8,128)} %refs_2_.1, f32[1024,1024]{1,0:T(8,128)} %refs_3_.1), custom_call_target="tpu_custom_call" | custom-call | tf_op jit(solution)/shard_map/pack_mlp/pallas_call | solution.py:494
  47.5 9.1 %collective-permute-done.10 = bf16[256,1024]{1,0:T(8,128)(2,1)} collective-permute-done((bf16[256,1024]{1,0:T(8,128)(2,1)}, bf16[256,1024]{1,0:T(8,128)(2,1)}, u32[]{:S(2)}, u32[]{:S(2)}) %collective-permute-start.10) | collective-permute-done | bytes 524320 | tf_op jit(solution)/shard_map/ppermute | solution.py:233
  77.1 6.5 %collective-permute-done.11 = bf16[272,1024]{1,0:T(8,128)(2,1)S(1)} collective-permute-done((bf16[272,1024]{1,0:T(8,128)(2,1)}, bf16[272,1024]{1,0:T(8,128)(2,1)S(1)}, u32[]{:S(2)}, u32[]{:S(2)}) %collective-permute-start.11) | collective-permute-done | bytes 557088 | tf_op jit(solution)/shard_map/ppermute | solution.py:233
  90.5 4.4 collective-permute-done.17
  140.2 9.3 %collective-permute-start.24 = (bf16[1024,1024]{1,0:T(8,128)(2,1)S(1)}, bf16[1024,1024]{1,0:T(8,128)(2,1)S(1)}, u32[]{:S(2)}, u32[]{:S(2)}) collective-permute-start(bf16[1024,1024]{1,0:T(8,128)(2,1)S(1)} %select_convert_fusion.1), channel_id=1, source_target_pairs={{0,4},{1,5},{2,6},{3,7},{4,0},{5,1},{6,2},{7,3},{8,12},{9,13},{10,... | collective-permute-start | bytes 6291464 | tf_op jit(solution)/shard_map/ppermute | solution.py:233
  157.9 7.9 %collective-permute-done.25 = bf16[256,1024]{1,0:T(8,128)(2,1)S(1)} collective-permute-done((bf16[256,1024]{1,0:T(8,128)(2,1)S(1)}, bf16[256,1024]{1,0:T(8,128)(2,1)S(1)}, u32[]{:S(2)}, u32[]{:S(2)}) %collective-permute-start.25) | collective-permute-done | bytes 524320 | tf_op jit(solution)/shard_map/ppermute | solution.py:233
  176.0 12.6 %collective-permute-done.27 = bf16[256,512]{1,0:T(8,128)(2,1)S(1)} collective-permute-done((bf16[256,512]{1,0:T(8,128)(2,1)S(1)}, bf16[256,512]{1,0:T(8,128)(2,1)S(1)}, u32[]{:S(2)}, u32[]{:S(2)}) %collective-permute-start.27) | collective-permute-done | bytes 262176 | tf_op jit(solution)/shard_map/ppermute | solution.py:233
  205.4 4.3 multiply_convert_fusion
  213.0 9.0 %add_convert_fusion.2 = bf16[1024,1024]{1,0:T(8,128)(2,1)S(1)} fusion(f32[1024,1024]{1,0:T(8,128)} %fusion.151, f32[1024,1024]{1,0:T(8,128)} %fusion.42, bf16[1024,1024]{1,0:T(8,128)(2,1)S(1)} %get-tuple-element.476.refs_1_, bf16[256,512]{1,0:T(8,128)(2,1)S(1)} %collective-permute-done.32, bf16[256,512]{1,0:T(8,128)(2,1)S(1)} %collective-permute-done.31, ...), kind=kOutput, calls=%fused_computation.23 | convolution fusion | flops 2161115136 | bytes 14680064 | tf_op jit(solution)/shard_map/dot_general | solution.py:26
  229.8 9.7 %convert_reduce_fusion.1 = (f32[1024]{0:T(1024)S(1)}, bf16[1024,1024]{1,0:T(8,128)(2,1)S(1)}) fusion(f32[1024,1024]{1,0:T(8,128)} %get-tuple-element.477, f32[1024]{0:T(1024)S(1)} %pad_maximum_fusion.60, bf16[1024,1024]{1,0:T(8,128)(2,1)S(1)} %get-tuple-element.163.refs_0_, bf16[256,512]{1,0:T(8,128)(2,1)S(1)} %collective-permute-done.32, ...), kind=kOutput, calls=%fused_computation.13 | convolution fusion | flops 2171599872 | bytes 10493952 | tf_op jit(solution)/shard_map/dot_general | solution.py:30
  264.3 10.2 %collective-permute-done.38 = bf16[512,1024]{1,0:T(8,128)(2,1)S(1)} collective-permute-done((bf16[512,1024]{1,0:T(8,128)(2,1)S(1)}, bf16[512,1024]{1,0:T(8,128)(2,1)S(1)}, u32[]{:S(2)}, u32[]{:S(2)}) %collective-permute-start.38) | collective-permute-done | bytes 1048608 | tf_op jit(solution)/shard_map/ppermute | solution.py:233
  279.6 6.4 %collective-permute-done.39 = bf16[256,1024]{1,0:T(8,128)(2,1)S(1)} collective-permute-done((bf16[256,1024]{1,0:T(8,128)(2,1)S(1)}, bf16[256,1024]{1,0:T(8,128)(2,1)S(1)}, u32[]{:S(2)}, u32[]{:S(2)}) %collective-permute-start.39) | collective-permute-done | bytes 524320 | tf_op jit(solution)/shard_map/ppermute | solution.py:233
  286.0 4.5 collective-permute-done.44
  306.0 8.2 %attend_back.4 = (bf16[1024,384]{1,0:T(8,128)(2,1)S(1)}, f32[2,2048]{1,0:T(2,128)S(1)}) custom-call(s32[1]{0:T(128)} %dynamic_slice.186.refs_0_, bf16[1024,384]{1,0:T(8,128)(2,1)S(1)} %convolution_convert_fusion.refs_1_, f32[2,2048]{1,0:T(2,128)S(1)} %get-tuple-element.416.refs_2_, f32[2,1024]{1,0:T(2,128)S(1)} %get-tuple-element.170.refs_3_, ...), custom_call_target="tpu_custom_call" | custom-call | flops 8589934592 | bytes 4194304 | tf_op jit(solution)/shard_map/attend_back/pallas_call | solution.py:165
  315.5 8.3 %attend_back.5 = (bf16[1024,384]{1,0:T(8,128)(2,1)S(1)}, f32[2,2048]{1,0:T(2,128)S(1)}) custom-call(s32[1]{0:T(128)} %dynamic_slice.186.refs_0_, bf16[1024,384]{1,0:T(8,128)(2,1)S(1)} %convolution_convert_fusion.1.refs_1_, f32[2,2048]{1,0:T(2,128)S(1)} %get-tuple-element.417.refs_2_, f32[2,1024]{1,0:T(2,128)S(1)} %get-tuple-element.173.refs_3_, ...), custom_call_target="tpu_custom_call" | custom-call | flops 8589934592 | bytes 4194304 | tf_op jit(solution)/shard_map/attend_back/pallas_call | solution.py:165
  323.8 8.3 %attend_back.6 = (bf16[1024,384]{1,0:T(8,128)(2,1)S(1)}, f32[2,2048]{1,0:T(2,128)S(1)}) custom-call(s32[1]{0:T(128)} %dynamic_slice.186.refs_0_, bf16[1024,384]{1,0:T(8,128)(2,1)S(1)} %convolution_convert_fusion.2.refs_1_, f32[2,2048]{1,0:T(2,128)S(1)} %get-tuple-element.418.refs_2_, f32[2,1024]{1,0:T(2,128)S(1)} %get-tuple-element.178.refs_3_, ...), custom_call_target="tpu_custom_call" | custom-call | flops 8589934592 | bytes 4194304 | tf_op jit(solution)/shard_map/attend_back/pallas_call | solution.py:165
  350.5 8.3 %attend_back.7 = (bf16[1024,384]{1,0:T(8,128)(2,1)S(1)}, f32[2,2048]{1,0:T(2,128)S(1)}) custom-call(s32[1]{0:T(128)} %dynamic_slice.186.refs_0_, bf16[1024,384]{1,0:T(8,128)(2,1)S(1)} %copy-done.44, f32[2,2048]{1,0:T(2,128)S(1)} %copy-done.36, f32[2,1024]{1,0:T(2,128)S(1)} %get-tuple-element.180.refs_3_, bf16[1024,128]{1,0:T(8,128)(2,1)S(1)} %convolution_convert_fusion.4.refs_4_), custom_call_target="tpu_custom_call" | custom-call | flops 8589934592 | bytes 4194304 | tf_op jit(solution)/shard_map/attend_back/pallas_call | solution.py:165
  376.1 5.9 %collective-permute-done.53 = bf16[512,512]{1,0:T(8,128)(2,1)} collective-permute-done((bf16[512,512]{1,0:T(8,128)(2,1)}, bf16[512,512]{1,0:T(8,128)(2,1)}, u32[]{:S(2)}, u32[]{:S(2)}) %collective-permute-start.53) | collective-permute-done | bytes 524320 | tf_op jit(solution)/shard_map/ppermute | solution.py:233
  417.2 6.3 %collective-permute-start.49 = (bf16[512,1024]{1,0:T(8,128)(2,1)}, bf16[512,1024]{1,0:T(8,128)(2,1)}, u32[]{:S(2)}, u32[]{:S(2)}) collective-permute-start(bf16[512,1024]{1,0:T(8,128)(2,1)} %fusion.22), channel_id=1, source_target_pairs={{2,4},{3,5},{4,2},{5,3},{10,12},{11,13},{12,10},{13,11},{18,20},{1... | collective-permute-start | bytes 3145736 | tf_op jit(solution)/shard_map/ppermute | solution.py:233
  428.0 10.2 %collective-permute-done.73 = f32[10752]{0:T(1024)S(1)} collective-permute-done((f32[10752]{0:T(1024)S(1)}, f32[10752]{0:T(1024)S(1)}, u32[]{:S(2)}, u32[]{:S(2)}) %collective-permute-start.73) | collective-permute-done | bytes 43040 | tf_op jit(solution)/shard_map/ppermute | solution.py:233
  438.3 10.0 %collective-permute-start.66 = (bf16[256,1024]{1,0:T(8,128)(2,1)}, bf16[256,1024]{1,0:T(8,128)(2,1)}, u32[]{:S(2)}, u32[]{:S(2)}) collective-permute-start(bf16[256,1024]{1,0:T(8,128)(2,1)} %fusion.26), channel_id=1, source_target_pairs={{0,1},{1,0},{2,3},{3,2},{4,5},{5,4},{6,7},{7,6},{8,9},{9,8},{10,11... | collective-permute-start | bytes 1572872 | tf_op jit(solution)/shard_map/ppermute | solution.py:233
  466.1 6.4 %collective-permute-start.63 = (bf16[256,512]{1,0:T(8,128)(2,1)S(1)}, bf16[256,512]{1,0:T(8,128)(2,1)S(1)}, u32[]{:S(2)}, u32[]{:S(2)}) collective-permute-start(bf16[256,512]{1,0:T(8,128)(2,1)S(1)} %fusion.28), channel_id=1, source_target_pairs={{0,1},{1,0},{2,3},{3,2},{4,5},{5,4},{6,7},{7,6},{8,9},{9,8},{10,11... | collective-permute-start | bytes 786440 | tf_op jit(solution)/shard_map/ppermute | solution.py:233
  (773 shorter events, 332.4 us)
Async XLA Ops:
  0.7 33.3 %collective-permute-start.9 = (s32[2]{0:T(128)}, s32[2]{0:T(128)S(1)}, u32[]{:S(2)}, u32[]{:S(2)}) collective-permute-start(s32[2]{0:T(128)} %param.21), channel_id=1, source_target_pairs={{0,4},{1,5},{2,6},{3,7},{4,0},{5,1},{6,2},{7,3},{8,12},{9,13},{10,... | collective-permute-start | bytes 32 | tf_op jit(solution)/shard_map/ppermute | solution.py:233
  3.4 33.2 %collective-permute-start = (bf16[256,1024]{1,0:T(8,128)(2,1)}, bf16[256,1024]{1,0:T(8,128)(2,1)}, u32[]{:S(2)}, u32[]{:S(2)}) collective-permute-start(bf16[256,1024]{1,0:T(8,128)(2,1)} %get-tuple-element.358), channel_id=1, source_target_pairs={{0,1},{1,0},{6,7},{7,6},{8,9},{9,8},{14,15},{15,14},{16,17},{17,16... | collective-permute-start | bytes 1572872 | tf_op jit(solution)/shard_map/ppermute | solution.py:233
  4.9 34.9 %collective-permute-start.1 = (bf16[256,1024]{1,0:T(8,128)(2,1)}, bf16[256,1024]{1,0:T(8,128)(2,1)}, u32[]{:S(2)}, u32[]{:S(2)}) collective-permute-start(bf16[256,1024]{1,0:T(8,128)(2,1)} %get-tuple-element.357), channel_id=1, source_target_pairs={{2,0},{3,1},{4,6},{5,7},{10,8},{11,9},{12,14},{13,15},{18,16},{19,... | collective-permute-start | bytes 1572872 | tf_op jit(solution)/shard_map/ppermute | solution.py:233
  66.0 42.2 %collective-permute-start.4 = (bf16[1024,1024]{1,0:T(8,128)(2,1)S(1)}, bf16[1024,1024]{1,0:T(8,128)(2,1)}, u32[]{:S(2)}, u32[]{:S(2)}) collective-permute-start(bf16[1024,1024]{1,0:T(8,128)(2,1)S(1)} %constant_dynamic-update-slice_fusion.3), channel_id=1, source_target_pairs={{0,4},{1,5},{6,2},{7,3},{8,12},{9,13},{14,10},{15,11},{16,20},{17,... | collective-permute-start | bytes 6291464 | tf_op jit(solution)/shard_map/ppermute | solution.py:233
  102.6 32.4 %collective-permute-start.23 = (bf16[256,1024]{1,0:T(8,128)(2,1)}, bf16[256,1024]{1,0:T(8,128)(2,1)S(1)}, u32[]{:S(2)}, u32[]{:S(2)}) collective-permute-start(bf16[256,1024]{1,0:T(8,128)(2,1)} %collective-permute-done.18), channel_id=1, source_target_pairs={{1,0},{2,3},{5,4},{6,7},{9,8},{10,11},{13,12},{14,15},{17,16},{18,... | collective-permute-start | bytes 1572872 | tf_op jit(solution)/shard_map/ppermute | solution.py:233
  106.4 28.6 %collective-permute-start.21 = (bf16[256,512]{1,0:T(8,128)(2,1)S(1)}, bf16[256,512]{1,0:T(8,128)(2,1)S(1)}, u32[]{:S(2)}, u32[]{:S(2)}) collective-permute-start(bf16[256,512]{1,0:T(8,128)(2,1)S(1)} %get-tuple-element.390), channel_id=1, source_target_pairs={{0,16},{1,17},{2,18},{3,19},{4,20},{5,21},{6,22},{7,23},{8,24},{9,... | collective-permute-start | bytes 786440 | tf_op jit(solution)/shard_map/ppermute | solution.py:233
  140.2 52.9 %collective-permute-start.24 = (bf16[1024,1024]{1,0:T(8,128)(2,1)S(1)}, bf16[1024,1024]{1,0:T(8,128)(2,1)S(1)}, u32[]{:S(2)}, u32[]{:S(2)}) collective-permute-start(bf16[1024,1024]{1,0:T(8,128)(2,1)S(1)} %select_convert_fusion.1), channel_id=1, source_target_pairs={{0,4},{1,5},{2,6},{3,7},{4,0},{5,1},{6,2},{7,3},{8,12},{9,13},{10,... | collective-permute-start | bytes 6291464 | tf_op jit(solution)/shard_map/ppermute | solution.py:233
  188.6 33.5 %collective-permute-start.36 = (bf16[1024,1024]{1,0:T(8,128)(2,1)S(1)}, bf16[1024,1024]{1,0:T(8,128)(2,1)S(1)}, u32[]{:S(2)}, u32[]{:S(2)}) collective-permute-start(bf16[1024,1024]{1,0:T(8,128)(2,1)S(1)} %constant_dynamic-update-slice_fusion), channel_id=1, source_target_pairs={{0,4},{1,5},{6,2},{7,3},{8,12},{9,13},{14,10},{15,11},{16,20},{17,... | collective-permute-start | bytes 6291464 | tf_op jit(solution)/shard_map/ppermute | solution.py:233
  229.8 33.3 %collective-permute-start.41 = (bf16[512,1024]{1,0:T(8,128)(2,1)S(1)}, bf16[512,1024]{1,0:T(8,128)(2,1)S(1)}, u32[]{:S(2)}, u32[]{:S(2)}) collective-permute-start(bf16[512,1024]{1,0:T(8,128)(2,1)S(1)} %get-tuple-element.168), channel_id=1, source_target_pairs={{0,8},{1,9},{2,10},{3,11},{4,12},{5,13},{6,14},{7,15},{8,0},{9,1},... | collective-permute-start | bytes 3145736 | tf_op jit(solution)/shard_map/ppermute | solution.py:233
  242.0 32.7 %collective-permute-start.42 = (bf16[512,1024]{1,0:T(8,128)(2,1)S(1)}, bf16[512,1024]{1,0:T(8,128)(2,1)S(1)}, u32[]{:S(2)}, u32[]{:S(2)}) collective-permute-start(bf16[512,1024]{1,0:T(8,128)(2,1)S(1)} %get-tuple-element.161), channel_id=1, source_target_pairs={{0,16},{1,17},{2,18},{3,19},{4,20},{5,21},{6,22},{7,23},{8,24},{9,... | collective-permute-start | bytes 3145736 | tf_op jit(solution)/shard_map/ppermute | solution.py:233
  247.0 27.5 %collective-permute-start.38 = (bf16[512,1024]{1,0:T(8,128)(2,1)S(1)}, bf16[512,1024]{1,0:T(8,128)(2,1)S(1)}, u32[]{:S(2)}, u32[]{:S(2)}) collective-permute-start(bf16[512,1024]{1,0:T(8,128)(2,1)S(1)} %fusion.21), channel_id=1, source_target_pairs={{2,4},{3,5},{4,2},{5,3},{10,12},{11,13},{12,10},{13,11},{18,20},{1... | collective-permute-start | bytes 3145736 | tf_op jit(solution)/shard_map/ppermute | solution.py:233
  263.1 33.5 %collective-permute-start.40 = (bf16[1024,1024]{1,0:T(8,128)(2,1)S(1)}, bf16[1024,1024]{1,0:T(8,128)(2,1)S(1)}, u32[]{:S(2)}, u32[]{:S(2)}) collective-permute-start(bf16[1024,1024]{1,0:T(8,128)(2,1)S(1)} %add_convert_fusion.1), channel_id=1, source_target_pairs={{0,4},{1,5},{2,6},{3,7},{4,0},{5,1},{6,2},{7,3},{8,12},{9,13},{10,... | collective-permute-start | bytes 6291464 | tf_op jit(solution)/shard_map/ppermute | solution.py:233
  290.6 53.6 %collective-permute-start.45 = (bf16[512,1024]{1,0:T(8,128)(2,1)S(1)}, bf16[512,1024]{1,0:T(8,128)(2,1)S(1)}, u32[]{:S(2)}, u32[]{:S(2)}) collective-permute-start(bf16[512,1024]{1,0:T(8,128)(2,1)S(1)} %get-tuple-element.182), channel_id=1, source_target_pairs={{0,8},{1,9},{2,10},{3,11},{4,12},{5,13},{6,14},{7,15},{8,0},{9,1},... | collective-permute-start | bytes 3145736 | tf_op jit(solution)/shard_map/ppermute | solution.py:233
  292.0 54.5 %collective-permute-start.46 = (bf16[512,1024]{1,0:T(8,128)(2,1)S(1)}, bf16[512,1024]{1,0:T(8,128)(2,1)S(1)}, u32[]{:S(2)}, u32[]{:S(2)}) collective-permute-start(bf16[512,1024]{1,0:T(8,128)(2,1)S(1)} %get-tuple-element.184), channel_id=1, source_target_pairs={{0,16},{1,17},{2,18},{3,19},{4,20},{5,21},{6,22},{7,23},{8,24},{9,... | collective-permute-start | bytes 3145736 | tf_op jit(solution)/shard_map/ppermute | solution.py:233
  292.9 54.9 %collective-permute-start.47 = (bf16[256,2048]{1,0:T(8,128)(2,1)S(1)}, bf16[256,2048]{1,0:T(8,128)(2,1)}, u32[]{:S(2)}, u32[]{:S(2)}) collective-permute-start(bf16[256,2048]{1,0:T(8,128)(2,1)S(1)} %pad_maximum_fusion.9), channel_id=1, source_target_pairs={{0,1},{3,2},{4,5},{7,6},{8,9},{11,10},{12,13},{15,14},{16,17},{19,... | collective-permute-start | bytes 3145736 | tf_op jit(solution)/shard_map/ppermute | solution.py:233
  345.5 45.1 %collective-permute-start.57 = (bf16[256,1024]{1,0:T(8,128)(2,1)}, bf16[256,1024]{1,0:T(8,128)(2,1)}, u32[]{:S(2)}, u32[]{:S(2)}) collective-permute-start(bf16[256,1024]{1,0:T(8,128)(2,1)} %add_convert_fusion.7), channel_id=1, source_target_pairs={{0,16},{1,17},{2,18},{3,19},{4,20},{5,21},{6,22},{7,23},{8,24},{9,... | collective-permute-start | bytes 1572872 | tf_op jit(solution)/shard_map/ppermute | solution.py:233
  347.7 39.5 %collective-permute-start.58 = (bf16[256,1024]{1,0:T(8,128)(2,1)}, bf16[256,1024]{1,0:T(8,128)(2,1)}, u32[]{:S(2)}, u32[]{:S(2)}) collective-permute-start(bf16[256,1024]{1,0:T(8,128)(2,1)} %add_convert_fusion.6), channel_id=1, source_target_pairs={{0,8},{1,9},{2,10},{3,11},{4,12},{5,13},{6,14},{7,15},{8,0},{9,1},... | collective-permute-start | bytes 1572872 | tf_op jit(solution)/shard_map/ppermute | solution.py:233
  364.0 37.7 %collective-permute-start.48 = (bf16[512,1024]{1,0:T(8,128)(2,1)}, bf16[512,1024]{1,0:T(8,128)(2,1)}, u32[]{:S(2)}, u32[]{:S(2)}) collective-permute-start(bf16[512,1024]{1,0:T(8,128)(2,1)} %pad_maximum_fusion.11), channel_id=1, source_target_pairs={{0,4},{1,5},{2,6},{3,7},{4,0},{5,1},{6,2},{7,3},{8,12},{9,13},{10,... | collective-permute-start | bytes 3145736 | tf_op jit(solution)/shard_map/ppermute | solution.py:233
  394.1 29.8 %collective-permute-start.59 = (bf16[512,512]{1,0:T(8,128)(2,1)S(1)}, bf16[512,512]{1,0:T(8,128)(2,1)}, u32[]{:S(2)}, u32[]{:S(2)}) collective-permute-start(bf16[512,512]{1,0:T(8,128)(2,1)S(1)} %copy-done.40), channel_id=1, source_target_pairs={{0,8},{1,9},{2,10},{3,11},{4,12},{5,13},{6,14},{7,15},{8,0},{9,1},... | collective-permute-start | bytes 1572872 | tf_op jit(solution)/shard_map/ppermute | solution.py:233
  397.9 54.9 %collective-permute-start.55 = (bf16[256,1024]{1,0:T(8,128)(2,1)}, bf16[256,1024]{1,0:T(8,128)(2,1)}, u32[]{:S(2)}, u32[]{:S(2)}) collective-permute-start(bf16[256,1024]{1,0:T(8,128)(2,1)} %pad_maximum_fusion.18), channel_id=1, source_target_pairs={{0,1},{3,2},{4,5},{7,6},{8,9},{11,10},{12,13},{15,14},{16,17},{19,... | collective-permute-start | bytes 1572872 | tf_op jit(solution)/shard_map/ppermute | solution.py:233
  417.2 64.3 %collective-permute-start.49 = (bf16[512,1024]{1,0:T(8,128)(2,1)}, bf16[512,1024]{1,0:T(8,128)(2,1)}, u32[]{:S(2)}, u32[]{:S(2)}) collective-permute-start(bf16[512,1024]{1,0:T(8,128)(2,1)} %fusion.22), channel_id=1, source_target_pairs={{2,4},{3,5},{4,2},{5,3},{10,12},{11,13},{12,10},{13,11},{18,20},{1... | collective-permute-start | bytes 3145736 | tf_op jit(solution)/shard_map/ppermute | solution.py:233
  438.3 34.3 %collective-permute-start.66 = (bf16[256,1024]{1,0:T(8,128)(2,1)}, bf16[256,1024]{1,0:T(8,128)(2,1)}, u32[]{:S(2)}, u32[]{:S(2)}) collective-permute-start(bf16[256,1024]{1,0:T(8,128)(2,1)} %fusion.26), channel_id=1, source_target_pairs={{0,1},{1,0},{2,3},{3,2},{4,5},{5,4},{6,7},{7,6},{8,9},{9,8},{10,11... | collective-permute-start | bytes 1572872 | tf_op jit(solution)/shard_map/ppermute | solution.py:233
  449.7 27.8 %collective-permute-start.60 = (bf16[256,512]{1,0:T(8,128)(2,1)}, bf16[256,512]{1,0:T(8,128)(2,1)}, u32[]{:S(2)}, u32[]{:S(2)}) collective-permute-start(bf16[256,512]{1,0:T(8,128)(2,1)} %add_convert_fusion.11), channel_id=1, source_target_pairs={{0,16},{1,17},{2,18},{3,19},{4,20},{5,21},{6,22},{7,23},{8,24},{9,... | collective-permute-start | bytes 786440 | tf_op jit(solution)/shard_map/ppermute | solution.py:233
  483.8 36.9 %collective-permute-start.50 = (bf16[256,1024]{1,0:T(8,128)(2,1)}, bf16[256,1024]{1,0:T(8,128)(2,1)}, u32[]{:S(2)}, u32[]{:S(2)}) collective-permute-start(bf16[256,1024]{1,0:T(8,128)(2,1)} %slice.787), channel_id=1, source_target_pairs={{0,1},{1,0},{2,3},{3,2},{4,5},{5,4},{6,7},{7,6},{8,9},{9,8},{10,11... | collective-permute-start | bytes 1572872 | tf_op jit(solution)/shard_map/ppermute | solution.py:233
  (230 other events, 3115.7 us)

commit v2 on v1

--- a/solution.py
+++ b/solution.py
@@ -151,9 +151,9 @@
         out_specs=(in_vmem, in_vmem),
         compiler_params=pltpu.CompilerParams(vmem_limit_bytes=kernel_bytes),
         cost_estimate=pl.CostEstimate(
-            flops=heads * rows * rows * HD * 32,
-            bytes_accessed=4 << 20,
-            transcendentals=heads * rows * rows,
+            flops=heads * rows * rows * HD * 10,
+            bytes_accessed=1 << 20,
+            transcendentals=0,
         ),
         name="attend",
     )(length, qkv, line)
@@ -177,9 +177,9 @@
         ],
         compiler_params=pltpu.CompilerParams(vmem_limit_bytes=back_bytes),
         cost_estimate=pl.CostEstimate(
-            flops=heads * rows * rows * HD * 64,
-            bytes_accessed=4 << 20,
-            transcendentals=heads * rows * rows,
+            flops=heads * rows * rows * HD * 20,
+            bytes_accessed=1 << 20,
+            transcendentals=0,
         ),
         name="attend_back",
     )(length, qkv, line, lse, grad)
@@ -287,15 +287,18 @@
         return jnp.where(self.at_home, whole, other)
 
     def deliver_first(self, blocks):
-        got = self.move(
+        return self.move(
             blocks, lambda q, c, s, t: (q, 1 - c, s ^ 2, t) if c != s // 2 else None
         )
+
+    def deliver_pair(self, blocks, got):
         return jnp.where(self.at_home, blocks, got)
 
-    def deliver_second(self, pair):
-        count = pair.shape[0] // 2
-        got = self.to_slot(pair[count:], 1)
-        mine = pair[:count]
+    def deliver_last(self, pair):
+        return self.to_slot(pair[pair.shape[0] // 2 :], 1)
+
+    def delivered(self, pair, got):
+        mine = pair[: pair.shape[0] // 2]
         even = self.s % 2 == 0
         return jnp.stack([jnp.where(even, mine, got), jnp.where(even, got, mine)])
 
@@ -341,16 +344,15 @@
         return jnp.where((self.s == 1) | (self.s == 2), turned, outer)
 
     def fold_outer(self, far):
+        return self.move(far, lambda q, c, s, t: (q, c, s ^ 1, t) if s in (0, 3) else None)
+
+    def fold_add(self, far, got):
         size = far.shape[1] // 2
-        got = self.move(far, lambda q, c, s, t: (q, c, s ^ 1, t) if s in (0, 3) else None)
-        return far.astype(f32) + jnp.concatenate([got[:, size:], got[:, :size]], axis=1).astype(f32)
+        turned = jnp.concatenate([got[:, size:], got[:, :size]], axis=1)
+        return (far.astype(f32) + turned.astype(f32)).astype(bf16)
 
     def fold_inner(self, far):
-        size = far.shape[1] // 2
-        got = self.move(
-            far.astype(bf16), lambda q, c, s, t: (q, c, s ^ 3, t) if s in (1, 2) else None
-        ).astype(f32)
-        return got[:, :size], got[:, size:]
+        return self.move(far, lambda q, c, s, t: (q, c, s ^ 3, t) if s in (1, 2) else None)
 
     def bits_from(self, first):
         return self.q_bits[first:] + self.q_bits[:first]
@@ -378,27 +380,8 @@
             order = order + [k | bit for k in order]
         return order
 
-    def scatter_first(self, kept, sent, first):
-        got = self.to_chip(sent, self.bits_from(first)[0])
-        half = kept.shape[0] // 2
-        if len(self.q_bits) == 1:
-            return kept.astype(f32) + got.astype(f32), None
-        sent_on = (kept[half:].astype(f32) + got[half:].astype(f32)).astype(bf16)
-        return kept[:half].astype(f32) + got[:half].astype(f32), sent_on
-
-    def scatter_rest(self, halves, first):
-        total, sent = halves
-        bits = self.bits_from(first)[1:]
-        for number, bit in enumerate(bits):
-            total = total + self.to_chip(sent, bit).astype(f32)
-            if number + 1 < len(bits):
-                half = total.shape[0] // 2
-                total, sent = total[:half], total[half:].astype(bf16)
-        return total
-
-    def sum_all(self, values, chips_only=False):
-        if not chips_only:
-            values = values + self.to_core(values)
+    def sum_all(self, values, *others):
+        values = values + self.to_core(values)
         for low in range(0, len(self.q_bits), 2):
             bits = self.q_bits[low : low + 2]
             got = [self.to_chip(values, bit) for bit in bits]
@@ -407,28 +390,58 @@
                 values = (values + got[0]) + (got[1] + both)
             else:
                 values = values + got[0]
-        if not chips_only:
-            bit, bits = 1, []
-            while bit < self.mp_n:
-                bits.append(bit)
-                bit *= 2
-            flip = lambda mask: self.move(
-                values,
-                lambda q, c, s, t: (
-                    q,
-                    c,
-                    ((s * self.t_n + t) ^ mask) // self.t_n,
-                    ((s * self.t_n + t) ^ mask) % self.t_n,
-                ),
-            )
-            for low in range(0, len(bits), 2):
-                pair = bits[low : low + 2]
-                if len(pair) == 2:
-                    one, two, both = flip(pair[0]), flip(pair[1]), flip(pair[0] | pair[1])
-                    values = (values + one) + (two + both)
-                else:
-                    values = values + flip(pair[0])
+        values = after(values, *others)
+        bit, bits = 1, []
+        while bit < self.mp_n:
+            bits.append(bit)
+            bit *= 2
+
+        def flip(mask):
+            def target(q, c, s, t):
+                place = (s * self.t_n + t) ^ mask
+                return (q, c, place // self.t_n, place % self.t_n)
+
+            return self.move(values, target)
+
+        for low in range(0, len(bits), 2):
+            pair = bits[low : low + 2]
+            if len(pair) == 2:
+                one, two, both = flip(pair[0]), flip(pair[1]), flip(pair[0] | pair[1])
+                values = (values + one) + (two + both)
+            else:
+                values = values + flip(pair[0])
         return values
+
+
+class ChipSum:
+    def __init__(self, at, halves, first):
+        self.at = at
+        self.bits = list(at.bits_from(first))
+        self.parts, sent = [halves[0]], halves[1]
+        self.exchange(sent)
+
+    def exchange(self, sent):
+        self.got = self.at.to_chip(sent, self.bits.pop(0))
+        self.parts.append(self.got)
+
+    def total(self, rows=None):
+        total = self.parts[0][rows].astype(f32) if rows else self.parts[0].astype(f32)
+        for part in self.parts[1:]:
+            total = total + (part[rows] if rows else part).astype(f32)
+        return total
+
+    def step(self, *others):
+        if not self.bits:
+            return
+        self.parts[-1] = after(self.parts[-1], *others)
+        half = self.got.shape[0] // 2
+        sent = self.total(slice(half, None)).astype(bf16)
+        self.parts = [part[:half] for part in self.parts]
+        self.exchange(sent)
+
+    def rest(self, *others):
+        while self.bits:
+            self.step(*others)
 
 
 def pack_attn_kernel(place_ref, qkv_ref, out_ref, qkv_full, out_full, piece_ref):
@@ -517,6 +530,122 @@
     return up, down, up[:part], down[:part]
 
 
+def join_kernel(plan, count, *refs):
+    pieces, outs = refs[:count], refs[count:]
+    for out_ref, (start_cols, rows) in zip(outs, plan):
+        part = out_ref.shape[0] // len(rows)
+        for k, chunks in enumerate(rows):
+            col = 0
+            for index, start, size in chunks:
+                out_ref[k * part : (k + 1) * part, col : col + size] = pieces[index][
+                    :part, start : start + size
+                ]
+                col += size
+
+
+def join(pieces, part, plans):
+    shapes = [
+        jax.ShapeDtypeStruct((part * len(rows), sum(size for _, _, size in rows[0])), bf16)
+        for rows in plans
+    ]
+    return pl.pallas_call(
+        lambda *refs: join_kernel([(0, rows) for rows in plans], len(pieces), *refs),
+        in_specs=[in_vmem] * len(pieces),
+        out_specs=(in_vmem,) * len(plans),
+        out_shape=tuple(shapes),
+        compiler_params=pltpu.CompilerParams(vmem_limit_bytes=kernel_bytes),
+        name="join",
+    )(*pieces)
+
+
+def gelu_parts(values):
+    half = 0.5 * (1.0 + lax.erf(values * (0.5**0.5)))
+    bell = jnp.exp(-0.5 * values * values) * 0.3989422804014327
+    return (values * half, half + values * bell)
+
+
+def row_tiles(rows, tile=256):
+    tile = min(tile, rows)
+    return [slice(start, start + tile) for start in range(0, rows, tile)]
+
+
+def sum_nt_kernel(count, *refs):
+    lefts, rights, out_ref = refs[:count], refs[count : 2 * count], refs[-1]
+    for here in row_tiles(out_ref.shape[0]):
+        total = dot_nt(lefts[0][here, :], rights[0][...])
+        for left, right in zip(lefts[1:], rights[1:]):
+            total = total + dot_nt(left[here, :], right[...])
+        out_ref[here, :] = total.astype(bf16)
+
+
+def cost_of(flops):
+    return pl.CostEstimate(flops=flops // 2, bytes_accessed=1 << 20, transcendentals=0)
+
+
+def sum_nt(lefts, rights):
+    rows, width = lefts[0].shape[0], rights[0].shape[0]
+    return pl.pallas_call(
+        lambda *refs: sum_nt_kernel(len(lefts), *refs),
+        in_specs=[in_vmem] * (2 * len(lefts)),
+        out_specs=in_vmem,
+        out_shape=jax.ShapeDtypeStruct((rows, width), bf16),
+        compiler_params=pltpu.CompilerParams(vmem_limit_bytes=kernel_bytes),
+        cost_estimate=cost_of(2 * rows * width * sum(v.shape[1] for v in lefts)),
+        name="sum_nt",
+    )(*lefts, *rights)
+
+
+def up_kernel(normed_ref, weight_ref, bias_ref, act_ref, slope_ref):
+    for here in row_tiles(act_ref.shape[0]):
+        pre = dot_nn(normed_ref[here, :], weight_ref[...]) + bias_ref[...]
+        act, slope = gelu_parts(pre)
+        act_ref[here, :] = act.astype(bf16)
+        slope_ref[here, :] = slope
+
+
+def up_project(normed, weight, bias):
+    rows, cols = normed.shape[0], weight.shape[1]
+    return pl.pallas_call(
+        up_kernel,
+        in_specs=[in_vmem] * 3,
+        out_specs=(in_vmem, in_vmem),
+        out_shape=(
+            jax.ShapeDtypeStruct((rows, cols), bf16),
+            jax.ShapeDtypeStruct((rows, cols), f32),
+        ),
+        compiler_params=pltpu.CompilerParams(vmem_limit_bytes=kernel_bytes),
+        cost_estimate=cost_of(2 * rows * cols * normed.shape[1]),
+        name="up_project",
+    )(normed, weight, bias[None, :])
+
+
+def down_back_kernel(kept_ref, weight_ref, slope_ref, pre_ref, bias_ref):
+    total = None
+    for here in row_tiles(pre_ref.shape[0]):
+        grad = (dot_nn(kept_ref[here, :], weight_ref[...]) * slope_ref[here, :]).astype(bf16)
+        pre_ref[here, :] = grad
+        part = jnp.sum(grad.astype(f32), axis=0, keepdims=True)
+        total = part if total is None else total + part
+    bias_ref[...] = total
+
+
+def down_back(kept, weight, slope):
+    rows, cols = slope.shape
+    pre, bias = pl.pallas_call(
+        down_back_kernel,
+        in_specs=[in_vmem] * 3,
+        out_specs=(in_vmem, in_vmem),
+        out_shape=(
+            jax.ShapeDtypeStruct((rows, cols), bf16),
+            jax.ShapeDtypeStruct((1, cols), f32),
+        ),
+        compiler_params=pltpu.CompilerParams(vmem_limit_bytes=kernel_bytes),
+        cost_estimate=cost_of(2 * rows * cols * kept.shape[1]),
+        name="down_back",
+    )(kept, weight, slope)
+    return pre, bias[0]
+
+
 def halves_kernel(order, shape, *refs):
     operands, (kept_ref, sent_ref) = refs[:-2], refs[-2:]
     part = operands[0].shape[1] // len(order)
@@ -553,7 +682,7 @@
             out_shape=(halves, halves),
             compiler_params=pltpu.CompilerParams(vmem_limit_bytes=kernel_bytes),
             cost_estimate=pl.CostEstimate(
-                flops=3 * rows * width * cols, bytes_accessed=1 << 20, transcendentals=0
+                flops=rows * width * cols, bytes_accessed=1 << 20, transcendentals=0
             ),
             name="grad_halves",
         )(*operands)
@@ -703,12 +832,6 @@
         - jnp.mean(scaled, axis=-1, keepdims=True)
         - normed * jnp.mean(scaled * normed, axis=-1, keepdims=True)
     )
-
-
-def gelu_parts(values):
-    half = 0.5 * (1.0 + lax.erf(values * (0.5**0.5)))
-    bell = jnp.exp(-0.5 * values * values) * 0.3989422804014327
-    return (values * half, half + values * bell)
 
 
 def local(
@@ -804,32 +927,68 @@
     turn = 1 % len(at.q_bits)
     attn_pair = at.spread_pair(attn_inner, attn_outer)
     pair_first = after(attn_pair[:part], *mlp_near.values(), up_inner)
-    pair_near = at.gather_start(pair_first)
-    up_outer = at.spread_outer(after(up_inner, *mlp_near.values()))
-    down_inner = at.spread_inner(after(down_piece, up_inner, *mlp_near.values()), down_one)
-    near_done = (*pair_near.values(), up_outer, down_inner)
-    pair_near = {b: after(v, *near_done) for b, v in pair_near.items()}
     small = [
         small_own,
         small_of(attn_one[part:]),
         small_of(attn_pair[part:, :attn_cols]),
         small_of(attn_pair[part:, attn_cols:]),
     ]
-    qkv_w = [qkv_own, jnp.concatenate([v[:, :qkv_cols] for v in attn_pieces], axis=0)]
-    out_w = [out_own, jnp.concatenate([v[:, qkv_cols:] for v in attn_pieces], axis=0)]
+    tile = tile_of(seq_len)
+    tiles = seq_len // tile
+    padded = jnp.concatenate([jnp.zeros((tile,), jnp.int32), buckets])
+    spread = jnp.concatenate(
+        [padded[kk * tile : (kk + 2) * tile] for kk in range(tiles)]
+    )
+    choose = (jnp.arange(bucket_count, dtype=jnp.int32)[:, None] == spread[None, :]).astype(f32)
+
+    def lines_of(r):
+        rel_rows = small[r][units:].reshape(heads, bucket_count)
+        return jnp.dot(rel_rows, choose, precision=lax.Precision.HIGHEST)
+
+
+    columns = range(q_n)
+    qkv_one, out_one = join(
+        attn_pieces,
+        part,
+        [
+            [[(k, 0, qkv_cols)] for k in columns],
+            [[(k, qkv_cols, head_width)] for k in columns],
+        ],
+    )
+    qkv_w, out_w = [qkv_own, qkv_one], [out_own, out_one]
+
+    first_parts = norm_parts(inputs_low.astype(f32))
+    first_normed, first_inverse = first_parts
+    first_low = (first_normed * vectors[0] + vectors[1]).astype(bf16)
+    qkv, contexts, totals = [], [], []
+
+    def attention(r, *others):
+        qkv.append(after(dot_nn(first_low, qkv_w[r]).astype(bf16), *others))
+        context, total = attend(length, qkv[r], lines_of(r), heads)
+        contexts.append(context)
+        totals.append(total)
+
+    attention(0, mlp_one)
+    pair_first = after(pair_first, contexts[0])
+    pair_near = at.gather_start(pair_first)
+    up_outer = at.spread_outer(after(up_inner, *mlp_near.values()))
+    down_inner = at.spread_inner(after(down_piece, up_inner, *mlp_near.values()), down_one)
+    attention(1, attn_outer)
+    near_done = (*pair_near.values(), up_outer, down_inner)
+    pair_near = {b: after(v, *near_done, contexts[1]) for b, v in pair_near.items()}
     pair_pieces = []
     for k in range(2):
         cols = slice(k * attn_cols, (k + 1) * attn_cols)
-        pieces = at.gather_end(
-            pair_first[:, cols], {b: v[:, cols] for b, v in pair_near.items()}, k * turn
+        pair_pieces.append(
+            at.gather_end(
+                pair_first[:, cols], {b: v[:, cols] for b, v in pair_near.items()}, k * turn
+            )
         )
-        pair_pieces += pieces
-        qkv_w.append(jnp.concatenate([v[:, :qkv_cols] for v in pieces], axis=0))
-        out_w.append(jnp.concatenate([v[:, qkv_cols:] for v in pieces], axis=0))
     down_outer = at.spread_outer(after(down_inner, *near_done))
     incoming_near = at.relative(after(cotangent, *near_done), 2)
     incoming_pieces = {step: at.collect_piece(incoming_near, step) for step in (2, 3)}
-    mlp_near = {b: after(v, *pair_pieces) for b, v in mlp_near.items()}
+    pair_done = [v for pieces in pair_pieces for v in pieces[1:]]
+    mlp_near = {b: after(v, *pair_done) for b, v in mlp_near.items()}
     up_one_pieces = at.gather_end(up_one, {b: v[:, :units] for b, v in mlp_near.items()}, 0)
     down_one_pieces = at.gather_end(
         down_one, {b: v[:, units:] for b, v in mlp_near.items()}, turn
@@ -841,63 +1000,44 @@
     incoming_pieces.update({step: at.collect_piece(incoming_near, step) for step in (0, 1)})
     down_pair = after(at.spread_pair(down_inner, down_outer), *up_near.values())
 
-    def pair_halves(piece, near, first):
+    def pair_halves(piece, near):
         halves = []
         for k in range(2):
             cols = slice(k * units, (k + 1) * units)
             halves.append(
                 at.gather_end(piece[:, cols], {b: v[:, cols] for b, v in near.items()}, k * turn)
             )
-        return [jnp.concatenate(pair, axis=1) for pair in zip(*halves)]
-
-    up_pair_pieces = pair_halves(up_pair, up_near, 0)
+        return halves
+
+    def pair_join(halves):
+        return join(
+            halves[0] + halves[1], part, [[[(k, 0, units), (k + q_n, 0, units)] for k in columns]]
+        )[0]
+
+    up_halves = pair_halves(up_pair, up_near)
     down_near = at.gather_start(down_pair)
-    down_near = {b: after(v, *up_pair_pieces) for b, v in down_near.items()}
-    down_pair_pieces = pair_halves(down_pair, down_near, turn)
+    down_near = {b: after(v, up_halves[0][-1], up_halves[1][-1]) for b, v in down_near.items()}
+    down_halves = pair_halves(down_pair, down_near)
+    joined = join(
+        pair_pieces[0] + pair_pieces[1],
+        part,
+        [
+            [[(k + half_at, start, size)] for k in columns]
+            for half_at in (0, q_n)
+            for start, size in ((0, qkv_cols), (qkv_cols, head_width))
+        ],
+    )
+    qkv_w += joined[0::2]
+    out_w += joined[1::2]
+    attention(2, *one_done)
+    attention(3, *up_near.values())
     incoming_home = at.collect_end([incoming_pieces[k] for k in range(blocks)])
-    up_w = [
-        up_own,
-        jnp.concatenate(up_one_pieces, axis=0),
-        jnp.concatenate(up_pair_pieces, axis=0),
-    ]
-    down_w = [
-        down_own,
-        jnp.concatenate(down_one_pieces, axis=0),
-        jnp.concatenate(down_pair_pieces, axis=0),
-    ]
-
-    tile = tile_of(seq_len)
-    tiles = seq_len // tile
-    padded = jnp.concatenate([jnp.zeros((tile,), jnp.int32), buckets])
-    spread = jnp.concatenate(
-        [padded[kk * tile : (kk + 2) * tile] for kk in range(tiles)]
-    )
-    choose = (jnp.arange(bucket_count, dtype=jnp.int32)[:, None] == spread[None, :]).astype(f32)
-    rel_rows = jnp.concatenate(
-        [values[units:].reshape(heads, bucket_count) for values in small], axis=0
-    )
-    lines = jnp.dot(rel_rows, choose, precision=lax.Precision.HIGHEST)
+    rows_of = [[(k, 0, units)] for k in columns]
+    up_w = [up_own, join(up_one_pieces, part, [rows_of])[0], pair_join(up_halves)]
+    down_w = [down_own, join(down_one_pieces, part, [rows_of])[0], pair_join(down_halves)]
 
     inputs = inputs_low.astype(f32)
-    first_normed, first_inverse = norm_parts(inputs)
-    first_low = (first_normed * vectors[0] + vectors[1]).astype(bf16)
-    qkv, contexts, totals = [], [], []
-    for r in range(blocks):
-        qkv_r = dot_nn(first_low, qkv_w[r]).astype(bf16)
-        if r == 0:
-            qkv_r = after(qkv_r, mlp_one)
-        if r == 1:
-            qkv_r = after(qkv_r, attn_outer)
-        if r == 3:
-            qkv_r = after(qkv_r, *one_done)
-        qkv.append(qkv_r)
-        context, total = attend(length, qkv[r], lines[r * heads : (r + 1) * heads], heads)
-        contexts.append(context)
-        totals.append(total)
-    mixed = dot_nt(contexts[0], out_w[0])
-    for r in range(1, blocks):
-        mixed = mixed + dot_nt(contexts[r], out_w[r])
-    mixed = at.sum_team(jnp.where(row_keep, mixed, 0.0).astype(bf16))
+    mixed = at.sum_team(sum_nt(contexts, out_w))
     mixed = after(mixed, *up_near.values())
     middle = inputs + (mixed + vectors[4]) * row_mask
     second_normed, second_inverse = norm_parts(middle)
@@ -905,44 +1045,34 @@
     acts, slopes = [], []
     biases = [small[0][:units], small[1][:units], jnp.concatenate([small[2][:units], small[3][:units]])]
     for r in range(3):
-        pre = dot_nn(second_low, up_w[r]) + biases[r]
-        act, slope = gelu_parts(pre)
-        acts.append(act.astype(bf16))
+        act, slope = up_project(second_low, up_w[r], biases[r])
+        acts.append(act)
         slopes.append(slope)
-    fed = dot_nt(acts[0], down_w[0])
-    for r in range(1, 3):
-        fed = fed + dot_nt(acts[r], down_w[r])
     incoming_low = at.collect_both(incoming_home)
     kept = jnp.where(row_keep, incoming_low, jnp.zeros_like(incoming_low))
     fed_bias_grad = jnp.sum(kept.astype(f32), axis=0)
     bias_grads = [None] * blocks
 
-    def back_through(r, kept=kept):
-        pre_low = (dot_nn(kept, down_w[r]) * slopes[r]).astype(bf16)
-        return pre_low, jnp.sum(pre_low.astype(f32), axis=0), dot_nt(pre_low, up_w[r])
-
-    down_far = at.scatter_first(*grad_halves(at, [(kept, [acts[2]])], 0), 0)
-    down_near_halves = grad_halves(at, [(kept, [acts[0], acts[1]])], 0)
-    fed_low = after(fed.astype(bf16), *down_near_halves)
+    pre_pair, bias_pair = down_back(kept, down_w[2], slopes[2])
+    bias_grads[2], bias_grads[3] = bias_pair[:units], bias_pair[units:]
+    up_far_halves = grad_halves(at, [(second_low, [pre_pair])], 1)
+    up_far = ChipSum(at, up_far_halves, 1)
+    down_far_halves = grad_halves(at, [(after(kept, *up_far_halves), [acts[2]])], 0)
+    down_far = ChipSum(at, down_far_halves, 0)
+    down_near_halves = grad_halves(at, [(after(kept, *down_far_halves), acts[:2])], 0)
+    fed_low = sum_nt([after(acts[0], *down_far_halves)] + acts[1:], down_w)
     fed_share = at.sum_share(fed_low, length_rows)
     middle_share = at.share(middle, length_rows, 0, 0)
     mask_share = at.share(row_mask, length_rows, 0, 0)
     out_share = (middle_share + (fed_share + vectors[5]) * mask_share).astype(bf16)
-    pre_pair, bias_pair, back = back_through(2)
-    bias_grads[2], bias_grads[3] = bias_pair[:units], bias_pair[units:]
-    up_far_halves = grad_halves(at, [(second_low, [pre_pair])], 1)
-    up_far = at.scatter_first(*up_far_halves, 1)
-    out_pair = at.deliver_first(out_share)
-    kept_late = after(kept, out_share, *up_far_halves)
-    pre_own, bias_grads[0], term = back_through(0, kept_late)
-    back = back + term
-    pre_one, bias_grads[1], term = back_through(1, kept_late)
-    back = back + term
-    up_near_halves = grad_halves(at, [(second_low, [pre_own, pre_one])], 1)
-    back_low = after(back.astype(bf16), *up_near_halves)
+    out_got = at.deliver_first(out_share)
+    kept_late = after(kept, fed_low, *down_far_halves)
+    pre_own, bias_grads[0] = down_back(kept_late, down_w[0], slopes[0])
+    pre_one, bias_grads[1] = down_back(kept_late, down_w[1], slopes[1])
+    back_low = sum_nt([pre_own, pre_one, pre_pair], up_w)
+    up_near_halves = grad_halves(at, [(after(second_low, back_low), [pre_own, pre_one])], 1)
     second_grad = at.sum_team(back_low)
-    second_grad = after(second_grad, *down_far)
-    down_far = at.scatter_rest(down_far, 0)
+    second_grad = after(second_grad, *up_near_halves)
     lead = jnp.where((c == 0) & (at.t == 0), 1.0, 0.0)
     gain_two = jnp.sum(second_grad * second_normed, axis=0)
     shift_two = jnp.sum(second_grad, axis=0)
@@ -951,77 +1081,85 @@
     )
     branch = jnp.where(row_keep, middle_grad, 0.0).astype(bf16)
     mix_bias_grad = jnp.sum(branch.astype(f32), axis=0)
-    back = None
     rel_grads = [None] * blocks
+    branch = after(branch, up_far.got, down_far.got)
     context_grads = [dot_nn(branch, out_w[r]).astype(bf16) for r in range(blocks)]
     own_cols = slice(0, units)
     far_cols = slice(units, 2 * units)
     attn_sums = [None] * blocks
     attn_halves = [None] * blocks
+    proj_grads = [None] * blocks
     for r in reversed(range(blocks)):
         context_grad = context_grads[r]
         if r == 3:
-            context_grad = after(context_grad, *up_far, out_pair)
-            up_far = at.scatter_rest([after(v, out_pair) for v in up_far], 1)
-            out_pair = after(out_pair, *up_far_halves)
-            block_out = at.deliver_second(out_pair)
+            up_far.rest(down_far.got)
+            down_far.rest(up_far.got)
         if r == 2:
-            context_grad = after(context_grad, down_far, up_far, block_out)
+            far_done = (up_far.got, down_far.got)
+            context_grad = after(context_grad, *far_done)
+            down_near_sum = ChipSum(at, [after(v, *far_done) for v in down_near_halves], 0)
+            up_near_sum = ChipSum(at, [after(v, *far_done) for v in up_near_halves], 1)
+            far_sums = (down_far.total(), up_far.total())
             mlp_far = jnp.concatenate(
-                [
-                    down_far[:, own_cols],
-                    up_far[:, own_cols],
-                    down_far[:, far_cols],
-                    up_far[:, far_cols],
-                ],
-                axis=1,
+                [v[:, cols] for cols in (own_cols, far_cols) for v in far_sums], axis=1
             ).astype(bf16)
-            mlp_far = at.fold_outer(after(mlp_far, block_out))
-            down_near_halves = [after(v, up_far, block_out) for v in down_near_halves]
-            up_near_halves = [after(v, down_far, block_out) for v in up_near_halves]
-            down_near_sum = at.scatter_first(*down_near_halves, 0)
-            up_near_sum = at.scatter_first(*up_near_halves, 1)
+            far_got = at.fold_outer(mlp_far)
+        if r == 1:
+            context_grad = after(context_grad, out_got)
         if r == 0:
-            context_grad = after(context_grad, *down_near_sum, *up_near_sum, mlp_far)
-            mlp_one, mlp_own = at.fold_inner(after(mlp_far, *up_near_sum))
-            for k in (3, 2):
-                held = [after(v, *down_near_sum, *up_near_sum) for v in attn_halves[k]]
-                attn_sums[k] = at.scatter_first(*held, k % 2)
-            down_near_sum = at.scatter_rest(down_near_sum, 0)
-            up_near_sum = at.scatter_rest(up_near_sum, 1)
+            near_firsts = (down_near_sum.got, up_near_sum.got)
+            context_grad = after(context_grad, *near_firsts, far_got)
+            mlp_far = at.fold_add(mlp_far, after(far_got, *near_firsts))
+            inner_got = at.fold_inner(mlp_far)
+            out_pair = at.deliver_pair(out_share, after(out_got, far_got))
+            out_last = at.deliver_last(out_pair)
+            down_near_sum.rest(*near_firsts)
+            up_near_sum.rest(*near_firsts)
+            near_done = (down_near_sum.got, up_near_sum.got)
         proj_grad, dist = attend_back(
-            length, qkv[r], lines[r * heads : (r + 1) * heads], totals[r], context_grad, heads
+            length, qkv[r], lines_of(r), totals[r], context_grad, heads
         )
         rel_grads[r] = dist
         attn_halves[r] = grad_halves(
             at, [(first_low, [proj_grad]), (branch, [contexts[r]])], r % 2
         )
-        term = dot_nt(proj_grad, qkv_w[r])
-        back = term if back is None else back + term
-    there = (*attn_sums[3], *attn_sums[2], down_near_sum, up_near_sum)
+        proj_grads[r] = proj_grad
+    back_low = after(sum_nt(proj_grads, qkv_w), *near_done)
+    for k in (3, 2):
+        attn_sums[k] = ChipSum(at, [after(v, *near_done) for v in attn_halves[k]], k % 2)
+    firsts = (attn_sums[3].got, attn_sums[2].got)
+    first_grad = at.sum_share(back_low, length_rows)
     for k in (1, 0):
-        held = [after(v, *there) for v in attn_halves[k]]
-        attn_sums[k] = at.scatter_first(*held, k % 2)
-    for k in (3, 2, 1, 0):
-        attn_sums[k] = at.scatter_rest(attn_sums[k], k % 2)
-    mlp_one = mlp_one + jnp.concatenate(
-        [down_near_sum[:, far_cols], up_near_sum[:, far_cols]], axis=1
-    )
-    mlp_own = mlp_own + jnp.concatenate(
-        [down_near_sum[:, own_cols], up_near_sum[:, own_cols]], axis=1
-    )
-    mlp_mine = mlp_own + at.to_slot(mlp_one.astype(bf16), 1).astype(f32)
-    attn_far = jnp.concatenate([attn_sums[2], attn_sums[3]], axis=1).astype(bf16)
-    attn_one_sum, attn_own_sum = at.fold_inner(at.fold_outer(attn_far))
-    attn_one_sum = (attn_one_sum + attn_sums[1]).astype(bf16)
-    attn_mine = attn_own_sum + attn_sums[0] + at.to_slot(attn_one_sum, 1).astype(f32)
+        attn_sums[k] = ChipSum(at, [after(v, *firsts) for v in attn_halves[k]], k % 2)
+    for k in (3, 2):
+        attn_sums[k].rest(*firsts)
+    first_grad = after(first_grad, *firsts)
+    attn_far = jnp.concatenate([attn_sums[2].total(), attn_sums[3].total()], axis=1).astype(bf16)
+    attn_got = at.fold_outer(attn_far)
+    for k in (1, 0):
+        attn_sums[k].rest(attn_sums[2].got, attn_sums[3].got, attn_sums[0].got, attn_sums[1].got)
+    mlp_size = 2 * units
+    mlp_near = (down_near_sum.total(), up_near_sum.total())
+    mlp_one = jnp.concatenate([v[:, far_cols] for v in mlp_near], axis=1)
+    mlp_own = jnp.concatenate([v[:, own_cols] for v in mlp_near], axis=1)
+    mlp_one = (mlp_one + inner_got[:, :mlp_size].astype(f32)).astype(bf16)
+    last_got = at.to_slot(mlp_one, 1)
+    mlp_mine = mlp_own + inner_got[:, mlp_size:].astype(f32) + last_got.astype(f32)
+    attn_got = after(attn_got, attn_sums[0].got, attn_sums[1].got)
+    attn_inner_got = at.fold_inner(at.fold_add(attn_far, attn_got))
+    attn_one_sum = attn_inner_got[:, :attn_cols].astype(f32) + attn_sums[1].total()
+    attn_last_got = at.to_slot(attn_one_sum.astype(bf16), 1)
+    attn_mine = (
+        attn_sums[0].total()
+        + attn_inner_got[:, attn_cols:].astype(f32)
+        + attn_last_got.astype(f32)
+    )
     rel_grad = lax.dot_general(
         jnp.concatenate(rel_grads, axis=0),
         choose,
         (((1,), (1,)), ((), ())),
         precision=lax.Precision.HIGHEST,
     )
-    first_grad = at.sum_share(back.astype(bf16), length_rows)
     normed_share = at.share(first_normed, length_rows, 0, 0)
     inverse_share = at.share(first_inverse, length_rows, 0, 0)
     middle_grad_share = at.share(middle_grad, length_rows, 0, 0)
@@ -1030,8 +1168,11 @@
     input_share = middle_grad_share + norm_back(
         first_grad, normed_share, inverse_share, vectors[0]
     )
-    input_pair = at.deliver_first(input_share.astype(bf16))
-    input_grad = at.relative(at.deliver_second(input_pair), 2).astype(f32)
+    input_low = input_share.astype(bf16)
+    input_got = at.deliver_first(after(input_low, attn_got))
+    input_pair = at.deliver_pair(input_low, input_got)
+    input_last = at.deliver_last(input_pair)
+    input_grad = at.relative(at.delivered(input_pair, input_last), 2).astype(f32)
 
     def by_place(rows_of):
         around = jnp.stack(rows_of)
@@ -1058,7 +1199,9 @@
         ]
     )
     joined = at.sum_all(
-        jnp.concatenate([at.relative(vector_grad, 1).reshape(-1), small_grad.reshape(-1)])
+        jnp.concatenate([at.relative(vector_grad, 1).reshape(-1), small_grad.reshape(-1)]),
+        attn_inner_got,
+        last_got,
     )
     vector_grad = joined[: vector_grad.size].reshape(vector_grad.shape)
     small_sum = lax.dynamic_index_in_dim(
@@ -1156,7 +1299,8 @@
     new, states = list(new), list(states)
     new[0] = jnp.transpose(new[0], (1, 0, 2))
     states[0] = jnp.transpose(states[0], (0, 2, 1, 3))
-    results = [at.relative(block_out, 2), input_grad]
+    block_out = at.relative(at.delivered(out_pair, out_last), 2)
+    results = [block_out, input_grad]
     for k in range(4):
         results += [new[k], states[k]]
     for k in range(2):

time: 534 us -> 486 us (0.910)
  matrix products: 65.9 us -> 8.79 us
  Pallas kernels: 85.2 us -> 115 us
  local copies, waits for them, and re-layouts: 67.6 us -> 58.1 us
  other arithmetic: 75.3 us -> 67.5 us
  starting transfers between devices: 134 us -> 127 us
    dot_general x15 -> x4, matrix products: 34.3 us -> 0.78 us  [lines_of(): return jnp.dot(rel_rows, choose, precision=lax.Precision.HIGHEST)]
    pallas_call x0 -> x16, Pallas kernels: none -> 30.3 us  [the longest x4 16.6 us: sum_nt(): pl.pallas_call(lambda *refs: sum_nt_kernel(len(lefts), *refs), in_specs=[...]
    dot_general x14 -> x8, matrix products: 31.3 us -> 7.8 us  [dot_nn(): lax.dot_general(left, right, (((1,), (0,)), ((), ())), preferred_element_...]
    slice x27 -> x9, local copies, waits for them, and re-layouts: 18.2 us -> 6.76 us  [the longest x2 3.2 us: fold_add(): turned = jnp.concatenate([got[:, size:], got[:, :size]], axis=1)]
    convert_element_type x15 -> x14, other arithmetic: 19.7 us -> 12.3 us  [the longest x8 4.64 us: step(): sent = self.total(slice(half, None)).astype(bf16)]
    ppermute x82, starting transfers between devices: 134 us -> 127 us  [move(): return lax.ppermute(values, ('dp', 'mp'), pairs)]
    unnamed x355 -> x252, local copies, waits for them, and re-layouts: 22.9 us -> 24.7 us
  transfers between devices with their start and end apart: 82 -> 82, of which waited for: 19 -> 27; matrix products, arithmetic and copies ran while one was open for 35% -> 20% of each run, Pallas kernels for 15% -> 22%
where the time goes in v2:
time: 486 us; the launch traced here: 476 us
  starting transfers between devices  127 us (26%)
  Pallas kernels  115 us (24%)
  waiting for transfers between devices  92.8 us (19%)
  other arithmetic  67.5 us (14%)
  local copies, waits for them, and re-layouts  58.1 us (12%)
  matrix products  8.79 us (2%)
  between operations  6.85 us (1%)
    ppermute x82, starting transfers between devices, move(): return lax.ppermute(values, ('dp', 'mp'), pairs)  127 us
    ppermute x82, waiting for transfers between devices, move(): return lax.ppermute(values, ('dp', 'mp'), pairs)  92.8 us
    pallas_call x4, Pallas kernels, attend_back(): pl.pallas_call(lambda *refs: attend_back_kernel(heads, *refs), out_shape=...  32.6 us
    unnamed x252, local copies, waits for them, and re-layouts  24.7 us
    pallas_call x8, Pallas kernels, grad_halves(): pl.pallas_call(lambda *refs: halves_kernel(order, [len(rights) for _, rig...  18.2 us
    pallas_call x4, Pallas kernels, sum_nt(): pl.pallas_call(lambda *refs: sum_nt_kernel(len(lefts), *refs), in_specs=[...  16.6 us
    pallas_call x4, Pallas kernels, attend(): pl.pallas_call(lambda *refs: attend_kernel(heads, *refs), out_shape=(jax....  15.6 us
  transfers between devices with their start and end apart: 82, of which 27 were waited for; matrix products, arithmetic and copies ran while one was open for 20% of the time, Pallas kernels for 22%

profile of v2, /device:TPU:1, one launch (start us, length us, event | category | flops | bytes accessed | tf_op | source)
XLA Modules:
  0.0 476.2 jit_solution(13242560046728463758)
XLA Ops:
  5.2 4.6 pack_attn.1
  13.3 5.6 %collective-permute-start.1 = (bf16[256,1024]{1,0:T(8,128)(2,1)S(1)}, bf16[256,1024]{1,0:T(8,128)(2,1)}, u32[]{:S(2)}, u32[]{:S(2)}) collective-permute-start(bf16[256,1024]{1,0:T(8,128)(2,1)S(1)} %get-tuple-element.421), channel_id=1, source_target_pairs={{2,0},{3,1},{4,6},{5,7},{10,8},{11,9},{12,14},{13,15},{18,16},{19,... | collective-permute-start | bytes 1572872 | tf_op jit(solution)/shard_map/ppermute | solution.py:233
  23.0 5.3 %pack_mlp.1 = (bf16[1024,512]{1,0:T(8,128)(2,1)}, bf16[1024,512]{1,0:T(8,128)(2,1)}, bf16[256,512]{1,0:T(8,128)(2,1)}, bf16[256,512]{1,0:T(8,128)(2,1)}) custom-call(s32[2]{0:T(128)} %pad_add_fusion.1.place_ref, f32[1024,1024]{1,0:T(8,128)} %refs_2_.1, f32[1024,1024]{1,0:T(8,128)} %refs_3_.1), custom_call_target="tpu_custom_call" | custom-call | tf_op jit(solution)/shard_map/pack_mlp/pallas_call | solution.py:507
  49.2 5.8 %collective-permute-done.10 = bf16[256,1024]{1,0:T(8,128)(2,1)} collective-permute-done((bf16[256,1024]{1,0:T(8,128)(2,1)}, bf16[256,1024]{1,0:T(8,128)(2,1)}, u32[]{:S(2)}, u32[]{:S(2)}) %collective-permute-start.10) | collective-permute-done | bytes 524320 | tf_op jit(solution)/shard_map/ppermute | solution.py:233
  64.2 5.2 %collective-permute-done.12 = bf16[256,1024]{1,0:T(8,128)(2,1)S(1)} collective-permute-done((bf16[256,1024]{1,0:T(8,128)(2,1)}, bf16[256,1024]{1,0:T(8,128)(2,1)S(1)}, u32[]{:S(2)}, u32[]{:S(2)}) %collective-permute-start.12) | collective-permute-done | bytes 524320 | tf_op jit(solution)/shard_map/ppermute | solution.py:233
  81.6 10.6 %collective-permute-done.17 = bf16[256,1024]{1,0:T(8,128)(2,1)} collective-permute-done((bf16[256,1024]{1,0:T(8,128)(2,1)}, bf16[256,1024]{1,0:T(8,128)(2,1)}, u32[]{:S(2)}, u32[]{:S(2)}) %collective-permute-start.17) | collective-permute-done | bytes 524320 | tf_op jit(solution)/shard_map/ppermute | solution.py:233
  110.9 5.3 %collective-permute-done.15 = bf16[256,1024]{1,0:T(8,128)(2,1)S(1)} collective-permute-done((bf16[256,1024]{1,0:T(8,128)(2,1)S(1)}, bf16[256,1024]{1,0:T(8,128)(2,1)S(1)}, u32[]{:S(2)}, u32[]{:S(2)}) %collective-permute-start.15) | collective-permute-done | bytes 524320 | tf_op jit(solution)/shard_map/ppermute | solution.py:233
  119.7 6.2 %collective-permute-start.28 = (bf16[256,1024]{1,0:T(8,128)(2,1)S(1)}, bf16[256,1024]{1,0:T(8,128)(2,1)S(1)}, u32[]{:S(2)}, u32[]{:S(2)}) collective-permute-start(bf16[256,1024]{1,0:T(8,128)(2,1)S(1)} %get-tuple-element.415), channel_id=1, source_target_pairs={{2,0},{3,1},{4,6},{5,7},{10,8},{11,9},{12,14},{13,15},{18,16},{19,... | collective-permute-start | bytes 1572872 | tf_op jit(solution)/shard_map/ppermute | solution.py:233
  142.5 4.7 collective-permute-done.24
  164.1 6.0 %collective-permute-start.29 = (bf16[256,1024]{1,0:T(8,128)(2,1)S(1)}, bf16[256,1024]{1,0:T(8,128)(2,1)S(1)}, u32[]{:S(2)}, u32[]{:S(2)}) collective-permute-start(bf16[256,1024]{1,0:T(8,128)(2,1)S(1)} %get-tuple-element.414), channel_id=1, source_target_pairs={{2,1},{3,0},{4,7},{5,6},{10,9},{11,8},{12,15},{13,14},{18,17},{19,... | collective-permute-start | bytes 1572872 | tf_op jit(solution)/shard_map/ppermute | solution.py:233
  170.1 6.3 %collective-permute-done.33.refs_7_ = bf16[256,512]{1,0:T(8,128)(2,1)S(1)} collective-permute-done((bf16[256,512]{1,0:T(8,128)(2,1)S(1)}, bf16[256,512]{1,0:T(8,128)(2,1)S(1)}, u32[]{:S(2)}, u32[]{:S(2)}) %collective-permute-start.33) | collective-permute-done | bytes 262176 | tf_op jit(solution)/shard_map/ppermute | solution.py:233
  214.5 5.0 %sum_nt.6 = bf16[1024,1024]{1,0:T(8,128)(2,1)S(1)} custom-call(bf16[1024,512]{1,0:T(8,128)(2,1)S(1)} %get-tuple-element.214.refs_0_.refs_1_, bf16[1024,512]{1,0:T(8,128)(2,1)S(1)} %get-tuple-element.216.refs_1_.refs_2_, bf16[1024,1024]{1,0:T(8,128)(2,1)S(1)} %get-tuple-element.199.refs_1_.refs_2_, bf16[1024,512]{1,0:T(8,128)(2,1)S(1)} %copy-done.10, ...), custom_call_target="tpu_custom_call" | custom-call | flops 2147483648 | bytes 1048576 | tf_op jit(solution)/shard_map/sum_nt/pallas_call | solution.py:587
  221.6 4.9 %collective-permute-done.39 = bf16[512,1024]{1,0:T(8,128)(2,1)S(1)} collective-permute-done((bf16[512,1024]{1,0:T(8,128)(2,1)S(1)}, bf16[512,1024]{1,0:T(8,128)(2,1)S(1)}, u32[]{:S(2)}, u32[]{:S(2)}) %collective-permute-start.39) | collective-permute-done | bytes 1048608 | tf_op jit(solution)/shard_map/ppermute | solution.py:233
  232.8 5.2 %collective-permute-done.41 = bf16[256,1024]{1,0:T(8,128)(2,1)S(1)} collective-permute-done((bf16[256,1024]{1,0:T(8,128)(2,1)S(1)}, bf16[256,1024]{1,0:T(8,128)(2,1)S(1)}, u32[]{:S(2)}, u32[]{:S(2)}) %collective-permute-start.41) | collective-permute-done | bytes 524320 | tf_op jit(solution)/shard_map/ppermute | solution.py:233
  243.3 5.1 %collective-permute-done.42 = bf16[256,1024]{1,0:T(8,128)(2,1)S(1)} collective-permute-done((bf16[256,1024]{1,0:T(8,128)(2,1)S(1)}, bf16[256,1024]{1,0:T(8,128)(2,1)S(1)}, u32[]{:S(2)}, u32[]{:S(2)}) %collective-permute-start.42) | collective-permute-done | bytes 524320 | tf_op jit(solution)/shard_map/ppermute | solution.py:233
  260.8 8.0 %attend_back.6 = (bf16[1024,384]{1,0:T(8,128)(2,1)S(1)}, f32[2,2048]{1,0:T(2,128)S(1)}) custom-call(s32[1]{0:T(128)} %dynamic_slice.186.refs_0_, bf16[1024,384]{1,0:T(8,128)(2,1)S(1)} %convolution_convert_fusion.1.refs_1_, f32[2,2048]{1,0:T(2,128)S(1)} %fusion.17.refs_2_, f32[2,1024]{1,0:T(2,128)S(1)} %get-tuple-element.232.refs_3_, ...), custom_call_target="tpu_custom_call" | custom-call | flops 2684354560 | bytes 1048576 | tf_op jit(solution)/shard_map/attend_back/pallas_call | solution.py:165
  270.3 8.4 %attend_back.7 = (bf16[1024,384]{1,0:T(8,128)(2,1)S(1)}, f32[2,2048]{1,0:T(2,128)S(1)}) custom-call(s32[1]{0:T(128)} %dynamic_slice.186.refs_0_, bf16[1024,384]{1,0:T(8,128)(2,1)S(1)} %convolution_convert_fusion.refs_1_, f32[2,2048]{1,0:T(2,128)S(1)} %fusion.16.refs_2_, f32[2,1024]{1,0:T(2,128)S(1)} %get-tuple-element.235.refs_3_, ...), custom_call_target="tpu_custom_call" | custom-call | flops 2684354560 | bytes 1048576 | tf_op jit(solution)/shard_map/attend_back/pallas_call | solution.py:165
  282.6 8.2 %attend_back.5 = (bf16[1024,384]{1,0:T(8,128)(2,1)S(1)}, f32[2,2048]{1,0:T(2,128)S(1)}) custom-call(s32[1]{0:T(128)} %dynamic_slice.186.refs_0_, bf16[1024,384]{1,0:T(8,128)(2,1)S(1)} %convolution_convert_fusion.2.refs_1_, f32[2,2048]{1,0:T(2,128)S(1)} %fusion.18.refs_2_, f32[2,1024]{1,0:T(2,128)S(1)} %get-tuple-element.229.refs_3_, ...), custom_call_target="tpu_custom_call" | custom-call | flops 2684354560 | bytes 1048576 | tf_op jit(solution)/shard_map/attend_back/pallas_call | solution.py:165
  305.7 8.0 %attend_back.4 = (bf16[1024,384]{1,0:T(8,128)(2,1)S(1)}, f32[2,2048]{1,0:T(2,128)S(1)}) custom-call(s32[1]{0:T(128)} %dynamic_slice.186.refs_0_, bf16[1024,384]{1,0:T(8,128)(2,1)S(1)} %convolution_convert_fusion.3.refs_1_, f32[2,2048]{1,0:T(2,128)S(1)} %fusion.19.refs_2_, f32[2,1024]{1,0:T(2,128)S(1)} %get-tuple-element.221.refs_3_, ...), custom_call_target="tpu_custom_call" | custom-call | flops 2684354560 | bytes 1048576 | tf_op jit(solution)/shard_map/attend_back/pallas_call | solution.py:165
  326.7 4.7 sum_nt.7
  332.7 6.7 %collective-permute-start.50 = (bf16[512,1024]{1,0:T(8,128)(2,1)S(1)}, bf16[512,1024]{1,0:T(8,128)(2,1)S(1)}, u32[]{:S(2)}, u32[]{:S(2)}) collective-permute-start(bf16[512,1024]{1,0:T(8,128)(2,1)S(1)} %pad_maximum_fusion.6), channel_id=1, source_target_pairs={{0,4},{1,5},{2,6},{3,7},{4,0},{5,1},{6,2},{7,3},{8,12},{9,13},{10,... | collective-permute-start | bytes 3145736 | tf_op jit(solution)/shard_map/ppermute | solution.py:233
  388.7 9.6 %collective-permute-start.60 = (bf16[512,1024]{1,0:T(8,128)(2,1)}, bf16[512,1024]{1,0:T(8,128)(2,1)}, u32[]{:S(2)}, u32[]{:S(2)}) collective-permute-start(bf16[512,1024]{1,0:T(8,128)(2,1)} %fusion.4), channel_id=1, source_target_pairs={{2,4},{3,5},{4,2},{5,3},{10,12},{11,13},{12,10},{13,11},{18,20},{1... | collective-permute-start | bytes 3145736 | tf_op jit(solution)/shard_map/ppermute | solution.py:233
  403.1 11.9 %collective-permute-done.72 = f32[10752]{0:T(1024)S(1)} collective-permute-done((f32[10752]{0:T(1024)S(1)}, f32[10752]{0:T(1024)S(1)}, u32[]{:S(2)}, u32[]{:S(2)}) %collective-permute-start.72) | collective-permute-done | bytes 43040 | tf_op jit(solution)/shard_map/ppermute | solution.py:233
  425.9 10.4 %collective-permute-start.64 = (f32[128,512]{1,0:T(8,128)S(1)}, f32[128,512]{1,0:T(8,128)S(1)}, u32[]{:S(2)}, u32[]{:S(2)}) collective-permute-start(f32[128,512]{1,0:T(8,128)S(1)} %get-tuple-element.433), channel_id=1, source_target_pairs={{0,4},{1,5},{2,6},{3,7},{4,0},{5,1},{6,2},{7,3},{8,12},{9,13},{10,... | collective-permute-start | bytes 786440 | tf_op jit(solution)/shard_map/ppermute | solution.py:233
  (647 shorter events, 307.6 us)
Async XLA Ops:
  3.1 36.5 %collective-permute-start = (bf16[256,1024]{1,0:T(8,128)(2,1)S(1)}, bf16[256,1024]{1,0:T(8,128)(2,1)}, u32[]{:S(2)}, u32[]{:S(2)}) collective-permute-start(bf16[256,1024]{1,0:T(8,128)(2,1)S(1)} %get-tuple-element.422), channel_id=1, source_target_pairs={{0,1},{1,0},{6,7},{7,6},{8,9},{9,8},{14,15},{15,14},{16,17},{17,16... | collective-permute-start | bytes 1572872 | tf_op jit(solution)/shard_map/ppermute | solution.py:233
  11.1 28.5 %collective-permute-start.2 = (bf16[272,512]{1,0:T(8,128)(2,1)S(1)}, bf16[272,512]{1,0:T(8,128)(2,1)S(1)}, u32[]{:S(2)}, u32[]{:S(2)}) collective-permute-start(bf16[272,512]{1,0:T(8,128)(2,1)S(1)} %constant_dynamic-update-slice_fusion), channel_id=1, source_target_pairs={{0,1},{1,0},{2,3},{3,2},{4,5},{5,4},{6,7},{7,6},{8,9},{9,8},{10,11... | collective-permute-start | bytes 835592 | tf_op jit(solution)/shard_map/ppermute | solution.py:233
  13.3 28.9 %collective-permute-start.1 = (bf16[256,1024]{1,0:T(8,128)(2,1)S(1)}, bf16[256,1024]{1,0:T(8,128)(2,1)}, u32[]{:S(2)}, u32[]{:S(2)}) collective-permute-start(bf16[256,1024]{1,0:T(8,128)(2,1)S(1)} %get-tuple-element.421), channel_id=1, source_target_pairs={{2,0},{3,1},{4,6},{5,7},{10,8},{11,9},{12,14},{13,15},{18,16},{19,... | collective-permute-start | bytes 1572872 | tf_op jit(solution)/shard_map/ppermute | solution.py:233
  18.9 23.4 %collective-permute-start.3 = (bf16[256,1024]{1,0:T(8,128)(2,1)}, bf16[256,1024]{1,0:T(8,128)(2,1)}, u32[]{:S(2)}, u32[]{:S(2)}) collective-permute-start(bf16[256,1024]{1,0:T(8,128)(2,1)} %get-tuple-element.420), channel_id=1, source_target_pairs={{2,1},{3,0},{4,7},{5,6},{10,9},{11,8},{12,15},{13,14},{18,17},{19,... | collective-permute-start | bytes 1572872 | tf_op jit(solution)/shard_map/ppermute | solution.py:233
  60.3 33.1 %collective-permute-start.4 = (bf16[1024,1024]{1,0:T(8,128)(2,1)}, bf16[1024,1024]{1,0:T(8,128)(2,1)}, u32[]{:S(2)}, u32[]{:S(2)}) collective-permute-start(bf16[1024,1024]{1,0:T(8,128)(2,1)} %constant_dynamic-update-slice_fusion.12), channel_id=1, source_target_pairs={{0,4},{1,5},{6,2},{7,3},{8,12},{9,13},{14,10},{15,11},{16,20},{17,... | collective-permute-start | bytes 6291464 | tf_op jit(solution)/shard_map/ppermute | solution.py:233
  119.7 38.0 %collective-permute-start.28 = (bf16[256,1024]{1,0:T(8,128)(2,1)S(1)}, bf16[256,1024]{1,0:T(8,128)(2,1)S(1)}, u32[]{:S(2)}, u32[]{:S(2)}) collective-permute-start(bf16[256,1024]{1,0:T(8,128)(2,1)S(1)} %get-tuple-element.415), channel_id=1, source_target_pairs={{2,0},{3,1},{4,6},{5,7},{10,8},{11,9},{12,14},{13,15},{18,16},{19,... | collective-permute-start | bytes 1572872 | tf_op jit(solution)/shard_map/ppermute | solution.py:233
  137.9 21.2 %collective-permute-start.27 = (bf16[256,1024]{1,0:T(8,128)(2,1)S(1)}, bf16[256,1024]{1,0:T(8,128)(2,1)S(1)}, u32[]{:S(2)}, u32[]{:S(2)}) collective-permute-start(bf16[256,1024]{1,0:T(8,128)(2,1)S(1)} %dynamic-slice_bitcast_fusion.2), channel_id=1, source_target_pairs={{0,1},{1,0},{6,7},{7,6},{8,9},{9,8},{14,15},{15,14},{16,17},{17,16... | collective-permute-start | bytes 1572872 | tf_op jit(solution)/shard_map/ppermute | solution.py:233
  153.5 30.8 %collective-permute-start.26 = (bf16[1024,1024]{1,0:T(8,128)(2,1)S(1)}, bf16[1024,1024]{1,0:T(8,128)(2,1)S(1)}, u32[]{:S(2)}, u32[]{:S(2)}) collective-permute-start(bf16[1024,1024]{1,0:T(8,128)(2,1)S(1)} %sum_nt.4), channel_id=1, source_target_pairs={{0,4},{1,5},{2,6},{3,7},{4,0},{5,1},{6,2},{7,3},{8,12},{9,13},{10,... | collective-permute-start | bytes 6291464 | tf_op jit(solution)/shard_map/ppermute | solution.py:233
  199.2 27.3 %collective-permute-start.40 = (bf16[512,1024]{1,0:T(8,128)(2,1)S(1)}, bf16[512,1024]{1,0:T(8,128)(2,1)S(1)}, u32[]{:S(2)}, u32[]{:S(2)}) collective-permute-start(bf16[512,1024]{1,0:T(8,128)(2,1)S(1)} %get-tuple-element.201), channel_id=1, source_target_pairs={{0,16},{1,17},{2,18},{3,19},{4,20},{5,21},{6,22},{7,23},{8,24},{9,... | collective-permute-start | bytes 3145736 | tf_op jit(solution)/shard_map/ppermute | solution.py:233
  203.1 23.4 %collective-permute-start.39 = (bf16[512,1024]{1,0:T(8,128)(2,1)S(1)}, bf16[512,1024]{1,0:T(8,128)(2,1)S(1)}, u32[]{:S(2)}, u32[]{:S(2)}) collective-permute-start(bf16[512,1024]{1,0:T(8,128)(2,1)S(1)} %get-tuple-element.205), channel_id=1, source_target_pairs={{0,8},{1,9},{2,10},{3,11},{4,12},{5,13},{6,14},{7,15},{8,0},{9,1},... | collective-permute-start | bytes 3145736 | tf_op jit(solution)/shard_map/ppermute | solution.py:233
  219.5 33.4 %collective-permute-start.45 = (bf16[1024,1024]{1,0:T(8,128)(2,1)S(1)}, bf16[1024,1024]{1,0:T(8,128)(2,1)S(1)}, u32[]{:S(2)}, u32[]{:S(2)}) collective-permute-start(bf16[1024,1024]{1,0:T(8,128)(2,1)S(1)} %sum_nt.6), channel_id=1, source_target_pairs={{0,4},{1,5},{2,6},{3,7},{4,0},{5,1},{6,2},{7,3},{8,12},{9,13},{10,... | collective-permute-start | bytes 6291464 | tf_op jit(solution)/shard_map/ppermute | solution.py:233
  239.1 39.6 %collective-permute-start.38 = (bf16[512,1024]{1,0:T(8,128)(2,1)S(1)}, bf16[512,1024]{1,0:T(8,128)(2,1)S(1)}, u32[]{:S(2)}, u32[]{:S(2)}) collective-permute-start(bf16[512,1024]{1,0:T(8,128)(2,1)S(1)} %fusion.3), channel_id=1, source_target_pairs={{2,4},{3,5},{4,2},{5,3},{10,12},{11,13},{12,10},{13,11},{18,20},{1... | collective-permute-start | bytes 3145736 | tf_op jit(solution)/shard_map/ppermute | solution.py:233
  248.4 48.2 %collective-permute-start.47 = (bf16[512,1024]{1,0:T(8,128)(2,1)S(1)}, bf16[512,1024]{1,0:T(8,128)(2,1)S(1)}, u32[]{:S(2)}, u32[]{:S(2)}) collective-permute-start(bf16[512,1024]{1,0:T(8,128)(2,1)S(1)} %get-tuple-element.226), channel_id=1, source_target_pairs={{0,16},{1,17},{2,18},{3,19},{4,20},{5,21},{6,22},{7,23},{8,24},{9,... | collective-permute-start | bytes 3145736 | tf_op jit(solution)/shard_map/ppermute | solution.py:233
  248.9 47.7 %collective-permute-start.46 = (bf16[512,1024]{1,0:T(8,128)(2,1)S(1)}, bf16[512,1024]{1,0:T(8,128)(2,1)S(1)}, u32[]{:S(2)}, u32[]{:S(2)}) collective-permute-start(bf16[512,1024]{1,0:T(8,128)(2,1)S(1)} %get-tuple-element.225), channel_id=1, source_target_pairs={{0,8},{1,9},{2,10},{3,11},{4,12},{5,13},{6,14},{7,15},{8,0},{9,1},... | collective-permute-start | bytes 3145736 | tf_op jit(solution)/shard_map/ppermute | solution.py:233
  250.7 46.0 %collective-permute-start.43 = (bf16[256,2048]{1,0:T(8,128)(2,1)}, bf16[256,2048]{1,0:T(8,128)(2,1)}, u32[]{:S(2)}, u32[]{:S(2)}) collective-permute-start(bf16[256,2048]{1,0:T(8,128)(2,1)} %pad_maximum_fusion.4), channel_id=1, source_target_pairs={{0,1},{3,2},{4,5},{7,6},{8,9},{11,10},{12,13},{15,14},{16,17},{19,... | collective-permute-start | bytes 3145736 | tf_op jit(solution)/shard_map/ppermute | solution.py:233
  300.0 47.6 %collective-permute-start.65 = (bf16[256,2048]{1,0:T(8,128)(2,1)}, bf16[256,2048]{1,0:T(8,128)(2,1)}, u32[]{:S(2)}, u32[]{:S(2)}) collective-permute-start(bf16[256,2048]{1,0:T(8,128)(2,1)} %add_convert_fusion.2), channel_id=1, source_target_pairs={{1,2},{2,1},{5,6},{6,5},{9,10},{10,9},{13,14},{14,13},{17,18},{18,... | collective-permute-start | bytes 3145736 | tf_op jit(solution)/shard_map/ppermute | solution.py:233
  302.6 28.8 %collective-permute-start.48 = (bf16[256,1024]{1,0:T(8,128)(2,1)}, bf16[256,1024]{1,0:T(8,128)(2,1)}, u32[]{:S(2)}, u32[]{:S(2)}) collective-permute-start(bf16[256,1024]{1,0:T(8,128)(2,1)} %add_convert_fusion.5), channel_id=1, source_target_pairs={{0,16},{1,17},{2,18},{3,19},{4,20},{5,21},{6,22},{7,23},{8,24},{9,... | collective-permute-start | bytes 1572872 | tf_op jit(solution)/shard_map/ppermute | solution.py:233
  304.6 26.9 %collective-permute-start.49 = (bf16[256,1024]{1,0:T(8,128)(2,1)}, bf16[256,1024]{1,0:T(8,128)(2,1)}, u32[]{:S(2)}, u32[]{:S(2)}) collective-permute-start(bf16[256,1024]{1,0:T(8,128)(2,1)} %add_convert_fusion.4), channel_id=1, source_target_pairs={{0,8},{1,9},{2,10},{3,11},{4,12},{5,13},{6,14},{7,15},{8,0},{9,1},... | collective-permute-start | bytes 1572872 | tf_op jit(solution)/shard_map/ppermute | solution.py:233
  318.4 21.0 %collective-permute-start.44 = (bf16[256,1024]{1,0:T(8,128)(2,1)}, bf16[256,1024]{1,0:T(8,128)(2,1)}, u32[]{:S(2)}, u32[]{:S(2)}) collective-permute-start(bf16[256,1024]{1,0:T(8,128)(2,1)} %slice.662), channel_id=1, source_target_pairs={{0,1},{1,0},{2,3},{3,2},{4,5},{5,4},{6,7},{7,6},{8,9},{9,8},{10,11... | collective-permute-start | bytes 1572872 | tf_op jit(solution)/shard_map/ppermute | solution.py:233
  332.7 25.5 %collective-permute-start.50 = (bf16[512,1024]{1,0:T(8,128)(2,1)S(1)}, bf16[512,1024]{1,0:T(8,128)(2,1)S(1)}, u32[]{:S(2)}, u32[]{:S(2)}) collective-permute-start(bf16[512,1024]{1,0:T(8,128)(2,1)S(1)} %pad_maximum_fusion.6), channel_id=1, source_target_pairs={{0,4},{1,5},{2,6},{3,7},{4,0},{5,1},{6,2},{7,3},{8,12},{9,13},{10,... | collective-permute-start | bytes 3145736 | tf_op jit(solution)/shard_map/ppermute | solution.py:233
  354.4 21.2 %collective-permute-start.55 = (bf16[256,1024]{1,0:T(8,128)(2,1)}, bf16[256,1024]{1,0:T(8,128)(2,1)}, u32[]{:S(2)}, u32[]{:S(2)}) collective-permute-start(bf16[256,1024]{1,0:T(8,128)(2,1)} %pad_maximum_fusion.10), channel_id=1, source_target_pairs={{0,1},{3,2},{4,5},{7,6},{8,9},{11,10},{12,13},{15,14},{16,17},{19,... | collective-permute-start | bytes 1572872 | tf_op jit(solution)/shard_map/ppermute | solution.py:233
  388.7 47.7 %collective-permute-start.60 = (bf16[512,1024]{1,0:T(8,128)(2,1)}, bf16[512,1024]{1,0:T(8,128)(2,1)}, u32[]{:S(2)}, u32[]{:S(2)}) collective-permute-start(bf16[512,1024]{1,0:T(8,128)(2,1)} %fusion.4), channel_id=1, source_target_pairs={{2,4},{3,5},{4,2},{5,3},{10,12},{11,13},{12,10},{13,11},{18,20},{1... | collective-permute-start | bytes 3145736 | tf_op jit(solution)/shard_map/ppermute | solution.py:233
  403.1 21.6 %collective-permute-start.63 = (bf16[256,512]{1,0:T(8,128)(2,1)S(1)}, bf16[256,512]{1,0:T(8,128)(2,1)S(1)}, u32[]{:S(2)}, u32[]{:S(2)}) collective-permute-start(bf16[256,512]{1,0:T(8,128)(2,1)S(1)} %add_convert_fusion.10), channel_id=1, source_target_pairs={{0,1},{1,0},{2,3},{3,2},{4,5},{5,4},{6,7},{7,6},{8,9},{9,8},{10,11... | collective-permute-start | bytes 786440 | tf_op jit(solution)/shard_map/ppermute | solution.py:233
  438.6 34.6 %collective-permute-start.61 = (bf16[256,1024]{1,0:T(8,128)(2,1)}, bf16[256,1024]{1,0:T(8,128)(2,1)}, u32[]{:S(2)}, u32[]{:S(2)}) collective-permute-start(bf16[256,1024]{1,0:T(8,128)(2,1)} %slice.664), channel_id=1, source_target_pairs={{0,1},{1,0},{2,3},{3,2},{4,5},{5,4},{6,7},{7,6},{8,9},{9,8},{10,11... | collective-permute-start | bytes 1572872 | tf_op jit(solution)/shard_map/ppermute | solution.py:233
  (178 other events, 1912.8 us)

commit v3 on v2

--- a/solution.py
+++ b/solution.py
@@ -15,8 +15,8 @@
 weight_decay = 0.1
 masked_score = -1000000000.0
 score_scale = HD ** (-0.5)
-kernel_bytes = 16 << 20
-back_bytes = 24 << 20
+kernel_bytes = 12 << 20
+back_bytes = 16 << 20
 
 in_vmem = pl.BlockSpec(memory_space=pltpu.VMEM)
 in_smem = pl.BlockSpec(memory_space=pltpu.SMEM)
@@ -380,7 +380,7 @@
             order = order + [k | bit for k in order]
         return order
 
-    def sum_all(self, values, *others):
+    def sum_plane(self, values):
         values = values + self.to_core(values)
         for low in range(0, len(self.q_bits), 2):
             bits = self.q_bits[low : low + 2]
@@ -390,7 +390,9 @@
                 values = (values + got[0]) + (got[1] + both)
             else:
                 values = values + got[0]
-        values = after(values, *others)
+        return values
+
+    def sum_column(self, values):
         bit, bits = 1, []
         while bit < self.mp_n:
             bits.append(bit)
@@ -718,7 +720,10 @@
     return jnp.where(c == 0, mine, other), jnp.where(c == 0, other, mine)
 
 
-def adjust_into(index, weight, moments_ref, gradient, fixes_ref, state_ref, update_ref, sums_ref):
+def adjust_into(
+    index, weight, moments_ref, gradient, fixes_ref, state_ref, update_ref, own_ref, sums_ref
+):
+    own_ref[...] = weight
     first_new, second_new, update = adjust(
         weight, moments_ref[0], moments_ref[1], gradient, weight_decay, fixes_ref[0], fixes_ref[1]
     )
@@ -731,7 +736,7 @@
 
 def adjust_attn_kernel(
     place_ref, fixes_ref, mine_ref, other_ref, qkv_ref, out_ref, qkv_moments, out_moments,
-    qkv_state, out_state, qkv_update, out_update, sums_ref,
+    qkv_state, out_state, qkv_update, out_update, qkv_own, out_own, sums_ref,
 ):
     size = qkv_ref.shape[2] // 2
     one, two = in_order(place_ref[1], mine_ref[...], other_ref[...])
@@ -740,24 +745,29 @@
         for j in range(4)
     ]
     adjust_into(
-        0, qkv_ref[...], qkv_moments, jnp.stack(parts[:3]), fixes_ref, qkv_state, qkv_update, sums_ref
+        0, qkv_ref[...], qkv_moments, jnp.stack(parts[:3]), fixes_ref,
+        qkv_state, qkv_update, qkv_own, sums_ref,
     )
     adjust_into(
-        1, out_ref[...], out_moments, parts[3].T, fixes_ref, out_state, out_update, sums_ref
+        1, out_ref[...], out_moments, parts[3].T, fixes_ref,
+        out_state, out_update, out_own, sums_ref,
     )
 
 
 def adjust_mlp_kernel(
     place_ref, fixes_ref, mine_ref, other_ref, up_ref, down_ref, up_moments, down_moments,
-    up_state, down_state, up_update, down_update, sums_ref,
+    up_state, down_state, up_update, down_update, up_own, down_own, sums_ref,
 ):
     size = up_ref.shape[1] // 2
     one, two = in_order(place_ref[1], mine_ref[...], other_ref[...])
     down_grad = jnp.concatenate([one[:, :size], two[:, :size]], axis=1)
     up_grad = jnp.concatenate([one[:, size:], two[:, size:]], axis=1)
-    adjust_into(0, up_ref[...], up_moments, up_grad, fixes_ref, up_state, up_update, sums_ref)
     adjust_into(
-        1, down_ref[...], down_moments, down_grad.T, fixes_ref, down_state, down_update, sums_ref
+        0, up_ref[...], up_moments, up_grad, fixes_ref, up_state, up_update, up_own, sums_ref
+    )
+    adjust_into(
+        1, down_ref[...], down_moments, down_grad.T, fixes_ref,
+        down_state, down_update, down_own, sums_ref,
     )
 
 
@@ -776,7 +786,7 @@
 def adjust_pair(at, kernel, place, fixes, mine, other, weights, dims, moments):
     parts = [m.shape[1:] for m in moments]
     shapes = [jax.ShapeDtypeStruct(m.shape, f32) for m in moments]
-    shapes += [jax.ShapeDtypeStruct(p, f32) for p in parts]
+    shapes += [jax.ShapeDtypeStruct(p, f32) for p in parts] * 2
     return pl.pallas_call(
         kernel,
         grid_spec=pltpu.PrefetchScalarGridSpec(
@@ -793,7 +803,63 @@
     )(place, fixes, mine, other, *weights, *moments)
 
 
-def apply_kernel(place_ref, rates_ref, *refs):
+def adjust_small_kernel(
+    fixes_ref, vec_grad, vec_moments, vec, bias_grad, bias_moments, bias, rel_grad, rel_moments,
+    rel, vec_state, vec_new, weight_norms, update_norms, bias_state, bias_update, rel_state,
+    rel_update, sums_ref,
+):
+    fixes = (fixes_ref[0], fixes_ref[1])
+    first, second, update = adjust(
+        vec[...], vec_moments[0], vec_moments[1], vec_grad[...], 0.0, *fixes
+    )
+    vec_state[0] = first
+    vec_state[1] = second
+    weight_norm = jnp.sqrt(jnp.sum(vec[...] * vec[...], axis=1, keepdims=True))
+    update_norm = jnp.sqrt(jnp.sum(update * update, axis=1, keepdims=True))
+    weight_norms[...] = weight_norm
+    update_norms[...] = update_norm
+    vec_new[...] = vec[...] - learn_rate * (weight_norm / (update_norm + adam_eps)) * update
+    first, second, update = adjust(
+        bias[...], bias_moments[0:1, :], bias_moments[1:2, :], bias_grad[...], 0.0, *fixes
+    )
+    bias_state[0:1, :] = first
+    bias_state[1:2, :] = second
+    bias_update[...] = update
+    sums_ref[0] = jnp.sum(bias[...] * bias[...])
+    sums_ref[1] = jnp.sum(update * update)
+    first, second, update = adjust(
+        rel[...], rel_moments[0], rel_moments[1], rel_grad[...], 0.0, *fixes
+    )
+    rel_state[0] = first
+    rel_state[1] = second
+    rel_update[...] = update
+    sums_ref[2] = jnp.sum(rel[...] * rel[...])
+    sums_ref[3] = jnp.sum(update * update)
+
+
+def adjust_small(fixes, vec, bias, rel):
+    shape = jax.ShapeDtypeStruct
+    rows = vec[2].shape[0]
+    return pl.pallas_call(
+        adjust_small_kernel,
+        in_specs=[in_smem] + [in_vmem] * 9,
+        out_specs=(in_vmem,) * 8 + (in_smem,),
+        out_shape=(
+            shape(vec[1].shape, f32),
+            shape(vec[2].shape, f32),
+            shape((rows, 1), f32),
+            shape((rows, 1), f32),
+            shape(bias[1].shape, f32),
+            shape(bias[2].shape, f32),
+            shape(rel[1].shape, f32),
+            shape(rel[2].shape, f32),
+            shape((4,), f32),
+        ),
+        name="adjust_small",
+    )(fixes, *vec, *bias, *rel)
+
+
+def apply_kernel(rates_ref, *refs):
     count = len(refs) // 3
     for index in range(count):
         refs[2 * count + index][...] = (
@@ -801,21 +867,15 @@
         )
 
 
-def apply_updates(at, place, rates, weights, dims, updates):
+def apply_updates(rates, weights, updates):
     return pl.pallas_call(
         apply_kernel,
-        grid_spec=pltpu.PrefetchScalarGridSpec(
-            num_scalar_prefetch=1,
-            grid=(1,),
-            in_specs=[in_smem]
-            + [own_spec(w.shape, d, at.dp_n) for w, d in zip(weights, dims)]
-            + [whole_spec(u.shape) for u in updates],
-            out_specs=tuple(whole_spec(u.shape) for u in updates),
-        ),
+        in_specs=[in_smem] + [in_vmem] * (2 * len(updates)),
+        out_specs=(in_vmem,) * len(updates),
         out_shape=tuple(jax.ShapeDtypeStruct(u.shape, f32) for u in updates),
-        compiler_params=pltpu.CompilerParams(vmem_limit_bytes=back_bytes),
+        compiler_params=pltpu.CompilerParams(vmem_limit_bytes=kernel_bytes),
         name="apply_updates",
-    )(place, rates, *weights, *updates)
+    )(rates, *weights, *updates)
 
 
 def norm_parts(values):
@@ -1092,8 +1152,9 @@
     for r in reversed(range(blocks)):
         context_grad = context_grads[r]
         if r == 3:
-            up_far.rest(down_far.got)
-            down_far.rest(up_far.got)
+            there = (up_far.got, down_far.got)
+            up_far.rest(*there)
+            down_far.rest(*there)
         if r == 2:
             far_done = (up_far.got, down_far.got)
             context_grad = after(context_grad, *far_done)
@@ -1110,9 +1171,6 @@
             near_firsts = (down_near_sum.got, up_near_sum.got)
             context_grad = after(context_grad, *near_firsts, far_got)
             mlp_far = at.fold_add(mlp_far, after(far_got, *near_firsts))
-            inner_got = at.fold_inner(mlp_far)
-            out_pair = at.deliver_pair(out_share, after(out_got, far_got))
-            out_last = at.deliver_last(out_pair)
             down_near_sum.rest(*near_firsts)
             up_near_sum.rest(*near_firsts)
             near_done = (down_near_sum.got, up_near_sum.got)
@@ -1120,40 +1178,28 @@
             length, qkv[r], lines_of(r), totals[r], context_grad, heads
         )
         rel_grads[r] = dist
+        if r == 0:
+            proj_grad = after(proj_grad, *near_done)
         attn_halves[r] = grad_halves(
             at, [(first_low, [proj_grad]), (branch, [contexts[r]])], r % 2
         )
         proj_grads[r] = proj_grad
-    back_low = after(sum_nt(proj_grads, qkv_w), *near_done)
+    back_low = sum_nt(proj_grads, qkv_w)
+    inner_got = at.fold_inner(after(mlp_far, back_low))
+    out_pair = at.deliver_pair(out_share, after(out_got, far_got, back_low))
+    out_last = at.deliver_last(out_pair)
     for k in (3, 2):
         attn_sums[k] = ChipSum(at, [after(v, *near_done) for v in attn_halves[k]], k % 2)
     firsts = (attn_sums[3].got, attn_sums[2].got)
     first_grad = at.sum_share(back_low, length_rows)
-    for k in (1, 0):
-        attn_sums[k] = ChipSum(at, [after(v, *firsts) for v in attn_halves[k]], k % 2)
     for k in (3, 2):
         attn_sums[k].rest(*firsts)
-    first_grad = after(first_grad, *firsts)
     attn_far = jnp.concatenate([attn_sums[2].total(), attn_sums[3].total()], axis=1).astype(bf16)
-    attn_got = at.fold_outer(attn_far)
-    for k in (1, 0):
-        attn_sums[k].rest(attn_sums[2].got, attn_sums[3].got, attn_sums[0].got, attn_sums[1].got)
     mlp_size = 2 * units
     mlp_near = (down_near_sum.total(), up_near_sum.total())
     mlp_one = jnp.concatenate([v[:, far_cols] for v in mlp_near], axis=1)
     mlp_own = jnp.concatenate([v[:, own_cols] for v in mlp_near], axis=1)
     mlp_one = (mlp_one + inner_got[:, :mlp_size].astype(f32)).astype(bf16)
-    last_got = at.to_slot(mlp_one, 1)
-    mlp_mine = mlp_own + inner_got[:, mlp_size:].astype(f32) + last_got.astype(f32)
-    attn_got = after(attn_got, attn_sums[0].got, attn_sums[1].got)
-    attn_inner_got = at.fold_inner(at.fold_add(attn_far, attn_got))
-    attn_one_sum = attn_inner_got[:, :attn_cols].astype(f32) + attn_sums[1].total()
-    attn_last_got = at.to_slot(attn_one_sum.astype(bf16), 1)
-    attn_mine = (
-        attn_sums[0].total()
-        + attn_inner_got[:, attn_cols:].astype(f32)
-        + attn_last_got.astype(f32)
-    )
     rel_grad = lax.dot_general(
         jnp.concatenate(rel_grads, axis=0),
         choose,
@@ -1169,11 +1215,6 @@
         first_grad, normed_share, inverse_share, vectors[0]
     )
     input_low = input_share.astype(bf16)
-    input_got = at.deliver_first(after(input_low, attn_got))
-    input_pair = at.deliver_pair(input_low, input_got)
-    input_last = at.deliver_last(input_pair)
-    input_grad = at.relative(at.delivered(input_pair, input_last), 2).astype(f32)
-
     def by_place(rows_of):
         around = jnp.stack(rows_of)
         moved = []
@@ -1198,16 +1239,37 @@
             for r in range(blocks)
         ]
     )
-    joined = at.sum_all(
-        jnp.concatenate([at.relative(vector_grad, 1).reshape(-1), small_grad.reshape(-1)]),
-        attn_inner_got,
-        last_got,
-    )
+    last_got = at.to_slot(mlp_one, 1)
+    plane = at.sum_plane(
+        jnp.concatenate([at.relative(vector_grad, 1).reshape(-1), small_grad.reshape(-1)])
+    )
+    there = (attn_sums[3].got, attn_sums[2].got, plane)
+    for k in (1, 0):
+        attn_sums[k] = ChipSum(at, [after(v, *there) for v in attn_halves[k]], k % 2)
+    there = (attn_sums[1].got, attn_sums[0].got)
+    for k in (1, 0):
+        attn_sums[k].rest(*there)
+    joined = at.sum_column(after(plane, last_got))
+    input_got = at.deliver_first(after(input_low, joined))
+    attn_got = at.fold_outer(after(attn_far, joined))
+    mlp_mine = mlp_own + inner_got[:, mlp_size:].astype(f32) + last_got.astype(f32)
+    attn_got = after(attn_got, attn_sums[0].got, attn_sums[1].got, input_got)
+    attn_inner_got = at.fold_inner(at.fold_add(attn_far, attn_got))
+    attn_one_sum = attn_inner_got[:, :attn_cols].astype(f32) + attn_sums[1].total()
+    attn_last_got = at.to_slot(attn_one_sum.astype(bf16), 1)
+    attn_mine = (
+        attn_sums[0].total()
+        + attn_inner_got[:, attn_cols:].astype(f32)
+        + attn_last_got.astype(f32)
+    )
+    input_pair = at.deliver_pair(input_low, input_got)
+    input_last = at.deliver_last(input_pair)
+    input_grad = at.relative(at.delivered(input_pair, input_last), 2).astype(f32)
     vector_grad = joined[: vector_grad.size].reshape(vector_grad.shape)
     small_sum = lax.dynamic_index_in_dim(
         joined[vector_grad.size :].reshape(small_grad.shape), at.mp_i, 0, keepdims=False
     )
-    bias_sum = small_sum[:, :units].reshape(-1)
+    bias_sum = small_sum[:, :units].reshape(1, -1)
     rel_sum = small_sum[:, units:].reshape(2 * heads, bucket_count).T
 
     rows = part // 2
@@ -1222,15 +1284,7 @@
     steps_done = step_count[0].astype(f32)
     first_fix = 1.0 - jnp.power(jnp.float32(0.9), steps_done)
     second_fix = 1.0 - jnp.power(jnp.float32(0.999), steps_done)
-    vector_pieces = [
-        (up_bias, bias_moments, bias_sum),
-        (rel_bias, rel_moments, rel_sum),
-        (norm_vectors, vector_moments, vector_grad),
-    ]
-    vector_adjusted = [
-        adjust(weight, moments[0], moments[1], grad, 0.0, first_fix, second_fix)
-        for weight, moments, grad in vector_pieces
-    ]
+    fixes = jnp.stack([first_fix, second_fix])
     qkv_view = jnp.transpose(qkv_weight, (1, 0, 2))
     qkv_mom = jnp.transpose(qkv_moments, (0, 2, 1, 3))
     weights = [qkv_view, out_weight, up_weight, down_weight]
@@ -1238,18 +1292,18 @@
     in_kernels = rows % 128 == 0
     if in_kernels:
         place = jnp.stack([at.dp_i, c]).astype(jnp.int32)
-        fixes = jnp.stack([first_fix, second_fix])
-        up_state, down_state, up_update, down_update, mlp_squares = adjust_pair(
-            at, adjust_mlp_kernel, place, fixes, mlp_mine, mlp_other,
+        up_state, down_state, up_update, down_update, up_mine, down_mine, mlp_squares = adjust_pair(
+            at, adjust_mlp_kernel, place, after(fixes, attn_inner_got), mlp_mine, mlp_other,
             weights[2:], dims[2:], [up_moments, down_moments],
         )
-        qkv_state, out_state, qkv_update, out_update, attn_squares = adjust_pair(
+        qkv_state, out_state, qkv_update, out_update, qkv_mine, out_mine, attn_squares = adjust_pair(
             at, adjust_attn_kernel, place, fixes, attn_mine, attn_other,
             weights[:2], dims[:2], [qkv_mom, out_moments],
         )
         squares = jnp.concatenate([attn_squares, mlp_squares])
         updates = [qkv_update, out_update, up_update, down_update]
         states = [qkv_state, out_state, up_state, down_state]
+        own_weights = [qkv_mine, out_mine, up_mine, down_mine]
     else:
         one, two = in_order(c, attn_mine, attn_other)
         parts = [
@@ -1279,23 +1333,30 @@
             states.append(jnp.stack([first_new, second_new]))
             squares += [jnp.sum(weight * weight), jnp.sum(update * update)]
         squares = jnp.stack(squares)
+    (
+        vector_state, vector_new, vector_norms, vector_update_norms,
+        bias_state, bias_update, rel_state, rel_update, small_squares,
+    ) = adjust_small(
+        fixes,
+        (vector_grad, vector_moments, norm_vectors),
+        (bias_sum, bias_moments, up_bias[None, :]),
+        (rel_sum, rel_moments, rel_bias),
+    )
     lead_dp = (at.dp_i == 0).astype(f32)
-    small_squares = jnp.stack(
-        [
-            lead_dp * jnp.sum(values * values)
-            for values in (up_bias, vector_adjusted[0][2], rel_bias, vector_adjusted[1][2])
-        ]
-    )
-    squares = at.sum_all(jnp.concatenate([squares, small_squares])).reshape(6, 2)
-    vector_squares = jnp.stack(
-        [jnp.sum(v * v, axis=1) for v in (norm_vectors, vector_adjusted[2][2])], axis=1
-    )
-    norms = jnp.sqrt(jnp.concatenate([squares, vector_squares]))
+    squares = jnp.concatenate([squares, lead_dp * small_squares])
+    squares = after(at.sum_plane(squares), input_last)
+    squares = at.sum_column(squares).reshape(6, 2)
+    norms = jnp.sqrt(squares)
     rates = learn_rate * (norms[:, 0] / (norms[:, 1] + adam_eps))
+    small_weights = [up_bias[None, :], rel_bias]
+    small_updates = [bias_update, rel_update]
     if in_kernels:
-        new = apply_updates(at, place, rates[:4], weights, dims, updates)
+        *new, bias_new, rel_new = apply_updates(
+            rates, own_weights + small_weights, updates + small_updates
+        )
     else:
         new = [own_weights[k] - rates[k] * updates[k] for k in range(4)]
+        bias_new, rel_new = apply_updates(rates[4:], small_weights, small_updates)
     new, states = list(new), list(states)
     new[0] = jnp.transpose(new[0], (1, 0, 2))
     states[0] = jnp.transpose(states[0], (0, 2, 1, 3))
@@ -1303,14 +1364,12 @@
     results = [block_out, input_grad]
     for k in range(4):
         results += [new[k], states[k]]
-    for k in range(2):
-        first_new, second_new, update = vector_adjusted[k]
-        results.append(vector_pieces[k][0] - rates[4 + k] * update)
-        results.append(jnp.stack([first_new, second_new]))
-    first_new, second_new, update = vector_adjusted[2]
-    results.append(norm_vectors - rates[6:, None] * update)
-    results.append(jnp.stack([first_new, second_new]))
-    results.append(norms.T)
+    results += [bias_new[0], bias_state, rel_new, rel_state, vector_new, vector_state]
+    results.append(
+        jnp.concatenate(
+            [norms, jnp.concatenate([vector_norms, vector_update_norms], axis=1)]
+        ).T
+    )
     return tuple(results)
 
 

time: 486 us -> 461 us (0.949)
  starting transfers between devices: 127 us -> 111 us
  waiting for transfers between devices: 92.8 us -> 104 us
  other arithmetic: 67.5 us -> 56.7 us
  local copies, waits for them, and re-layouts: 58.1 us -> 51.1 us
    ppermute x82, starting transfers between devices: 127 us -> 111 us  [move(): return lax.ppermute(values, ('dp', 'mp'), pairs)]
    ppermute x82, waiting for transfers between devices: 92.8 us -> 104 us  [move(): return lax.ppermute(values, ('dp', 'mp'), pairs)]
    unnamed x252 -> x236, local copies, waits for them, and re-layouts: 24.7 us -> 21.3 us
  transfers between devices with their start and end apart: 82 -> 82, of which waited for: 27 -> 30; matrix products, arithmetic and copies ran while one was open for 20% -> 20% of each run, Pallas kernels for 22% -> 23%
where the time goes in v3:
time: 461 us; the launch traced here: 452 us
  Pallas kernels  116 us (25%)
  starting transfers between devices  111 us (24%)
  waiting for transfers between devices  104 us (23%)
  other arithmetic  56.7 us (12%)
  local copies, waits for them, and re-layouts  51.1 us (11%)
  matrix products  8.81 us (2%)
    ppermute x82, starting transfers between devices, move(): return lax.ppermute(values, ('dp', 'mp'), pairs)  111 us
    ppermute x82, waiting for transfers between devices, move(): return lax.ppermute(values, ('dp', 'mp'), pairs)  104 us
    pallas_call x4, Pallas kernels, attend_back(): pl.pallas_call(lambda *refs: attend_back_kernel(heads, *refs), out_shape=...  32.8 us
    unnamed x236, local copies, waits for them, and re-layouts  21.3 us
    pallas_call x8, Pallas kernels, grad_halves(): pl.pallas_call(lambda *refs: halves_kernel(order, [len(rights) for _, rig...  17.5 us
    pallas_call x4, Pallas kernels, sum_nt(): pl.pallas_call(lambda *refs: sum_nt_kernel(len(lefts), *refs), in_specs=[...  16.5 us
    pallas_call x4, Pallas kernels, attend(): pl.pallas_call(lambda *refs: attend_kernel(heads, *refs), out_shape=(jax....  15.9 us
  transfers between devices with their start and end apart: 82, of which 30 were waited for; matrix products, arithmetic and copies ran while one was open for 20% of the time, Pallas kernels for 23%

profile of v3, /device:TPU:1, one launch (start us, length us, event | category | flops | bytes accessed | tf_op | source)
XLA Modules:
  0.0 451.9 jit_solution(16189384532661024710)
XLA Ops:
  4.4 4.6 %pack_attn.1 = (bf16[1024,384]{1,0:T(8,128)(2,1)}, bf16[1024,128]{1,0:T(8,128)(2,1)}, bf16[256,512]{1,0:T(8,128)(2,1)}) custom-call(s32[2]{0:T(128)} %pad_add_fusion.1.place_ref, f32[3,1024,256]{2,1,0:T(8,128)} %bitcast.89, f32[256,1024]{1,0:T(8,128)} %out_ref.3), custom_call_target="tpu_custom_call" | custom-call | tf_op jit(solution)/shard_map/pack_attn/pallas_call | solution.py:481
  12.5 5.6 %collective-permute-start.1 = (bf16[256,1024]{1,0:T(8,128)(2,1)S(1)}, bf16[256,1024]{1,0:T(8,128)(2,1)}, u32[]{:S(2)}, u32[]{:S(2)}) collective-permute-start(bf16[256,1024]{1,0:T(8,128)(2,1)S(1)} %get-tuple-element.434), channel_id=1, source_target_pairs={{2,0},{3,1},{4,6},{5,7},{10,8},{11,9},{12,14},{13,15},{18,16},{19,... | collective-permute-start | bytes 1572872 | tf_op jit(solution)/shard_map/ppermute | solution.py:233
  21.3 5.3 %pack_mlp.1 = (bf16[1024,512]{1,0:T(8,128)(2,1)}, bf16[1024,512]{1,0:T(8,128)(2,1)}, bf16[256,512]{1,0:T(8,128)(2,1)}, bf16[256,512]{1,0:T(8,128)(2,1)}) custom-call(s32[2]{0:T(128)} %pad_add_fusion.1.place_ref, f32[1024,1024]{1,0:T(8,128)} %up_ref.3, f32[1024,1024]{1,0:T(8,128)} %down_ref.3), custom_call_target="tpu_custom_call" | custom-call | tf_op jit(solution)/shard_map/pack_mlp/pallas_call | solution.py:509
  47.6 6.7 %collective-permute-done.10 = bf16[256,1024]{1,0:T(8,128)(2,1)} collective-permute-done((bf16[256,1024]{1,0:T(8,128)(2,1)}, bf16[256,1024]{1,0:T(8,128)(2,1)}, u32[]{:S(2)}, u32[]{:S(2)}) %collective-permute-start.10) | collective-permute-done | bytes 524320 | tf_op jit(solution)/shard_map/ppermute | solution.py:233
  62.1 6.5 %collective-permute-done.12 = bf16[256,1024]{1,0:T(8,128)(2,1)S(1)} collective-permute-done((bf16[256,1024]{1,0:T(8,128)(2,1)}, bf16[256,1024]{1,0:T(8,128)(2,1)S(1)}, u32[]{:S(2)}, u32[]{:S(2)}) %collective-permute-start.12) | collective-permute-done | bytes 524320 | tf_op jit(solution)/shard_map/ppermute | solution.py:233
  73.7 4.6 %collective-permute-done.11 = bf16[272,1024]{1,0:T(8,128)(2,1)S(1)} collective-permute-done((bf16[272,1024]{1,0:T(8,128)(2,1)S(1)}, bf16[272,1024]{1,0:T(8,128)(2,1)S(1)}, u32[]{:S(2)}, u32[]{:S(2)}) %collective-permute-start.11) | collective-permute-done | bytes 557088 | tf_op jit(solution)/shard_map/ppermute | solution.py:233
  80.4 10.3 %collective-permute-done.17 = bf16[256,1024]{1,0:T(8,128)(2,1)} collective-permute-done((bf16[256,1024]{1,0:T(8,128)(2,1)}, bf16[256,1024]{1,0:T(8,128)(2,1)}, u32[]{:S(2)}, u32[]{:S(2)}) %collective-permute-start.17) | collective-permute-done | bytes 524320 | tf_op jit(solution)/shard_map/ppermute | solution.py:233
  109.4 5.0 %collective-permute-done.15 = bf16[256,1024]{1,0:T(8,128)(2,1)S(1)} collective-permute-done((bf16[256,1024]{1,0:T(8,128)(2,1)S(1)}, bf16[256,1024]{1,0:T(8,128)(2,1)S(1)}, u32[]{:S(2)}, u32[]{:S(2)}) %collective-permute-start.15) | collective-permute-done | bytes 524320 | tf_op jit(solution)/shard_map/ppermute | solution.py:233
  118.1 7.0 %collective-permute-start.28 = (bf16[256,1024]{1,0:T(8,128)(2,1)S(1)}, bf16[256,1024]{1,0:T(8,128)(2,1)S(1)}, u32[]{:S(2)}, u32[]{:S(2)}) collective-permute-start(bf16[256,1024]{1,0:T(8,128)(2,1)S(1)} %get-tuple-element.428), channel_id=1, source_target_pairs={{2,0},{3,1},{4,6},{5,7},{10,8},{11,9},{12,14},{13,15},{18,16},{19,... | collective-permute-start | bytes 1572872 | tf_op jit(solution)/shard_map/ppermute | solution.py:233
  141.2 6.5 %collective-permute-done.24 = bf16[256,1024]{1,0:T(8,128)(2,1)S(1)} collective-permute-done((bf16[256,1024]{1,0:T(8,128)(2,1)S(1)}, bf16[256,1024]{1,0:T(8,128)(2,1)S(1)}, u32[]{:S(2)}, u32[]{:S(2)}) %collective-permute-start.24) | collective-permute-done | bytes 524320 | tf_op jit(solution)/shard_map/ppermute | solution.py:233
  163.7 5.5 %collective-permute-start.29 = (bf16[256,1024]{1,0:T(8,128)(2,1)S(1)}, bf16[256,1024]{1,0:T(8,128)(2,1)S(1)}, u32[]{:S(2)}, u32[]{:S(2)}) collective-permute-start(bf16[256,1024]{1,0:T(8,128)(2,1)S(1)} %get-tuple-element.427), channel_id=1, source_target_pairs={{2,1},{3,0},{4,7},{5,6},{10,9},{11,8},{12,15},{13,14},{18,17},{19,... | collective-permute-start | bytes 1572872 | tf_op jit(solution)/shard_map/ppermute | solution.py:233
  169.2 6.6 %collective-permute-done.33.refs_7_ = bf16[256,512]{1,0:T(8,128)(2,1)S(1)} collective-permute-done((bf16[256,512]{1,0:T(8,128)(2,1)S(1)}, bf16[256,512]{1,0:T(8,128)(2,1)S(1)}, u32[]{:S(2)}, u32[]{:S(2)}) %collective-permute-start.33) | collective-permute-done | bytes 262176 | tf_op jit(solution)/shard_map/ppermute | solution.py:233
  212.5 5.0 %sum_nt.6 = bf16[1024,1024]{1,0:T(8,128)(2,1)S(1)} custom-call(bf16[1024,512]{1,0:T(8,128)(2,1)S(1)} %get-tuple-element.232.refs_0_.refs_1_, bf16[1024,512]{1,0:T(8,128)(2,1)S(1)} %get-tuple-element.234.refs_1_.refs_2_, bf16[1024,1024]{1,0:T(8,128)(2,1)S(1)} %get-tuple-element.217.refs_1_.refs_2_, bf16[1024,512]{1,0:T(8,128)(2,1)S(1)} %copy-done.7, ...), custom_call_target="tpu_custom_call" | custom-call | flops 2147483648 | bytes 1048576 | tf_op jit(solution)/shard_map/sum_nt/pallas_call | solution.py:589
  229.6 4.7 %collective-permute-start.38 = (bf16[512,1024]{1,0:T(8,128)(2,1)S(1)}, bf16[512,1024]{1,0:T(8,128)(2,1)S(1)}, u32[]{:S(2)}, u32[]{:S(2)}) collective-permute-start(bf16[512,1024]{1,0:T(8,128)(2,1)S(1)} %fusion.3), channel_id=1, source_target_pairs={{2,4},{3,5},{4,2},{5,3},{10,12},{11,13},{12,10},{13,11},{18,20},{1... | collective-permute-start | bytes 3145736 | tf_op jit(solution)/shard_map/ppermute | solution.py:233
  250.5 7.7 %collective-permute-done.38 = bf16[512,1024]{1,0:T(8,128)(2,1)S(1)} collective-permute-done((bf16[512,1024]{1,0:T(8,128)(2,1)S(1)}, bf16[512,1024]{1,0:T(8,128)(2,1)S(1)}, u32[]{:S(2)}, u32[]{:S(2)}) %collective-permute-start.38) | collective-permute-done | bytes 1048608 | tf_op jit(solution)/shard_map/ppermute | solution.py:233
  258.1 8.1 %attend_back.5 = (bf16[1024,384]{1,0:T(8,128)(2,1)S(1)}, f32[2,2048]{1,0:T(2,128)S(1)}) custom-call(s32[1]{0:T(128)} %dynamic_slice.186.refs_0_, bf16[1024,384]{1,0:T(8,128)(2,1)S(1)} %convolution_convert_fusion.2.refs_1_, f32[2,2048]{1,0:T(2,128)S(1)} %fusion.21.refs_2_, f32[2,1024]{1,0:T(2,128)S(1)} %get-tuple-element.252.refs_3_, ...), custom_call_target="tpu_custom_call" | custom-call | flops 2684354560 | bytes 1048576 | tf_op jit(solution)/shard_map/attend_back/pallas_call | solution.py:165
  268.9 8.3 %attend_back.6 = (bf16[1024,384]{1,0:T(8,128)(2,1)S(1)}, f32[2,2048]{1,0:T(2,128)S(1)}) custom-call(s32[1]{0:T(128)} %dynamic_slice.186.refs_0_, bf16[1024,384]{1,0:T(8,128)(2,1)S(1)} %convolution_convert_fusion.1.refs_1_, f32[2,2048]{1,0:T(2,128)S(1)} %fusion.20.refs_2_, f32[2,1024]{1,0:T(2,128)S(1)} %get-tuple-element.255.refs_3_, ...), custom_call_target="tpu_custom_call" | custom-call | flops 2684354560 | bytes 1048576 | tf_op jit(solution)/shard_map/attend_back/pallas_call | solution.py:165
  280.7 8.4 %attend_back.7 = (bf16[1024,384]{1,0:T(8,128)(2,1)S(1)}, f32[2,2048]{1,0:T(2,128)S(1)}) custom-call(s32[1]{0:T(128)} %dynamic_slice.186.refs_0_, bf16[1024,384]{1,0:T(8,128)(2,1)S(1)} %convolution_convert_fusion.refs_1_, f32[2,2048]{1,0:T(2,128)S(1)} %fusion.19.refs_2_, f32[2,1024]{1,0:T(2,128)S(1)} %get-tuple-element.258.refs_3_, ...), custom_call_target="tpu_custom_call" | custom-call | flops 2684354560 | bytes 1048576 | tf_op jit(solution)/shard_map/attend_back/pallas_call | solution.py:165
  298.2 8.0 %attend_back.4 = (bf16[1024,384]{1,0:T(8,128)(2,1)S(1)}, f32[2,2048]{1,0:T(2,128)S(1)}) custom-call(s32[1]{0:T(128)} %dynamic_slice.186.refs_0_, bf16[1024,384]{1,0:T(8,128)(2,1)S(1)} %convolution_convert_fusion.3.refs_1_, f32[2,2048]{1,0:T(2,128)S(1)} %fusion.22.refs_2_, f32[2,1024]{1,0:T(2,128)S(1)} %get-tuple-element.229.refs_3_, ...), custom_call_target="tpu_custom_call" | custom-call | flops 2684354560 | bytes 1048576 | tf_op jit(solution)/shard_map/attend_back/pallas_call | solution.py:165
  314.8 4.7 %sum_nt.7 = bf16[1024,1024]{1,0:T(8,128)(2,1)S(1)} custom-call(bf16[1024,384]{1,0:T(8,128)(2,1)S(1)} %copy-done.11, bf16[1024,384]{1,0:T(8,128)(2,1)S(1)} %get-tuple-element.254.refs_1_, bf16[1024,384]{1,0:T(8,128)(2,1)S(1)} %copy-done.9, bf16[1024,384]{1,0:T(8,128)(2,1)S(1)} %copy-done.13, bf16[1024,384]{1,0:T(8,128)(2,1)S(1)} %copy-done.23, ...), custom_call_target="tpu_custom_call" | custom-call | flops 1610612736 | bytes 1048576 | tf_op jit(solution)/shard_map/sum_nt/pallas_call | solution.py:589
  344.2 4.5 %collective-permute-start.56 = (bf16[256,1024]{1,0:T(8,128)(2,1)S(1)}, bf16[256,1024]{1,0:T(8,128)(2,1)S(1)}, u32[]{:S(2)}, u32[]{:S(2)}) collective-permute-start(bf16[256,1024]{1,0:T(8,128)(2,1)S(1)} %fusion.8), channel_id=1, source_target_pairs={{0,1},{1,0},{2,3},{3,2},{4,5},{5,4},{6,7},{7,6},{8,9},{9,8},{10,11... | collective-permute-start | bytes 1572872 | tf_op jit(solution)/shard_map/ppermute | solution.py:233
  353.9 6.1 %collective-permute-done.56 = bf16[256,1024]{1,0:T(8,128)(2,1)S(1)} collective-permute-done((bf16[256,1024]{1,0:T(8,128)(2,1)S(1)}, bf16[256,1024]{1,0:T(8,128)(2,1)S(1)}, u32[]{:S(2)}, u32[]{:S(2)}) %collective-permute-start.56) | collective-permute-done | bytes 524320 | tf_op jit(solution)/shard_map/ppermute | solution.py:233
  368.2 6.0 %collective-permute-start.60 = (bf16[512,1024]{1,0:T(8,128)(2,1)}, bf16[512,1024]{1,0:T(8,128)(2,1)S(1)}, u32[]{:S(2)}, u32[]{:S(2)}) collective-permute-start(bf16[512,1024]{1,0:T(8,128)(2,1)} %fusion.4), channel_id=1, source_target_pairs={{2,4},{3,5},{4,2},{5,3},{10,12},{11,13},{12,10},{13,11},{18,20},{1... | collective-permute-start | bytes 3145736 | tf_op jit(solution)/shard_map/ppermute | solution.py:233
  387.9 9.6 %collective-permute-done.69 = bf16[256,1024]{1,0:T(8,128)(2,1)} collective-permute-done((bf16[256,1024]{1,0:T(8,128)(2,1)}, bf16[256,1024]{1,0:T(8,128)(2,1)}, u32[]{:S(2)}, u32[]{:S(2)}) %collective-permute-start.69) | collective-permute-done | bytes 524320 | tf_op jit(solution)/shard_map/ppermute | solution.py:233
  (618 shorter events, 292.3 us)
Async XLA Ops:
  2.3 35.8 %collective-permute-start = (bf16[256,1024]{1,0:T(8,128)(2,1)S(1)}, bf16[256,1024]{1,0:T(8,128)(2,1)}, u32[]{:S(2)}, u32[]{:S(2)}) collective-permute-start(bf16[256,1024]{1,0:T(8,128)(2,1)S(1)} %get-tuple-element.435), channel_id=1, source_target_pairs={{0,1},{1,0},{6,7},{7,6},{8,9},{9,8},{14,15},{15,14},{16,17},{17,16... | collective-permute-start | bytes 1572872 | tf_op jit(solution)/shard_map/ppermute | solution.py:233
  10.3 27.8 %collective-permute-start.2 = (bf16[272,512]{1,0:T(8,128)(2,1)S(1)}, bf16[272,512]{1,0:T(8,128)(2,1)S(1)}, u32[]{:S(2)}, u32[]{:S(2)}) collective-permute-start(bf16[272,512]{1,0:T(8,128)(2,1)S(1)} %constant_dynamic-update-slice_fusion), channel_id=1, source_target_pairs={{0,1},{1,0},{2,3},{3,2},{4,5},{5,4},{6,7},{7,6},{8,9},{9,8},{10,11... | collective-permute-start | bytes 835592 | tf_op jit(solution)/shard_map/ppermute | solution.py:233
  12.5 28.2 %collective-permute-start.1 = (bf16[256,1024]{1,0:T(8,128)(2,1)S(1)}, bf16[256,1024]{1,0:T(8,128)(2,1)}, u32[]{:S(2)}, u32[]{:S(2)}) collective-permute-start(bf16[256,1024]{1,0:T(8,128)(2,1)S(1)} %get-tuple-element.434), channel_id=1, source_target_pairs={{2,0},{3,1},{4,6},{5,7},{10,8},{11,9},{12,14},{13,15},{18,16},{19,... | collective-permute-start | bytes 1572872 | tf_op jit(solution)/shard_map/ppermute | solution.py:233
  18.2 23.4 %collective-permute-start.3 = (bf16[256,1024]{1,0:T(8,128)(2,1)S(1)}, bf16[256,1024]{1,0:T(8,128)(2,1)}, u32[]{:S(2)}, u32[]{:S(2)}) collective-permute-start(bf16[256,1024]{1,0:T(8,128)(2,1)S(1)} %get-tuple-element.433), channel_id=1, source_target_pairs={{2,1},{3,0},{4,7},{5,6},{10,9},{11,8},{12,15},{13,14},{18,17},{19,... | collective-permute-start | bytes 1572872 | tf_op jit(solution)/shard_map/ppermute | solution.py:233
  59.3 32.7 %collective-permute-start.4 = (bf16[1024,1024]{1,0:T(8,128)(2,1)}, bf16[1024,1024]{1,0:T(8,128)(2,1)}, u32[]{:S(2)}, u32[]{:S(2)}) collective-permute-start(bf16[1024,1024]{1,0:T(8,128)(2,1)} %constant_dynamic-update-slice_fusion.12), channel_id=1, source_target_pairs={{0,4},{1,5},{6,2},{7,3},{8,12},{9,13},{14,10},{15,11},{16,20},{17,... | collective-permute-start | bytes 6291464 | tf_op jit(solution)/shard_map/ppermute | solution.py:233
  71.1 19.7 %collective-permute-start.17 = (bf16[256,1024]{1,0:T(8,128)(2,1)}, bf16[256,1024]{1,0:T(8,128)(2,1)}, u32[]{:S(2)}, u32[]{:S(2)}) collective-permute-start(bf16[256,1024]{1,0:T(8,128)(2,1)} %collective-permute-done.14), channel_id=1, source_target_pairs={{1,0},{2,3},{5,4},{6,7},{9,8},{10,11},{13,12},{14,15},{17,16},{18,... | collective-permute-start | bytes 1572872 | tf_op jit(solution)/shard_map/ppermute | solution.py:233
  118.1 39.2 %collective-permute-start.28 = (bf16[256,1024]{1,0:T(8,128)(2,1)S(1)}, bf16[256,1024]{1,0:T(8,128)(2,1)S(1)}, u32[]{:S(2)}, u32[]{:S(2)}) collective-permute-start(bf16[256,1024]{1,0:T(8,128)(2,1)S(1)} %get-tuple-element.428), channel_id=1, source_target_pairs={{2,0},{3,1},{4,6},{5,7},{10,8},{11,9},{12,14},{13,15},{18,16},{19,... | collective-permute-start | bytes 1572872 | tf_op jit(solution)/shard_map/ppermute | solution.py:233
  136.5 22.4 %collective-permute-start.27 = (bf16[256,1024]{1,0:T(8,128)(2,1)S(1)}, bf16[256,1024]{1,0:T(8,128)(2,1)S(1)}, u32[]{:S(2)}, u32[]{:S(2)}) collective-permute-start(bf16[256,1024]{1,0:T(8,128)(2,1)S(1)} %dynamic-slice_bitcast_fusion.2), channel_id=1, source_target_pairs={{0,1},{1,0},{6,7},{7,6},{8,9},{9,8},{14,15},{15,14},{16,17},{17,16... | collective-permute-start | bytes 1572872 | tf_op jit(solution)/shard_map/ppermute | solution.py:233
  154.0 29.8 %collective-permute-start.26 = (bf16[1024,1024]{1,0:T(8,128)(2,1)S(1)}, bf16[1024,1024]{1,0:T(8,128)(2,1)S(1)}, u32[]{:S(2)}, u32[]{:S(2)}) collective-permute-start(bf16[1024,1024]{1,0:T(8,128)(2,1)S(1)} %sum_nt.4), channel_id=1, source_target_pairs={{0,4},{1,5},{2,6},{3,7},{4,0},{5,1},{6,2},{7,3},{8,12},{9,13},{10,... | collective-permute-start | bytes 6291464 | tf_op jit(solution)/shard_map/ppermute | solution.py:233
  156.2 19.7 %collective-permute-start.34 = (bf16[256,1024]{1,0:T(8,128)(2,1)S(1)}, bf16[256,1024]{1,0:T(8,128)(2,1)S(1)}, u32[]{:S(2)}, u32[]{:S(2)}) collective-permute-start(bf16[256,1024]{1,0:T(8,128)(2,1)S(1)} %maximum_select_fusion.2), channel_id=1, source_target_pairs={{0,16},{1,17},{2,18},{3,19},{4,20},{5,21},{6,22},{7,23},{8,24},{9,... | collective-permute-start | bytes 1572872 | tf_op jit(solution)/shard_map/ppermute | solution.py:233
  157.3 20.2 %collective-permute-start.31 = (bf16[256,1024]{1,0:T(8,128)(2,1)S(1)}, bf16[256,1024]{1,0:T(8,128)(2,1)S(1)}, u32[]{:S(2)}, u32[]{:S(2)}) collective-permute-start(bf16[256,1024]{1,0:T(8,128)(2,1)S(1)} %maximum_select_fusion.2), channel_id=1, source_target_pairs={{0,8},{1,9},{2,10},{3,11},{4,12},{5,13},{6,14},{7,15},{8,0},{9,1},... | collective-permute-start | bytes 1572872 | tf_op jit(solution)/shard_map/ppermute | solution.py:233
  198.2 26.4 %collective-permute-start.40 = (bf16[512,1024]{1,0:T(8,128)(2,1)S(1)}, bf16[512,1024]{1,0:T(8,128)(2,1)S(1)}, u32[]{:S(2)}, u32[]{:S(2)}) collective-permute-start(bf16[512,1024]{1,0:T(8,128)(2,1)S(1)} %get-tuple-element.219), channel_id=1, source_target_pairs={{0,16},{1,17},{2,18},{3,19},{4,20},{5,21},{6,22},{7,23},{8,24},{9,... | collective-permute-start | bytes 3145736 | tf_op jit(solution)/shard_map/ppermute | solution.py:233
  201.2 23.4 %collective-permute-start.39 = (bf16[512,1024]{1,0:T(8,128)(2,1)S(1)}, bf16[512,1024]{1,0:T(8,128)(2,1)S(1)}, u32[]{:S(2)}, u32[]{:S(2)}) collective-permute-start(bf16[512,1024]{1,0:T(8,128)(2,1)S(1)} %get-tuple-element.223), channel_id=1, source_target_pairs={{0,8},{1,9},{2,10},{3,11},{4,12},{5,13},{6,14},{7,15},{8,0},{9,1},... | collective-permute-start | bytes 3145736 | tf_op jit(solution)/shard_map/ppermute | solution.py:233
  217.5 24.0 %collective-permute-start.44 = (bf16[1024,1024]{1,0:T(8,128)(2,1)S(1)}, bf16[1024,1024]{1,0:T(8,128)(2,1)S(1)}, u32[]{:S(2)}, u32[]{:S(2)}) collective-permute-start(bf16[1024,1024]{1,0:T(8,128)(2,1)S(1)} %sum_nt.6), channel_id=1, source_target_pairs={{0,4},{1,5},{2,6},{3,7},{4,0},{5,1},{6,2},{7,3},{8,12},{9,13},{10,... | collective-permute-start | bytes 6291464 | tf_op jit(solution)/shard_map/ppermute | solution.py:233
  229.6 28.5 %collective-permute-start.38 = (bf16[512,1024]{1,0:T(8,128)(2,1)S(1)}, bf16[512,1024]{1,0:T(8,128)(2,1)S(1)}, u32[]{:S(2)}, u32[]{:S(2)}) collective-permute-start(bf16[512,1024]{1,0:T(8,128)(2,1)S(1)} %fusion.3), channel_id=1, source_target_pairs={{2,4},{3,5},{4,2},{5,3},{10,12},{11,13},{12,10},{13,11},{18,20},{1... | collective-permute-start | bytes 3145736 | tf_op jit(solution)/shard_map/ppermute | solution.py:233
  237.2 57.3 %collective-permute-start.46 = (bf16[512,1024]{1,0:T(8,128)(2,1)S(1)}, bf16[512,1024]{1,0:T(8,128)(2,1)S(1)}, u32[]{:S(2)}, u32[]{:S(2)}) collective-permute-start(bf16[512,1024]{1,0:T(8,128)(2,1)S(1)} %get-tuple-element.243), channel_id=1, source_target_pairs={{0,16},{1,17},{2,18},{3,19},{4,20},{5,21},{6,22},{7,23},{8,24},{9,... | collective-permute-start | bytes 3145736 | tf_op jit(solution)/shard_map/ppermute | solution.py:233
  237.5 57.1 %collective-permute-start.45 = (bf16[512,1024]{1,0:T(8,128)(2,1)S(1)}, bf16[512,1024]{1,0:T(8,128)(2,1)S(1)}, u32[]{:S(2)}, u32[]{:S(2)}) collective-permute-start(bf16[512,1024]{1,0:T(8,128)(2,1)S(1)} %get-tuple-element.242), channel_id=1, source_target_pairs={{0,8},{1,9},{2,10},{3,11},{4,12},{5,13},{6,14},{7,15},{8,0},{9,1},... | collective-permute-start | bytes 3145736 | tf_op jit(solution)/shard_map/ppermute | solution.py:233
  239.6 58.6 %collective-permute-start.43 = (bf16[256,2048]{1,0:T(8,128)(2,1)}, bf16[256,2048]{1,0:T(8,128)(2,1)S(1)}, u32[]{:S(2)}, u32[]{:S(2)}) collective-permute-start(bf16[256,2048]{1,0:T(8,128)(2,1)} %pad_maximum_fusion.4), channel_id=1, source_target_pairs={{0,1},{3,2},{4,5},{7,6},{8,9},{11,10},{12,13},{15,14},{16,17},{19,... | collective-permute-start | bytes 3145736 | tf_op jit(solution)/shard_map/ppermute | solution.py:233
  319.9 19.8 %collective-permute-start.50 = (bf16[512,1024]{1,0:T(8,128)(2,1)S(1)}, bf16[512,1024]{1,0:T(8,128)(2,1)S(1)}, u32[]{:S(2)}, u32[]{:S(2)}) collective-permute-start(bf16[512,1024]{1,0:T(8,128)(2,1)S(1)} %pad_maximum_fusion.7), channel_id=1, source_target_pairs={{0,4},{1,5},{2,6},{3,7},{4,0},{5,1},{6,2},{7,3},{8,12},{9,13},{10,... | collective-permute-start | bytes 3145736 | tf_op jit(solution)/shard_map/ppermute | solution.py:233
  319.9 22.9 %collective-permute-start.55 = (bf16[256,2048]{1,0:T(8,128)(2,1)}, bf16[256,2048]{1,0:T(8,128)(2,1)}, u32[]{:S(2)}, u32[]{:S(2)}) collective-permute-start(bf16[256,2048]{1,0:T(8,128)(2,1)} %add_convert_fusion.2), channel_id=1, source_target_pairs={{1,2},{2,1},{5,6},{6,5},{9,10},{10,9},{13,14},{14,13},{17,18},{18,... | collective-permute-start | bytes 3145736 | tf_op jit(solution)/shard_map/ppermute | solution.py:233
  368.2 29.9 %collective-permute-start.60 = (bf16[512,1024]{1,0:T(8,128)(2,1)}, bf16[512,1024]{1,0:T(8,128)(2,1)S(1)}, u32[]{:S(2)}, u32[]{:S(2)}) collective-permute-start(bf16[512,1024]{1,0:T(8,128)(2,1)} %fusion.4), channel_id=1, source_target_pairs={{2,4},{3,5},{4,2},{5,3},{10,12},{11,13},{12,10},{13,11},{18,20},{1... | collective-permute-start | bytes 3145736 | tf_op jit(solution)/shard_map/ppermute | solution.py:233
  375.1 22.4 %collective-permute-start.69 = (bf16[256,1024]{1,0:T(8,128)(2,1)}, bf16[256,1024]{1,0:T(8,128)(2,1)}, u32[]{:S(2)}, u32[]{:S(2)}) collective-permute-start(bf16[256,1024]{1,0:T(8,128)(2,1)} %pad_maximum_fusion.11), channel_id=1, source_target_pairs={{0,1},{3,2},{4,5},{7,6},{8,9},{11,10},{12,13},{15,14},{16,17},{19,... | collective-permute-start | bytes 1572872 | tf_op jit(solution)/shard_map/ppermute | solution.py:233
  384.0 32.9 %collective-permute-start.74 = (f32[128,1024]{1,0:T(8,128)}, f32[128,1024]{1,0:T(8,128)}, u32[]{:S(2)}, u32[]{:S(2)}) collective-permute-start(f32[128,1024]{1,0:T(8,128)} %get-tuple-element.411), channel_id=1, source_target_pairs={{0,4},{1,5},{2,6},{3,7},{4,0},{5,1},{6,2},{7,3},{8,12},{9,13},{10,... | collective-permute-start | bytes 1572872 | tf_op jit(solution)/shard_map/ppermute | solution.py:233
  403.8 21.5 %collective-permute-start.61 = (bf16[256,1024]{1,0:T(8,128)(2,1)}, bf16[256,1024]{1,0:T(8,128)(2,1)}, u32[]{:S(2)}, u32[]{:S(2)}) collective-permute-start(bf16[256,1024]{1,0:T(8,128)(2,1)} %slice.617), channel_id=1, source_target_pairs={{0,1},{1,0},{2,3},{3,2},{4,5},{5,4},{6,7},{7,6},{8,9},{9,8},{10,11... | collective-permute-start | bytes 1572872 | tf_op jit(solution)/shard_map/ppermute | solution.py:233
  (168 other events, 1763.1 us)

commit v4 on v3

--- a/solution.py
+++ b/solution.py
@@ -1254,24 +1254,6 @@
     attn_got = at.fold_outer(after(attn_far, joined))
     mlp_mine = mlp_own + inner_got[:, mlp_size:].astype(f32) + last_got.astype(f32)
     attn_got = after(attn_got, attn_sums[0].got, attn_sums[1].got, input_got)
-    attn_inner_got = at.fold_inner(at.fold_add(attn_far, attn_got))
-    attn_one_sum = attn_inner_got[:, :attn_cols].astype(f32) + attn_sums[1].total()
-    attn_last_got = at.to_slot(attn_one_sum.astype(bf16), 1)
-    attn_mine = (
-        attn_sums[0].total()
-        + attn_inner_got[:, attn_cols:].astype(f32)
-        + attn_last_got.astype(f32)
-    )
-    input_pair = at.deliver_pair(input_low, input_got)
-    input_last = at.deliver_last(input_pair)
-    input_grad = at.relative(at.delivered(input_pair, input_last), 2).astype(f32)
-    vector_grad = joined[: vector_grad.size].reshape(vector_grad.shape)
-    small_sum = lax.dynamic_index_in_dim(
-        joined[vector_grad.size :].reshape(small_grad.shape), at.mp_i, 0, keepdims=False
-    )
-    bias_sum = small_sum[:, :units].reshape(1, -1)
-    rel_sum = small_sum[:, units:].reshape(2 * heads, bucket_count).T
-
     rows = part // 2
 
     def exchanged(mine):
@@ -1279,8 +1261,6 @@
         return lax.dynamic_slice_in_dim(mine, c * rows, rows, 0), at.to_core(sent)
 
     mlp_mine, mlp_other = exchanged(mlp_mine)
-    attn_mine, attn_other = exchanged(attn_mine)
-
     steps_done = step_count[0].astype(f32)
     first_fix = 1.0 - jnp.power(jnp.float32(0.9), steps_done)
     second_fix = 1.0 - jnp.power(jnp.float32(0.999), steps_done)
@@ -1293,9 +1273,31 @@
     if in_kernels:
         place = jnp.stack([at.dp_i, c]).astype(jnp.int32)
         up_state, down_state, up_update, down_update, up_mine, down_mine, mlp_squares = adjust_pair(
-            at, adjust_mlp_kernel, place, after(fixes, attn_inner_got), mlp_mine, mlp_other,
+            at, adjust_mlp_kernel, place, fixes, mlp_mine, mlp_other,
             weights[2:], dims[2:], [up_moments, down_moments],
         )
+        attn_got = after(attn_got, mlp_squares)
+    attn_inner_got = at.fold_inner(at.fold_add(attn_far, attn_got))
+    attn_one_sum = attn_inner_got[:, :attn_cols].astype(f32) + attn_sums[1].total()
+    attn_last_got = at.to_slot(attn_one_sum.astype(bf16), 1)
+    attn_mine = (
+        attn_sums[0].total()
+        + attn_inner_got[:, attn_cols:].astype(f32)
+        + attn_last_got.astype(f32)
+    )
+    input_pair = at.deliver_pair(input_low, input_got)
+    input_last = at.deliver_last(input_pair)
+    input_grad = at.relative(at.delivered(input_pair, input_last), 2).astype(f32)
+    vector_grad = joined[: vector_grad.size].reshape(vector_grad.shape)
+    small_sum = lax.dynamic_index_in_dim(
+        joined[vector_grad.size :].reshape(small_grad.shape), at.mp_i, 0, keepdims=False
+    )
+    bias_sum = small_sum[:, :units].reshape(1, -1)
+    rel_sum = small_sum[:, units:].reshape(2 * heads, bucket_count).T
+
+    attn_mine, attn_other = exchanged(attn_mine)
+
+    if in_kernels:
         qkv_state, out_state, qkv_update, out_update, qkv_mine, out_mine, attn_squares = adjust_pair(
             at, adjust_attn_kernel, place, fixes, attn_mine, attn_other,
             weights[:2], dims[:2], [qkv_mom, out_moments],

time: 461 us -> 452 us (0.980)
  waiting for transfers between devices: 104 us -> 83 us
  starting transfers between devices: 111 us -> 124 us
    ppermute x82, waiting for transfers between devices: 104 us -> 83 us  [move(): return lax.ppermute(values, ('dp', 'mp'), pairs)]
    ppermute x82, starting transfers between devices: 111 us -> 124 us  [move(): return lax.ppermute(values, ('dp', 'mp'), pairs)]
    unnamed x236 -> x240, local copies, waits for them, and re-layouts: 21.3 us -> 20.7 us
  transfers between devices with their start and end apart: 82 -> 82, of which waited for: 30 -> 27; matrix products, arithmetic and copies ran while one was open for 20% -> 20% of each run, Pallas kernels for 23% -> 23%
where the time goes in v4:
time: 452 us; the launch traced here: 443 us
  starting transfers between devices  124 us (27%)
  Pallas kernels  117 us (26%)
  waiting for transfers between devices  83 us (18%)
  other arithmetic  55.4 us (12%)
  local copies, waits for them, and re-layouts  50.5 us (11%)
  matrix products  8.82 us (2%)
    ppermute x82, starting transfers between devices, move(): return lax.ppermute(values, ('dp', 'mp'), pairs)  124 us
    ppermute x82, waiting for transfers between devices, move(): return lax.ppermute(values, ('dp', 'mp'), pairs)  83 us
    pallas_call x4, Pallas kernels, attend_back(): pl.pallas_call(lambda *refs: attend_back_kernel(heads, *refs), out_shape=...  33.1 us
    unnamed x240, local copies, waits for them, and re-layouts  20.7 us
    pallas_call x8, Pallas kernels, grad_halves(): pl.pallas_call(lambda *refs: halves_kernel(order, [len(rights) for _, rig...  17.5 us
    pallas_call x4, Pallas kernels, sum_nt(): pl.pallas_call(lambda *refs: sum_nt_kernel(len(lefts), *refs), in_specs=[...  16.5 us
    pallas_call x4, Pallas kernels, attend(): pl.pallas_call(lambda *refs: attend_kernel(heads, *refs), out_shape=(jax....  16.1 us
  transfers between devices with their start and end apart: 82, of which 27 were waited for; matrix products, arithmetic and copies ran while one was open for 20% of the time, Pallas kernels for 23%

profile of v4, /device:TPU:1, one launch (start us, length us, event | category | flops | bytes accessed | tf_op | source)
XLA Modules:
  0.0 443.2 jit_solution(7609357513914387100)
XLA Ops:
  4.4 4.6 %pack_attn.1 = (bf16[1024,384]{1,0:T(8,128)(2,1)}, bf16[1024,128]{1,0:T(8,128)(2,1)}, bf16[256,512]{1,0:T(8,128)(2,1)}) custom-call(s32[2]{0:T(128)} %pad_add_fusion.1.place_ref, f32[3,1024,256]{2,1,0:T(8,128)} %bitcast.89, f32[256,1024]{1,0:T(8,128)} %out_ref.3), custom_call_target="tpu_custom_call" | custom-call | tf_op jit(solution)/shard_map/pack_attn/pallas_call | solution.py:481
  12.5 5.6 %collective-permute-start.1 = (bf16[256,1024]{1,0:T(8,128)(2,1)S(1)}, bf16[256,1024]{1,0:T(8,128)(2,1)}, u32[]{:S(2)}, u32[]{:S(2)}) collective-permute-start(bf16[256,1024]{1,0:T(8,128)(2,1)S(1)} %get-tuple-element.434), channel_id=1, source_target_pairs={{2,0},{3,1},{4,6},{5,7},{10,8},{11,9},{12,14},{13,15},{18,16},{19,... | collective-permute-start | bytes 1572872 | tf_op jit(solution)/shard_map/ppermute | solution.py:233
  21.3 5.4 %pack_mlp.1 = (bf16[1024,512]{1,0:T(8,128)(2,1)}, bf16[1024,512]{1,0:T(8,128)(2,1)}, bf16[256,512]{1,0:T(8,128)(2,1)}, bf16[256,512]{1,0:T(8,128)(2,1)}) custom-call(s32[2]{0:T(128)} %pad_add_fusion.1.place_ref, f32[1024,1024]{1,0:T(8,128)} %up_ref.3, f32[1024,1024]{1,0:T(8,128)} %down_ref.3), custom_call_target="tpu_custom_call" | custom-call | tf_op jit(solution)/shard_map/pack_mlp/pallas_call | solution.py:509
  47.6 6.2 %collective-permute-done.10 = bf16[256,1024]{1,0:T(8,128)(2,1)} collective-permute-done((bf16[256,1024]{1,0:T(8,128)(2,1)}, bf16[256,1024]{1,0:T(8,128)(2,1)}, u32[]{:S(2)}, u32[]{:S(2)}) %collective-permute-start.10) | collective-permute-done | bytes 524320 | tf_op jit(solution)/shard_map/ppermute | solution.py:233
  62.1 6.0 %collective-permute-done.12 = bf16[256,1024]{1,0:T(8,128)(2,1)S(1)} collective-permute-done((bf16[256,1024]{1,0:T(8,128)(2,1)}, bf16[256,1024]{1,0:T(8,128)(2,1)S(1)}, u32[]{:S(2)}, u32[]{:S(2)}) %collective-permute-start.12) | collective-permute-done | bytes 524320 | tf_op jit(solution)/shard_map/ppermute | solution.py:233
  73.2 5.1 %collective-permute-done.11 = bf16[272,1024]{1,0:T(8,128)(2,1)S(1)} collective-permute-done((bf16[272,1024]{1,0:T(8,128)(2,1)S(1)}, bf16[272,1024]{1,0:T(8,128)(2,1)S(1)}, u32[]{:S(2)}, u32[]{:S(2)}) %collective-permute-start.11) | collective-permute-done | bytes 557088 | tf_op jit(solution)/shard_map/ppermute | solution.py:233
  80.4 10.4 %collective-permute-done.17 = bf16[256,1024]{1,0:T(8,128)(2,1)} collective-permute-done((bf16[256,1024]{1,0:T(8,128)(2,1)}, bf16[256,1024]{1,0:T(8,128)(2,1)}, u32[]{:S(2)}, u32[]{:S(2)}) %collective-permute-start.17) | collective-permute-done | bytes 524320 | tf_op jit(solution)/shard_map/ppermute | solution.py:233
  109.5 5.1 %collective-permute-done.15 = bf16[256,1024]{1,0:T(8,128)(2,1)S(1)} collective-permute-done((bf16[256,1024]{1,0:T(8,128)(2,1)S(1)}, bf16[256,1024]{1,0:T(8,128)(2,1)S(1)}, u32[]{:S(2)}, u32[]{:S(2)}) %collective-permute-start.15) | collective-permute-done | bytes 524320 | tf_op jit(solution)/shard_map/ppermute | solution.py:233
  118.3 5.8 %collective-permute-start.28 = (bf16[256,1024]{1,0:T(8,128)(2,1)S(1)}, bf16[256,1024]{1,0:T(8,128)(2,1)S(1)}, u32[]{:S(2)}, u32[]{:S(2)}) collective-permute-start(bf16[256,1024]{1,0:T(8,128)(2,1)S(1)} %get-tuple-element.428), channel_id=1, source_target_pairs={{2,0},{3,1},{4,6},{5,7},{10,8},{11,9},{12,14},{13,15},{18,16},{19,... | collective-permute-start | bytes 1572872 | tf_op jit(solution)/shard_map/ppermute | solution.py:233
  157.5 4.3 collective-permute-done.32.refs_3_
  161.8 6.7 %collective-permute-start.29 = (bf16[256,1024]{1,0:T(8,128)(2,1)S(1)}, bf16[256,1024]{1,0:T(8,128)(2,1)S(1)}, u32[]{:S(2)}, u32[]{:S(2)}) collective-permute-start(bf16[256,1024]{1,0:T(8,128)(2,1)S(1)} %get-tuple-element.427), channel_id=1, source_target_pairs={{2,1},{3,0},{4,7},{5,6},{10,9},{11,8},{12,15},{13,14},{18,17},{19,... | collective-permute-start | bytes 1572872 | tf_op jit(solution)/shard_map/ppermute | solution.py:233
  168.6 5.6 %collective-permute-done.33.refs_7_ = bf16[256,512]{1,0:T(8,128)(2,1)S(1)} collective-permute-done((bf16[256,512]{1,0:T(8,128)(2,1)S(1)}, bf16[256,512]{1,0:T(8,128)(2,1)S(1)}, u32[]{:S(2)}, u32[]{:S(2)}) %collective-permute-start.33) | collective-permute-done | bytes 262176 | tf_op jit(solution)/shard_map/ppermute | solution.py:233
  203.4 4.5 %sum_nt.5 = bf16[1024,1024]{1,0:T(8,128)(2,1)S(1)} custom-call(bf16[1024,512]{1,0:T(8,128)(2,1)S(1)} %get-tuple-element.224.refs_0_.refs_1_, bf16[1024,512]{1,0:T(8,128)(2,1)S(1)} %get-tuple-element.225.refs_1_.refs_2_, bf16[1024,1024]{1,0:T(8,128)(2,1)S(1)} %get-tuple-element.221.refs_1_.refs_2_, bf16[1024,512]{1,0:T(8,128)(2,1)S(1)} %copy-done.5, ...), custom_call_target="tpu_custom_call" | custom-call | flops 2147483648 | bytes 1048576 | tf_op jit(solution)/shard_map/sum_nt/pallas_call | solution.py:589
  210.6 5.0 %sum_nt.6 = bf16[1024,1024]{1,0:T(8,128)(2,1)S(1)} custom-call(bf16[1024,512]{1,0:T(8,128)(2,1)S(1)} %get-tuple-element.232.refs_0_.refs_1_, bf16[1024,512]{1,0:T(8,128)(2,1)S(1)} %get-tuple-element.234.refs_1_.refs_2_, bf16[1024,1024]{1,0:T(8,128)(2,1)S(1)} %get-tuple-element.217.refs_1_.refs_2_, bf16[1024,512]{1,0:T(8,128)(2,1)S(1)} %copy-done.7, ...), custom_call_target="tpu_custom_call" | custom-call | flops 2147483648 | bytes 1048576 | tf_op jit(solution)/shard_map/sum_nt/pallas_call | solution.py:589
  226.8 7.8 %collective-permute-start.38 = (bf16[512,1024]{1,0:T(8,128)(2,1)S(1)}, bf16[512,1024]{1,0:T(8,128)(2,1)}, u32[]{:S(2)}, u32[]{:S(2)}) collective-permute-start(bf16[512,1024]{1,0:T(8,128)(2,1)S(1)} %fusion.3), channel_id=1, source_target_pairs={{2,4},{3,5},{4,2},{5,3},{10,12},{11,13},{12,10},{13,11},{18,20},{1... | collective-permute-start | bytes 3145736 | tf_op jit(solution)/shard_map/ppermute | solution.py:233
  238.2 4.6 %collective-permute-start.43 = (bf16[256,2048]{1,0:T(8,128)(2,1)}, bf16[256,2048]{1,0:T(8,128)(2,1)}, u32[]{:S(2)}, u32[]{:S(2)}) collective-permute-start(bf16[256,2048]{1,0:T(8,128)(2,1)} %pad_maximum_fusion.4), channel_id=1, source_target_pairs={{0,1},{3,2},{4,5},{7,6},{8,9},{11,10},{12,13},{15,14},{16,17},{19,... | collective-permute-start | bytes 3145736 | tf_op jit(solution)/shard_map/ppermute | solution.py:233
  249.4 8.1 %attend_back.6 = (bf16[1024,384]{1,0:T(8,128)(2,1)S(1)}, f32[2,2048]{1,0:T(2,128)S(1)}) custom-call(s32[1]{0:T(128)} %dynamic_slice.186.refs_0_, bf16[1024,384]{1,0:T(8,128)(2,1)S(1)} %convolution_convert_fusion.1.refs_1_, f32[2,2048]{1,0:T(2,128)S(1)} %fusion.20.refs_2_, f32[2,1024]{1,0:T(2,128)S(1)} %get-tuple-element.255.refs_3_, ...), custom_call_target="tpu_custom_call" | custom-call | flops 2684354560 | bytes 1048576 | tf_op jit(solution)/shard_map/attend_back/pallas_call | solution.py:165
  258.9 8.3 %attend_back.7 = (bf16[1024,384]{1,0:T(8,128)(2,1)S(1)}, f32[2,2048]{1,0:T(2,128)S(1)}) custom-call(s32[1]{0:T(128)} %dynamic_slice.186.refs_0_, bf16[1024,384]{1,0:T(8,128)(2,1)S(1)} %convolution_convert_fusion.refs_1_, f32[2,2048]{1,0:T(2,128)S(1)} %fusion.19.refs_2_, f32[2,1024]{1,0:T(2,128)S(1)} %get-tuple-element.258.refs_3_, ...), custom_call_target="tpu_custom_call" | custom-call | flops 2684354560 | bytes 1048576 | tf_op jit(solution)/shard_map/attend_back/pallas_call | solution.py:165
  272.0 8.6 %attend_back.5 = (bf16[1024,384]{1,0:T(8,128)(2,1)S(1)}, f32[2,2048]{1,0:T(2,128)S(1)}) custom-call(s32[1]{0:T(128)} %dynamic_slice.186.refs_0_, bf16[1024,384]{1,0:T(8,128)(2,1)S(1)} %convolution_convert_fusion.2.refs_1_, f32[2,2048]{1,0:T(2,128)S(1)} %fusion.21.refs_2_, f32[2,1024]{1,0:T(2,128)S(1)} %get-tuple-element.252.refs_3_, ...), custom_call_target="tpu_custom_call" | custom-call | flops 2684354560 | bytes 1048576 | tf_op jit(solution)/shard_map/attend_back/pallas_call | solution.py:165
  290.2 8.1 %attend_back.4 = (bf16[1024,384]{1,0:T(8,128)(2,1)S(1)}, f32[2,2048]{1,0:T(2,128)S(1)}) custom-call(s32[1]{0:T(128)} %dynamic_slice.186.refs_0_, bf16[1024,384]{1,0:T(8,128)(2,1)S(1)} %convolution_convert_fusion.3.refs_1_, f32[2,2048]{1,0:T(2,128)S(1)} %fusion.22.refs_2_, f32[2,1024]{1,0:T(2,128)S(1)} %get-tuple-element.229.refs_3_, ...), custom_call_target="tpu_custom_call" | custom-call | flops 2684354560 | bytes 1048576 | tf_op jit(solution)/shard_map/attend_back/pallas_call | solution.py:165
  306.6 4.7 %sum_nt.7 = bf16[1024,1024]{1,0:T(8,128)(2,1)S(1)} custom-call(bf16[1024,384]{1,0:T(8,128)(2,1)S(1)} %copy-done.11, bf16[1024,384]{1,0:T(8,128)(2,1)S(1)} %copy-done.13, bf16[1024,384]{1,0:T(8,128)(2,1)S(1)} %get-tuple-element.257.refs_2_.refs_1_, bf16[1024,384]{1,0:T(8,128)(2,1)S(1)} %copy-done.9, bf16[1024,384]{1,0:T(8,128)(2,1)S(1)} %copy-done.23, ...), custom_call_target="tpu_custom_call" | custom-call | flops 1610612736 | bytes 1048576 | tf_op jit(solution)/shard_map/sum_nt/pallas_call | solution.py:589
  347.9 6.0 %collective-permute-done.56 = bf16[256,1024]{1,0:T(8,128)(2,1)S(1)} collective-permute-done((bf16[256,1024]{1,0:T(8,128)(2,1)S(1)}, bf16[256,1024]{1,0:T(8,128)(2,1)S(1)}, u32[]{:S(2)}, u32[]{:S(2)}) %collective-permute-start.56) | collective-permute-done | bytes 524320 | tf_op jit(solution)/shard_map/ppermute | solution.py:233
  362.8 6.0 %collective-permute-start.60 = (bf16[512,1024]{1,0:T(8,128)(2,1)}, bf16[512,1024]{1,0:T(8,128)(2,1)}, u32[]{:S(2)}, u32[]{:S(2)}) collective-permute-start(bf16[512,1024]{1,0:T(8,128)(2,1)} %fusion.4), channel_id=1, source_target_pairs={{2,4},{3,5},{4,2},{5,3},{10,12},{11,13},{12,10},{13,11},{18,20},{1... | collective-permute-start | bytes 3145736 | tf_op jit(solution)/shard_map/ppermute | solution.py:233
  414.1 5.0 %collective-permute-done.73 = bf16[256,512]{1,0:T(8,128)(2,1)S(1)} collective-permute-done((bf16[256,512]{1,0:T(8,128)(2,1)S(1)}, bf16[256,512]{1,0:T(8,128)(2,1)S(1)}, u32[]{:S(2)}, u32[]{:S(2)}) %collective-permute-start.73) | collective-permute-done | bytes 262176 | tf_op jit(solution)/shard_map/ppermute | solution.py:233
  (622 shorter events, 291.5 us)
Async XLA Ops:
  2.3 35.3 %collective-permute-start = (bf16[256,1024]{1,0:T(8,128)(2,1)S(1)}, bf16[256,1024]{1,0:T(8,128)(2,1)}, u32[]{:S(2)}, u32[]{:S(2)}) collective-permute-start(bf16[256,1024]{1,0:T(8,128)(2,1)S(1)} %get-tuple-element.435), channel_id=1, source_target_pairs={{0,1},{1,0},{6,7},{7,6},{8,9},{9,8},{14,15},{15,14},{16,17},{17,16... | collective-permute-start | bytes 1572872 | tf_op jit(solution)/shard_map/ppermute | solution.py:233
  10.3 27.3 %collective-permute-start.2 = (bf16[272,512]{1,0:T(8,128)(2,1)S(1)}, bf16[272,512]{1,0:T(8,128)(2,1)S(1)}, u32[]{:S(2)}, u32[]{:S(2)}) collective-permute-start(bf16[272,512]{1,0:T(8,128)(2,1)S(1)} %constant_dynamic-update-slice_fusion), channel_id=1, source_target_pairs={{0,1},{1,0},{2,3},{3,2},{4,5},{5,4},{6,7},{7,6},{8,9},{9,8},{10,11... | collective-permute-start | bytes 835592 | tf_op jit(solution)/shard_map/ppermute | solution.py:233
  12.5 27.6 %collective-permute-start.1 = (bf16[256,1024]{1,0:T(8,128)(2,1)S(1)}, bf16[256,1024]{1,0:T(8,128)(2,1)}, u32[]{:S(2)}, u32[]{:S(2)}) collective-permute-start(bf16[256,1024]{1,0:T(8,128)(2,1)S(1)} %get-tuple-element.434), channel_id=1, source_target_pairs={{2,0},{3,1},{4,6},{5,7},{10,8},{11,9},{12,14},{13,15},{18,16},{19,... | collective-permute-start | bytes 1572872 | tf_op jit(solution)/shard_map/ppermute | solution.py:233
  18.2 22.9 %collective-permute-start.3 = (bf16[256,1024]{1,0:T(8,128)(2,1)S(1)}, bf16[256,1024]{1,0:T(8,128)(2,1)}, u32[]{:S(2)}, u32[]{:S(2)}) collective-permute-start(bf16[256,1024]{1,0:T(8,128)(2,1)S(1)} %get-tuple-element.433), channel_id=1, source_target_pairs={{2,1},{3,0},{4,7},{5,6},{10,9},{11,8},{12,15},{13,14},{18,17},{19,... | collective-permute-start | bytes 1572872 | tf_op jit(solution)/shard_map/ppermute | solution.py:233
  59.3 32.7 %collective-permute-start.4 = (bf16[1024,1024]{1,0:T(8,128)(2,1)}, bf16[1024,1024]{1,0:T(8,128)(2,1)}, u32[]{:S(2)}, u32[]{:S(2)}) collective-permute-start(bf16[1024,1024]{1,0:T(8,128)(2,1)} %constant_dynamic-update-slice_fusion.12), channel_id=1, source_target_pairs={{0,4},{1,5},{6,2},{7,3},{8,12},{9,13},{14,10},{15,11},{16,20},{17,... | collective-permute-start | bytes 6291464 | tf_op jit(solution)/shard_map/ppermute | solution.py:233
  70.5 20.3 %collective-permute-start.17 = (bf16[256,1024]{1,0:T(8,128)(2,1)}, bf16[256,1024]{1,0:T(8,128)(2,1)}, u32[]{:S(2)}, u32[]{:S(2)}) collective-permute-start(bf16[256,1024]{1,0:T(8,128)(2,1)} %collective-permute-done.14), channel_id=1, source_target_pairs={{1,0},{2,3},{5,4},{6,7},{9,8},{10,11},{13,12},{14,15},{17,16},{18,... | collective-permute-start | bytes 1572872 | tf_op jit(solution)/shard_map/ppermute | solution.py:233
  118.3 37.1 %collective-permute-start.28 = (bf16[256,1024]{1,0:T(8,128)(2,1)S(1)}, bf16[256,1024]{1,0:T(8,128)(2,1)S(1)}, u32[]{:S(2)}, u32[]{:S(2)}) collective-permute-start(bf16[256,1024]{1,0:T(8,128)(2,1)S(1)} %get-tuple-element.428), channel_id=1, source_target_pairs={{2,0},{3,1},{4,6},{5,7},{10,8},{11,9},{12,14},{13,15},{18,16},{19,... | collective-permute-start | bytes 1572872 | tf_op jit(solution)/shard_map/ppermute | solution.py:233
  135.5 21.2 %collective-permute-start.27 = (bf16[256,1024]{1,0:T(8,128)(2,1)S(1)}, bf16[256,1024]{1,0:T(8,128)(2,1)S(1)}, u32[]{:S(2)}, u32[]{:S(2)}) collective-permute-start(bf16[256,1024]{1,0:T(8,128)(2,1)S(1)} %dynamic-slice_bitcast_fusion.2), channel_id=1, source_target_pairs={{0,1},{1,0},{6,7},{7,6},{8,9},{9,8},{14,15},{15,14},{16,17},{17,16... | collective-permute-start | bytes 1572872 | tf_op jit(solution)/shard_map/ppermute | solution.py:233
  150.4 31.5 %collective-permute-start.26 = (bf16[1024,1024]{1,0:T(8,128)(2,1)S(1)}, bf16[1024,1024]{1,0:T(8,128)(2,1)S(1)}, u32[]{:S(2)}, u32[]{:S(2)}) collective-permute-start(bf16[1024,1024]{1,0:T(8,128)(2,1)S(1)} %sum_nt.4), channel_id=1, source_target_pairs={{0,4},{1,5},{2,6},{3,7},{4,0},{5,1},{6,2},{7,3},{8,12},{9,13},{10,... | collective-permute-start | bytes 6291464 | tf_op jit(solution)/shard_map/ppermute | solution.py:233
  155.3 18.8 %collective-permute-start.34 = (bf16[256,1024]{1,0:T(8,128)(2,1)S(1)}, bf16[256,1024]{1,0:T(8,128)(2,1)S(1)}, u32[]{:S(2)}, u32[]{:S(2)}) collective-permute-start(bf16[256,1024]{1,0:T(8,128)(2,1)S(1)} %maximum_select_fusion.2), channel_id=1, source_target_pairs={{0,16},{1,17},{2,18},{3,19},{4,20},{5,21},{6,22},{7,23},{8,24},{9,... | collective-permute-start | bytes 1572872 | tf_op jit(solution)/shard_map/ppermute | solution.py:233
  155.5 20.0 %collective-permute-start.31 = (bf16[256,1024]{1,0:T(8,128)(2,1)S(1)}, bf16[256,1024]{1,0:T(8,128)(2,1)S(1)}, u32[]{:S(2)}, u32[]{:S(2)}) collective-permute-start(bf16[256,1024]{1,0:T(8,128)(2,1)S(1)} %maximum_select_fusion.2), channel_id=1, source_target_pairs={{0,8},{1,9},{2,10},{3,11},{4,12},{5,13},{6,14},{7,15},{8,0},{9,1},... | collective-permute-start | bytes 1572872 | tf_op jit(solution)/shard_map/ppermute | solution.py:233
  195.2 26.6 %collective-permute-start.40 = (bf16[512,1024]{1,0:T(8,128)(2,1)S(1)}, bf16[512,1024]{1,0:T(8,128)(2,1)S(1)}, u32[]{:S(2)}, u32[]{:S(2)}) collective-permute-start(bf16[512,1024]{1,0:T(8,128)(2,1)S(1)} %get-tuple-element.219), channel_id=1, source_target_pairs={{0,16},{1,17},{2,18},{3,19},{4,20},{5,21},{6,22},{7,23},{8,24},{9,... | collective-permute-start | bytes 3145736 | tf_op jit(solution)/shard_map/ppermute | solution.py:233
  199.1 22.7 %collective-permute-start.39 = (bf16[512,1024]{1,0:T(8,128)(2,1)S(1)}, bf16[512,1024]{1,0:T(8,128)(2,1)S(1)}, u32[]{:S(2)}, u32[]{:S(2)}) collective-permute-start(bf16[512,1024]{1,0:T(8,128)(2,1)S(1)} %get-tuple-element.223), channel_id=1, source_target_pairs={{0,8},{1,9},{2,10},{3,11},{4,12},{5,13},{6,14},{7,15},{8,0},{9,1},... | collective-permute-start | bytes 3145736 | tf_op jit(solution)/shard_map/ppermute | solution.py:233
  215.5 27.2 %collective-permute-start.44 = (bf16[1024,1024]{1,0:T(8,128)(2,1)S(1)}, bf16[1024,1024]{1,0:T(8,128)(2,1)S(1)}, u32[]{:S(2)}, u32[]{:S(2)}) collective-permute-start(bf16[1024,1024]{1,0:T(8,128)(2,1)S(1)} %sum_nt.6), channel_id=1, source_target_pairs={{0,4},{1,5},{2,6},{3,7},{4,0},{5,1},{6,2},{7,3},{8,12},{9,13},{10,... | collective-permute-start | bytes 6291464 | tf_op jit(solution)/shard_map/ppermute | solution.py:233
  226.8 40.5 %collective-permute-start.38 = (bf16[512,1024]{1,0:T(8,128)(2,1)S(1)}, bf16[512,1024]{1,0:T(8,128)(2,1)}, u32[]{:S(2)}, u32[]{:S(2)}) collective-permute-start(bf16[512,1024]{1,0:T(8,128)(2,1)S(1)} %fusion.3), channel_id=1, source_target_pairs={{2,4},{3,5},{4,2},{5,3},{10,12},{11,13},{12,10},{13,11},{18,20},{1... | collective-permute-start | bytes 3145736 | tf_op jit(solution)/shard_map/ppermute | solution.py:233
  234.6 51.7 %collective-permute-start.46 = (bf16[512,1024]{1,0:T(8,128)(2,1)S(1)}, bf16[512,1024]{1,0:T(8,128)(2,1)S(1)}, u32[]{:S(2)}, u32[]{:S(2)}) collective-permute-start(bf16[512,1024]{1,0:T(8,128)(2,1)S(1)} %get-tuple-element.243), channel_id=1, source_target_pairs={{0,16},{1,17},{2,18},{3,19},{4,20},{5,21},{6,22},{7,23},{8,24},{9,... | collective-permute-start | bytes 3145736 | tf_op jit(solution)/shard_map/ppermute | solution.py:233
  235.5 50.9 %collective-permute-start.45 = (bf16[512,1024]{1,0:T(8,128)(2,1)S(1)}, bf16[512,1024]{1,0:T(8,128)(2,1)S(1)}, u32[]{:S(2)}, u32[]{:S(2)}) collective-permute-start(bf16[512,1024]{1,0:T(8,128)(2,1)S(1)} %get-tuple-element.242), channel_id=1, source_target_pairs={{0,8},{1,9},{2,10},{3,11},{4,12},{5,13},{6,14},{7,15},{8,0},{9,1},... | collective-permute-start | bytes 3145736 | tf_op jit(solution)/shard_map/ppermute | solution.py:233
  238.2 52.0 %collective-permute-start.43 = (bf16[256,2048]{1,0:T(8,128)(2,1)}, bf16[256,2048]{1,0:T(8,128)(2,1)}, u32[]{:S(2)}, u32[]{:S(2)}) collective-permute-start(bf16[256,2048]{1,0:T(8,128)(2,1)} %pad_maximum_fusion.4), channel_id=1, source_target_pairs={{0,1},{3,2},{4,5},{7,6},{8,9},{11,10},{12,13},{15,14},{16,17},{19,... | collective-permute-start | bytes 3145736 | tf_op jit(solution)/shard_map/ppermute | solution.py:233
  304.1 22.1 %collective-permute-start.63 = (bf16[512,512]{1,0:T(8,128)(2,1)S(1)}, bf16[512,512]{1,0:T(8,128)(2,1)S(1)}, u32[]{:S(2)}, u32[]{:S(2)}) collective-permute-start(bf16[512,512]{1,0:T(8,128)(2,1)S(1)} %copy-done.57), channel_id=1, source_target_pairs={{0,8},{1,9},{2,10},{3,11},{4,12},{5,13},{6,14},{7,15},{8,0},{9,1},... | collective-permute-start | bytes 1572872 | tf_op jit(solution)/shard_map/ppermute | solution.py:233
  304.3 21.9 %collective-permute-start.62 = (bf16[512,512]{1,0:T(8,128)(2,1)}, bf16[512,512]{1,0:T(8,128)(2,1)S(1)}, u32[]{:S(2)}, u32[]{:S(2)}) collective-permute-start(bf16[512,512]{1,0:T(8,128)(2,1)} %copy-done.58), channel_id=1, source_target_pairs={{0,16},{1,17},{2,18},{3,19},{4,20},{5,21},{6,22},{7,23},{8,24},{9,... | collective-permute-start | bytes 1572872 | tf_op jit(solution)/shard_map/ppermute | solution.py:233
  311.6 24.2 %collective-permute-start.50 = (bf16[512,1024]{1,0:T(8,128)(2,1)S(1)}, bf16[512,1024]{1,0:T(8,128)(2,1)S(1)}, u32[]{:S(2)}, u32[]{:S(2)}) collective-permute-start(bf16[512,1024]{1,0:T(8,128)(2,1)S(1)} %pad_maximum_fusion.7), channel_id=1, source_target_pairs={{0,4},{1,5},{2,6},{3,7},{4,0},{5,1},{6,2},{7,3},{8,12},{9,13},{10,... | collective-permute-start | bytes 3145736 | tf_op jit(solution)/shard_map/ppermute | solution.py:233
  314.2 23.5 %collective-permute-start.55 = (bf16[256,2048]{1,0:T(8,128)(2,1)}, bf16[256,2048]{1,0:T(8,128)(2,1)}, u32[]{:S(2)}, u32[]{:S(2)}) collective-permute-start(bf16[256,2048]{1,0:T(8,128)(2,1)} %add_convert_fusion.2), channel_id=1, source_target_pairs={{1,2},{2,1},{5,6},{6,5},{9,10},{10,9},{13,14},{14,13},{17,18},{18,... | collective-permute-start | bytes 3145736 | tf_op jit(solution)/shard_map/ppermute | solution.py:233
  362.8 30.0 %collective-permute-start.60 = (bf16[512,1024]{1,0:T(8,128)(2,1)}, bf16[512,1024]{1,0:T(8,128)(2,1)}, u32[]{:S(2)}, u32[]{:S(2)}) collective-permute-start(bf16[512,1024]{1,0:T(8,128)(2,1)} %fusion.4), channel_id=1, source_target_pairs={{2,4},{3,5},{4,2},{5,3},{10,12},{11,13},{12,10},{13,11},{18,20},{1... | collective-permute-start | bytes 3145736 | tf_op jit(solution)/shard_map/ppermute | solution.py:233
  371.0 21.1 %collective-permute-start.69 = (bf16[256,1024]{1,0:T(8,128)(2,1)}, bf16[256,1024]{1,0:T(8,128)(2,1)}, u32[]{:S(2)}, u32[]{:S(2)}) collective-permute-start(bf16[256,1024]{1,0:T(8,128)(2,1)} %pad_maximum_fusion.11), channel_id=1, source_target_pairs={{0,1},{3,2},{4,5},{7,6},{8,9},{11,10},{12,13},{15,14},{16,17},{19,... | collective-permute-start | bytes 1572872 | tf_op jit(solution)/shard_map/ppermute | solution.py:233
  (170 other events, 2098.6 us)

commit v5 on v4

--- a/solution.py
+++ b/solution.py
@@ -15,8 +15,8 @@
 weight_decay = 0.1
 masked_score = -1000000000.0
 score_scale = HD ** (-0.5)
-kernel_bytes = 12 << 20
-back_bytes = 16 << 20
+kernel_bytes = 16 << 20
+back_bytes = 24 << 20
 
 in_vmem = pl.BlockSpec(memory_space=pltpu.VMEM)
 in_smem = pl.BlockSpec(memory_space=pltpu.SMEM)

time: 452 us -> 451 us (level)
  transfers between devices with their start and end apart: 82 -> 82, of which waited for: 27 -> 26; matrix products, arithmetic and copies ran while one was open for 20% -> 20% of each run, Pallas kernels for 23% -> 23%
where the time goes in v5:
time: 451 us; the launch traced here: 442 us
  starting transfers between devices  125 us (28%)
  Pallas kernels  117 us (26%)
  waiting for transfers between devices  83 us (18%)
  other arithmetic  55.4 us (12%)
  local copies, waits for them, and re-layouts  48.6 us (11%)
  matrix products  8.81 us (2%)
    ppermute x82, starting transfers between devices, move(): return lax.ppermute(values, ('dp', 'mp'), pairs)  125 us
    ppermute x82, waiting for transfers between devices, move(): return lax.ppermute(values, ('dp', 'mp'), pairs)  83 us
    pallas_call x4, Pallas kernels, attend_back(): pl.pallas_call(lambda *refs: attend_back_kernel(heads, *refs), out_shape=...  33.1 us
    unnamed x240, local copies, waits for them, and re-layouts  18.8 us
    pallas_call x8, Pallas kernels, grad_halves(): pl.pallas_call(lambda *refs: halves_kernel(order, [len(rights) for _, rig...  17.5 us
    pallas_call x4, Pallas kernels, sum_nt(): pl.pallas_call(lambda *refs: sum_nt_kernel(len(lefts), *refs), in_specs=[...  16.5 us
    pallas_call x4, Pallas kernels, attend(): pl.pallas_call(lambda *refs: attend_kernel(heads, *refs), out_shape=(jax....  16.1 us
  transfers between devices with their start and end apart: 82, of which 26 were waited for; matrix products, arithmetic and copies ran while one was open for 20% of the time, Pallas kernels for 23%

profile of v5, /device:TPU:1, one launch (start us, length us, event | category | flops | bytes accessed | tf_op | source)
XLA Modules:
  0.0 442.2 jit_solution(16418473508887402224)
XLA Ops:
  4.4 4.6 %pack_attn.1 = (bf16[1024,384]{1,0:T(8,128)(2,1)}, bf16[1024,128]{1,0:T(8,128)(2,1)}, bf16[256,512]{1,0:T(8,128)(2,1)}) custom-call(s32[2]{0:T(128)} %pad_add_fusion.1.place_ref, f32[3,1024,256]{2,1,0:T(8,128)} %bitcast.89, f32[256,1024]{1,0:T(8,128)} %out_ref.3), custom_call_target="tpu_custom_call" | custom-call | tf_op jit(solution)/shard_map/pack_attn/pallas_call | solution.py:481
  12.5 5.6 %collective-permute-start.1 = (bf16[256,1024]{1,0:T(8,128)(2,1)S(1)}, bf16[256,1024]{1,0:T(8,128)(2,1)}, u32[]{:S(2)}, u32[]{:S(2)}) collective-permute-start(bf16[256,1024]{1,0:T(8,128)(2,1)S(1)} %get-tuple-element.434), channel_id=1, source_target_pairs={{2,0},{3,1},{4,6},{5,7},{10,8},{11,9},{12,14},{13,15},{18,16},{19,... | collective-permute-start | bytes 1572872 | tf_op jit(solution)/shard_map/ppermute | solution.py:233
  21.3 5.4 %pack_mlp.1 = (bf16[1024,512]{1,0:T(8,128)(2,1)}, bf16[1024,512]{1,0:T(8,128)(2,1)}, bf16[256,512]{1,0:T(8,128)(2,1)}, bf16[256,512]{1,0:T(8,128)(2,1)}) custom-call(s32[2]{0:T(128)} %pad_add_fusion.1.place_ref, f32[1024,1024]{1,0:T(8,128)} %up_ref.3, f32[1024,1024]{1,0:T(8,128)} %down_ref.3), custom_call_target="tpu_custom_call" | custom-call | tf_op jit(solution)/shard_map/pack_mlp/pallas_call | solution.py:509
  47.6 6.2 %collective-permute-done.10 = bf16[256,1024]{1,0:T(8,128)(2,1)} collective-permute-done((bf16[256,1024]{1,0:T(8,128)(2,1)}, bf16[256,1024]{1,0:T(8,128)(2,1)}, u32[]{:S(2)}, u32[]{:S(2)}) %collective-permute-start.10) | collective-permute-done | bytes 524320 | tf_op jit(solution)/shard_map/ppermute | solution.py:233
  62.1 6.0 %collective-permute-done.12 = bf16[256,1024]{1,0:T(8,128)(2,1)S(1)} collective-permute-done((bf16[256,1024]{1,0:T(8,128)(2,1)}, bf16[256,1024]{1,0:T(8,128)(2,1)S(1)}, u32[]{:S(2)}, u32[]{:S(2)}) %collective-permute-start.12) | collective-permute-done | bytes 524320 | tf_op jit(solution)/shard_map/ppermute | solution.py:233
  73.2 5.1 %collective-permute-done.11 = bf16[272,1024]{1,0:T(8,128)(2,1)S(1)} collective-permute-done((bf16[272,1024]{1,0:T(8,128)(2,1)S(1)}, bf16[272,1024]{1,0:T(8,128)(2,1)S(1)}, u32[]{:S(2)}, u32[]{:S(2)}) %collective-permute-start.11) | collective-permute-done | bytes 557088 | tf_op jit(solution)/shard_map/ppermute | solution.py:233
  80.4 10.4 %collective-permute-done.17 = bf16[256,1024]{1,0:T(8,128)(2,1)} collective-permute-done((bf16[256,1024]{1,0:T(8,128)(2,1)}, bf16[256,1024]{1,0:T(8,128)(2,1)}, u32[]{:S(2)}, u32[]{:S(2)}) %collective-permute-start.17) | collective-permute-done | bytes 524320 | tf_op jit(solution)/shard_map/ppermute | solution.py:233
  109.5 5.1 %collective-permute-done.15 = bf16[256,1024]{1,0:T(8,128)(2,1)S(1)} collective-permute-done((bf16[256,1024]{1,0:T(8,128)(2,1)S(1)}, bf16[256,1024]{1,0:T(8,128)(2,1)S(1)}, u32[]{:S(2)}, u32[]{:S(2)}) %collective-permute-start.15) | collective-permute-done | bytes 524320 | tf_op jit(solution)/shard_map/ppermute | solution.py:233
  118.3 5.8 %collective-permute-start.28 = (bf16[256,1024]{1,0:T(8,128)(2,1)S(1)}, bf16[256,1024]{1,0:T(8,128)(2,1)S(1)}, u32[]{:S(2)}, u32[]{:S(2)}) collective-permute-start(bf16[256,1024]{1,0:T(8,128)(2,1)S(1)} %get-tuple-element.428), channel_id=1, source_target_pairs={{2,0},{3,1},{4,6},{5,7},{10,8},{11,9},{12,14},{13,15},{18,16},{19,... | collective-permute-start | bytes 1572872 | tf_op jit(solution)/shard_map/ppermute | solution.py:233
  157.5 4.3 collective-permute-done.32.refs_3_
  161.8 6.7 %collective-permute-start.29 = (bf16[256,1024]{1,0:T(8,128)(2,1)S(1)}, bf16[256,1024]{1,0:T(8,128)(2,1)S(1)}, u32[]{:S(2)}, u32[]{:S(2)}) collective-permute-start(bf16[256,1024]{1,0:T(8,128)(2,1)S(1)} %get-tuple-element.427), channel_id=1, source_target_pairs={{2,1},{3,0},{4,7},{5,6},{10,9},{11,8},{12,15},{13,14},{18,17},{19,... | collective-permute-start | bytes 1572872 | tf_op jit(solution)/shard_map/ppermute | solution.py:233
  168.6 5.6 %collective-permute-done.33.refs_7_ = bf16[256,512]{1,0:T(8,128)(2,1)S(1)} collective-permute-done((bf16[256,512]{1,0:T(8,128)(2,1)S(1)}, bf16[256,512]{1,0:T(8,128)(2,1)S(1)}, u32[]{:S(2)}, u32[]{:S(2)}) %collective-permute-start.33) | collective-permute-done | bytes 262176 | tf_op jit(solution)/shard_map/ppermute | solution.py:233
  203.4 4.5 %sum_nt.5 = bf16[1024,1024]{1,0:T(8,128)(2,1)S(1)} custom-call(bf16[1024,512]{1,0:T(8,128)(2,1)S(1)} %get-tuple-element.224.refs_0_.refs_1_, bf16[1024,512]{1,0:T(8,128)(2,1)S(1)} %get-tuple-element.225.refs_1_.refs_2_, bf16[1024,1024]{1,0:T(8,128)(2,1)S(1)} %get-tuple-element.221.refs_1_.refs_2_, bf16[1024,512]{1,0:T(8,128)(2,1)S(1)} %copy-done.5, ...), custom_call_target="tpu_custom_call" | custom-call | flops 2147483648 | bytes 1048576 | tf_op jit(solution)/shard_map/sum_nt/pallas_call | solution.py:589
  210.5 5.0 %sum_nt.6 = bf16[1024,1024]{1,0:T(8,128)(2,1)S(1)} custom-call(bf16[1024,512]{1,0:T(8,128)(2,1)S(1)} %get-tuple-element.232.refs_0_.refs_1_, bf16[1024,512]{1,0:T(8,128)(2,1)S(1)} %get-tuple-element.234.refs_1_.refs_2_, bf16[1024,1024]{1,0:T(8,128)(2,1)S(1)} %get-tuple-element.217.refs_1_.refs_2_, bf16[1024,512]{1,0:T(8,128)(2,1)S(1)} %copy-done.7, ...), custom_call_target="tpu_custom_call" | custom-call | flops 2147483648 | bytes 1048576 | tf_op jit(solution)/shard_map/sum_nt/pallas_call | solution.py:589
  226.7 7.8 %collective-permute-start.38 = (bf16[512,1024]{1,0:T(8,128)(2,1)S(1)}, bf16[512,1024]{1,0:T(8,128)(2,1)}, u32[]{:S(2)}, u32[]{:S(2)}) collective-permute-start(bf16[512,1024]{1,0:T(8,128)(2,1)S(1)} %fusion.3), channel_id=1, source_target_pairs={{2,4},{3,5},{4,2},{5,3},{10,12},{11,13},{12,10},{13,11},{18,20},{1... | collective-permute-start | bytes 3145736 | tf_op jit(solution)/shard_map/ppermute | solution.py:233
  238.2 4.6 %collective-permute-start.43 = (bf16[256,2048]{1,0:T(8,128)(2,1)}, bf16[256,2048]{1,0:T(8,128)(2,1)}, u32[]{:S(2)}, u32[]{:S(2)}) collective-permute-start(bf16[256,2048]{1,0:T(8,128)(2,1)} %pad_maximum_fusion.4), channel_id=1, source_target_pairs={{0,1},{3,2},{4,5},{7,6},{8,9},{11,10},{12,13},{15,14},{16,17},{19,... | collective-permute-start | bytes 3145736 | tf_op jit(solution)/shard_map/ppermute | solution.py:233
  249.4 8.1 %attend_back.6 = (bf16[1024,384]{1,0:T(8,128)(2,1)S(1)}, f32[2,2048]{1,0:T(2,128)S(1)}) custom-call(s32[1]{0:T(128)} %dynamic_slice.186.refs_0_, bf16[1024,384]{1,0:T(8,128)(2,1)S(1)} %convolution_convert_fusion.1.refs_1_, f32[2,2048]{1,0:T(2,128)S(1)} %fusion.20.refs_2_, f32[2,1024]{1,0:T(2,128)S(1)} %get-tuple-element.255.refs_3_, ...), custom_call_target="tpu_custom_call" | custom-call | flops 2684354560 | bytes 1048576 | tf_op jit(solution)/shard_map/attend_back/pallas_call | solution.py:165
  259.0 8.3 %attend_back.7 = (bf16[1024,384]{1,0:T(8,128)(2,1)S(1)}, f32[2,2048]{1,0:T(2,128)S(1)}) custom-call(s32[1]{0:T(128)} %dynamic_slice.186.refs_0_, bf16[1024,384]{1,0:T(8,128)(2,1)S(1)} %convolution_convert_fusion.refs_1_, f32[2,2048]{1,0:T(2,128)S(1)} %fusion.19.refs_2_, f32[2,1024]{1,0:T(2,128)S(1)} %get-tuple-element.258.refs_3_, ...), custom_call_target="tpu_custom_call" | custom-call | flops 2684354560 | bytes 1048576 | tf_op jit(solution)/shard_map/attend_back/pallas_call | solution.py:165
  271.3 8.6 %attend_back.5 = (bf16[1024,384]{1,0:T(8,128)(2,1)S(1)}, f32[2,2048]{1,0:T(2,128)S(1)}) custom-call(s32[1]{0:T(128)} %dynamic_slice.186.refs_0_, bf16[1024,384]{1,0:T(8,128)(2,1)S(1)} %convolution_convert_fusion.2.refs_1_, f32[2,2048]{1,0:T(2,128)S(1)} %fusion.21.refs_2_, f32[2,1024]{1,0:T(2,128)S(1)} %get-tuple-element.252.refs_3_, ...), custom_call_target="tpu_custom_call" | custom-call | flops 2684354560 | bytes 1048576 | tf_op jit(solution)/shard_map/attend_back/pallas_call | solution.py:165
  289.2 8.1 %attend_back.4 = (bf16[1024,384]{1,0:T(8,128)(2,1)S(1)}, f32[2,2048]{1,0:T(2,128)S(1)}) custom-call(s32[1]{0:T(128)} %dynamic_slice.186.refs_0_, bf16[1024,384]{1,0:T(8,128)(2,1)S(1)} %convolution_convert_fusion.3.refs_1_, f32[2,2048]{1,0:T(2,128)S(1)} %fusion.22.refs_2_, f32[2,1024]{1,0:T(2,128)S(1)} %get-tuple-element.229.refs_3_, ...), custom_call_target="tpu_custom_call" | custom-call | flops 2684354560 | bytes 1048576 | tf_op jit(solution)/shard_map/attend_back/pallas_call | solution.py:165
  305.5 4.7 %sum_nt.7 = bf16[1024,1024]{1,0:T(8,128)(2,1)S(1)} custom-call(bf16[1024,384]{1,0:T(8,128)(2,1)S(1)} %copy-done.11, bf16[1024,384]{1,0:T(8,128)(2,1)S(1)} %copy-done.13, bf16[1024,384]{1,0:T(8,128)(2,1)S(1)} %get-tuple-element.257.refs_2_.refs_1_, bf16[1024,384]{1,0:T(8,128)(2,1)S(1)} %copy-done.9, bf16[1024,384]{1,0:T(8,128)(2,1)S(1)} %copy-done.23, ...), custom_call_target="tpu_custom_call" | custom-call | flops 1610612736 | bytes 1048576 | tf_op jit(solution)/shard_map/sum_nt/pallas_call | solution.py:589
  346.8 6.1 %collective-permute-done.56 = bf16[256,1024]{1,0:T(8,128)(2,1)S(1)} collective-permute-done((bf16[256,1024]{1,0:T(8,128)(2,1)S(1)}, bf16[256,1024]{1,0:T(8,128)(2,1)S(1)}, u32[]{:S(2)}, u32[]{:S(2)}) %collective-permute-start.56) | collective-permute-done | bytes 524320 | tf_op jit(solution)/shard_map/ppermute | solution.py:233
  361.7 6.0 %collective-permute-start.60 = (bf16[512,1024]{1,0:T(8,128)(2,1)}, bf16[512,1024]{1,0:T(8,128)(2,1)}, u32[]{:S(2)}, u32[]{:S(2)}) collective-permute-start(bf16[512,1024]{1,0:T(8,128)(2,1)} %fusion.4), channel_id=1, source_target_pairs={{2,4},{3,5},{4,2},{5,3},{10,12},{11,13},{12,10},{13,11},{18,20},{1... | collective-permute-start | bytes 3145736 | tf_op jit(solution)/shard_map/ppermute | solution.py:233
  413.0 5.0 %collective-permute-done.73 = bf16[256,512]{1,0:T(8,128)(2,1)S(1)} collective-permute-done((bf16[256,512]{1,0:T(8,128)(2,1)S(1)}, bf16[256,512]{1,0:T(8,128)(2,1)S(1)}, u32[]{:S(2)}, u32[]{:S(2)}) %collective-permute-start.73) | collective-permute-done | bytes 262176 | tf_op jit(solution)/shard_map/ppermute | solution.py:233
  (622 shorter events, 290.2 us)
Async XLA Ops:
  2.3 35.3 %collective-permute-start = (bf16[256,1024]{1,0:T(8,128)(2,1)S(1)}, bf16[256,1024]{1,0:T(8,128)(2,1)}, u32[]{:S(2)}, u32[]{:S(2)}) collective-permute-start(bf16[256,1024]{1,0:T(8,128)(2,1)S(1)} %get-tuple-element.435), channel_id=1, source_target_pairs={{0,1},{1,0},{6,7},{7,6},{8,9},{9,8},{14,15},{15,14},{16,17},{17,16... | collective-permute-start | bytes 1572872 | tf_op jit(solution)/shard_map/ppermute | solution.py:233
  10.3 27.3 %collective-permute-start.2 = (bf16[272,512]{1,0:T(8,128)(2,1)S(1)}, bf16[272,512]{1,0:T(8,128)(2,1)S(1)}, u32[]{:S(2)}, u32[]{:S(2)}) collective-permute-start(bf16[272,512]{1,0:T(8,128)(2,1)S(1)} %constant_dynamic-update-slice_fusion), channel_id=1, source_target_pairs={{0,1},{1,0},{2,3},{3,2},{4,5},{5,4},{6,7},{7,6},{8,9},{9,8},{10,11... | collective-permute-start | bytes 835592 | tf_op jit(solution)/shard_map/ppermute | solution.py:233
  12.5 27.6 %collective-permute-start.1 = (bf16[256,1024]{1,0:T(8,128)(2,1)S(1)}, bf16[256,1024]{1,0:T(8,128)(2,1)}, u32[]{:S(2)}, u32[]{:S(2)}) collective-permute-start(bf16[256,1024]{1,0:T(8,128)(2,1)S(1)} %get-tuple-element.434), channel_id=1, source_target_pairs={{2,0},{3,1},{4,6},{5,7},{10,8},{11,9},{12,14},{13,15},{18,16},{19,... | collective-permute-start | bytes 1572872 | tf_op jit(solution)/shard_map/ppermute | solution.py:233
  18.2 22.9 %collective-permute-start.3 = (bf16[256,1024]{1,0:T(8,128)(2,1)S(1)}, bf16[256,1024]{1,0:T(8,128)(2,1)}, u32[]{:S(2)}, u32[]{:S(2)}) collective-permute-start(bf16[256,1024]{1,0:T(8,128)(2,1)S(1)} %get-tuple-element.433), channel_id=1, source_target_pairs={{2,1},{3,0},{4,7},{5,6},{10,9},{11,8},{12,15},{13,14},{18,17},{19,... | collective-permute-start | bytes 1572872 | tf_op jit(solution)/shard_map/ppermute | solution.py:233
  59.3 32.7 %collective-permute-start.4 = (bf16[1024,1024]{1,0:T(8,128)(2,1)}, bf16[1024,1024]{1,0:T(8,128)(2,1)}, u32[]{:S(2)}, u32[]{:S(2)}) collective-permute-start(bf16[1024,1024]{1,0:T(8,128)(2,1)} %constant_dynamic-update-slice_fusion.12), channel_id=1, source_target_pairs={{0,4},{1,5},{6,2},{7,3},{8,12},{9,13},{14,10},{15,11},{16,20},{17,... | collective-permute-start | bytes 6291464 | tf_op jit(solution)/shard_map/ppermute | solution.py:233
  70.5 20.3 %collective-permute-start.17 = (bf16[256,1024]{1,0:T(8,128)(2,1)}, bf16[256,1024]{1,0:T(8,128)(2,1)}, u32[]{:S(2)}, u32[]{:S(2)}) collective-permute-start(bf16[256,1024]{1,0:T(8,128)(2,1)} %collective-permute-done.14), channel_id=1, source_target_pairs={{1,0},{2,3},{5,4},{6,7},{9,8},{10,11},{13,12},{14,15},{17,16},{18,... | collective-permute-start | bytes 1572872 | tf_op jit(solution)/shard_map/ppermute | solution.py:233
  118.3 37.1 %collective-permute-start.28 = (bf16[256,1024]{1,0:T(8,128)(2,1)S(1)}, bf16[256,1024]{1,0:T(8,128)(2,1)S(1)}, u32[]{:S(2)}, u32[]{:S(2)}) collective-permute-start(bf16[256,1024]{1,0:T(8,128)(2,1)S(1)} %get-tuple-element.428), channel_id=1, source_target_pairs={{2,0},{3,1},{4,6},{5,7},{10,8},{11,9},{12,14},{13,15},{18,16},{19,... | collective-permute-start | bytes 1572872 | tf_op jit(solution)/shard_map/ppermute | solution.py:233
  135.5 21.2 %collective-permute-start.27 = (bf16[256,1024]{1,0:T(8,128)(2,1)S(1)}, bf16[256,1024]{1,0:T(8,128)(2,1)S(1)}, u32[]{:S(2)}, u32[]{:S(2)}) collective-permute-start(bf16[256,1024]{1,0:T(8,128)(2,1)S(1)} %dynamic-slice_bitcast_fusion.2), channel_id=1, source_target_pairs={{0,1},{1,0},{6,7},{7,6},{8,9},{9,8},{14,15},{15,14},{16,17},{17,16... | collective-permute-start | bytes 1572872 | tf_op jit(solution)/shard_map/ppermute | solution.py:233
  150.4 31.5 %collective-permute-start.26 = (bf16[1024,1024]{1,0:T(8,128)(2,1)S(1)}, bf16[1024,1024]{1,0:T(8,128)(2,1)S(1)}, u32[]{:S(2)}, u32[]{:S(2)}) collective-permute-start(bf16[1024,1024]{1,0:T(8,128)(2,1)S(1)} %sum_nt.4), channel_id=1, source_target_pairs={{0,4},{1,5},{2,6},{3,7},{4,0},{5,1},{6,2},{7,3},{8,12},{9,13},{10,... | collective-permute-start | bytes 6291464 | tf_op jit(solution)/shard_map/ppermute | solution.py:233
  155.3 18.8 %collective-permute-start.34 = (bf16[256,1024]{1,0:T(8,128)(2,1)S(1)}, bf16[256,1024]{1,0:T(8,128)(2,1)S(1)}, u32[]{:S(2)}, u32[]{:S(2)}) collective-permute-start(bf16[256,1024]{1,0:T(8,128)(2,1)S(1)} %maximum_select_fusion.2), channel_id=1, source_target_pairs={{0,16},{1,17},{2,18},{3,19},{4,20},{5,21},{6,22},{7,23},{8,24},{9,... | collective-permute-start | bytes 1572872 | tf_op jit(solution)/shard_map/ppermute | solution.py:233
  155.5 20.0 %collective-permute-start.31 = (bf16[256,1024]{1,0:T(8,128)(2,1)S(1)}, bf16[256,1024]{1,0:T(8,128)(2,1)S(1)}, u32[]{:S(2)}, u32[]{:S(2)}) collective-permute-start(bf16[256,1024]{1,0:T(8,128)(2,1)S(1)} %maximum_select_fusion.2), channel_id=1, source_target_pairs={{0,8},{1,9},{2,10},{3,11},{4,12},{5,13},{6,14},{7,15},{8,0},{9,1},... | collective-permute-start | bytes 1572872 | tf_op jit(solution)/shard_map/ppermute | solution.py:233
  195.2 26.6 %collective-permute-start.40 = (bf16[512,1024]{1,0:T(8,128)(2,1)S(1)}, bf16[512,1024]{1,0:T(8,128)(2,1)S(1)}, u32[]{:S(2)}, u32[]{:S(2)}) collective-permute-start(bf16[512,1024]{1,0:T(8,128)(2,1)S(1)} %get-tuple-element.219), channel_id=1, source_target_pairs={{0,16},{1,17},{2,18},{3,19},{4,20},{5,21},{6,22},{7,23},{8,24},{9,... | collective-permute-start | bytes 3145736 | tf_op jit(solution)/shard_map/ppermute | solution.py:233
  199.1 22.7 %collective-permute-start.39 = (bf16[512,1024]{1,0:T(8,128)(2,1)S(1)}, bf16[512,1024]{1,0:T(8,128)(2,1)S(1)}, u32[]{:S(2)}, u32[]{:S(2)}) collective-permute-start(bf16[512,1024]{1,0:T(8,128)(2,1)S(1)} %get-tuple-element.223), channel_id=1, source_target_pairs={{0,8},{1,9},{2,10},{3,11},{4,12},{5,13},{6,14},{7,15},{8,0},{9,1},... | collective-permute-start | bytes 3145736 | tf_op jit(solution)/shard_map/ppermute | solution.py:233
  215.5 27.3 %collective-permute-start.44 = (bf16[1024,1024]{1,0:T(8,128)(2,1)S(1)}, bf16[1024,1024]{1,0:T(8,128)(2,1)S(1)}, u32[]{:S(2)}, u32[]{:S(2)}) collective-permute-start(bf16[1024,1024]{1,0:T(8,128)(2,1)S(1)} %sum_nt.6), channel_id=1, source_target_pairs={{0,4},{1,5},{2,6},{3,7},{4,0},{5,1},{6,2},{7,3},{8,12},{9,13},{10,... | collective-permute-start | bytes 6291464 | tf_op jit(solution)/shard_map/ppermute | solution.py:233
  226.7 40.5 %collective-permute-start.38 = (bf16[512,1024]{1,0:T(8,128)(2,1)S(1)}, bf16[512,1024]{1,0:T(8,128)(2,1)}, u32[]{:S(2)}, u32[]{:S(2)}) collective-permute-start(bf16[512,1024]{1,0:T(8,128)(2,1)S(1)} %fusion.3), channel_id=1, source_target_pairs={{2,4},{3,5},{4,2},{5,3},{10,12},{11,13},{12,10},{13,11},{18,20},{1... | collective-permute-start | bytes 3145736 | tf_op jit(solution)/shard_map/ppermute | solution.py:233
  234.6 50.7 %collective-permute-start.46 = (bf16[512,1024]{1,0:T(8,128)(2,1)S(1)}, bf16[512,1024]{1,0:T(8,128)(2,1)S(1)}, u32[]{:S(2)}, u32[]{:S(2)}) collective-permute-start(bf16[512,1024]{1,0:T(8,128)(2,1)S(1)} %get-tuple-element.243), channel_id=1, source_target_pairs={{0,16},{1,17},{2,18},{3,19},{4,20},{5,21},{6,22},{7,23},{8,24},{9,... | collective-permute-start | bytes 3145736 | tf_op jit(solution)/shard_map/ppermute | solution.py:233
  235.5 49.8 %collective-permute-start.45 = (bf16[512,1024]{1,0:T(8,128)(2,1)S(1)}, bf16[512,1024]{1,0:T(8,128)(2,1)S(1)}, u32[]{:S(2)}, u32[]{:S(2)}) collective-permute-start(bf16[512,1024]{1,0:T(8,128)(2,1)S(1)} %get-tuple-element.242), channel_id=1, source_target_pairs={{0,8},{1,9},{2,10},{3,11},{4,12},{5,13},{6,14},{7,15},{8,0},{9,1},... | collective-permute-start | bytes 3145736 | tf_op jit(solution)/shard_map/ppermute | solution.py:233
  238.2 51.0 %collective-permute-start.43 = (bf16[256,2048]{1,0:T(8,128)(2,1)}, bf16[256,2048]{1,0:T(8,128)(2,1)}, u32[]{:S(2)}, u32[]{:S(2)}) collective-permute-start(bf16[256,2048]{1,0:T(8,128)(2,1)} %pad_maximum_fusion.4), channel_id=1, source_target_pairs={{0,1},{3,2},{4,5},{7,6},{8,9},{11,10},{12,13},{15,14},{16,17},{19,... | collective-permute-start | bytes 3145736 | tf_op jit(solution)/shard_map/ppermute | solution.py:233
  303.0 21.3 %collective-permute-start.63 = (bf16[512,512]{1,0:T(8,128)(2,1)S(1)}, bf16[512,512]{1,0:T(8,128)(2,1)S(1)}, u32[]{:S(2)}, u32[]{:S(2)}) collective-permute-start(bf16[512,512]{1,0:T(8,128)(2,1)S(1)} %copy-done.57), channel_id=1, source_target_pairs={{0,8},{1,9},{2,10},{3,11},{4,12},{5,13},{6,14},{7,15},{8,0},{9,1},... | collective-permute-start | bytes 1572872 | tf_op jit(solution)/shard_map/ppermute | solution.py:233
  303.3 21.1 %collective-permute-start.62 = (bf16[512,512]{1,0:T(8,128)(2,1)}, bf16[512,512]{1,0:T(8,128)(2,1)S(1)}, u32[]{:S(2)}, u32[]{:S(2)}) collective-permute-start(bf16[512,512]{1,0:T(8,128)(2,1)} %copy-done.58), channel_id=1, source_target_pairs={{0,16},{1,17},{2,18},{3,19},{4,20},{5,21},{6,22},{7,23},{8,24},{9,... | collective-permute-start | bytes 1572872 | tf_op jit(solution)/shard_map/ppermute | solution.py:233
  310.6 23.4 %collective-permute-start.50 = (bf16[512,1024]{1,0:T(8,128)(2,1)S(1)}, bf16[512,1024]{1,0:T(8,128)(2,1)S(1)}, u32[]{:S(2)}, u32[]{:S(2)}) collective-permute-start(bf16[512,1024]{1,0:T(8,128)(2,1)S(1)} %pad_maximum_fusion.7), channel_id=1, source_target_pairs={{0,4},{1,5},{2,6},{3,7},{4,0},{5,1},{6,2},{7,3},{8,12},{9,13},{10,... | collective-permute-start | bytes 3145736 | tf_op jit(solution)/shard_map/ppermute | solution.py:233
  313.1 22.7 %collective-permute-start.55 = (bf16[256,2048]{1,0:T(8,128)(2,1)}, bf16[256,2048]{1,0:T(8,128)(2,1)}, u32[]{:S(2)}, u32[]{:S(2)}) collective-permute-start(bf16[256,2048]{1,0:T(8,128)(2,1)} %add_convert_fusion.2), channel_id=1, source_target_pairs={{1,2},{2,1},{5,6},{6,5},{9,10},{10,9},{13,14},{14,13},{17,18},{18,... | collective-permute-start | bytes 3145736 | tf_op jit(solution)/shard_map/ppermute | solution.py:233
  361.7 30.0 %collective-permute-start.60 = (bf16[512,1024]{1,0:T(8,128)(2,1)}, bf16[512,1024]{1,0:T(8,128)(2,1)}, u32[]{:S(2)}, u32[]{:S(2)}) collective-permute-start(bf16[512,1024]{1,0:T(8,128)(2,1)} %fusion.4), channel_id=1, source_target_pairs={{2,4},{3,5},{4,2},{5,3},{10,12},{11,13},{12,10},{13,11},{18,20},{1... | collective-permute-start | bytes 3145736 | tf_op jit(solution)/shard_map/ppermute | solution.py:233
  369.9 21.1 %collective-permute-start.69 = (bf16[256,1024]{1,0:T(8,128)(2,1)}, bf16[256,1024]{1,0:T(8,128)(2,1)}, u32[]{:S(2)}, u32[]{:S(2)}) collective-permute-start(bf16[256,1024]{1,0:T(8,128)(2,1)} %pad_maximum_fusion.11), channel_id=1, source_target_pairs={{0,1},{3,2},{4,5},{7,6},{8,9},{11,10},{12,13},{15,14},{16,17},{19,... | collective-permute-start | bytes 1572872 | tf_op jit(solution)/shard_map/ppermute | solution.py:233
  (170 other events, 2105.9 us)
